TPU v7x, 32 devices: a whole 2x2x4 slice. The times are simulated.
32 devices in a mesh: parts: 2 (over y), seq: 4 (over z), head: 4 (over x, core).
Axes of the slice: x: 2, y: 2, z: 4, core: 2. Of those that a mesh axis runs over, the one named last changes fastest.
Arguments:
- query_rows: bfloat16 [6144, 4096], P(('parts', 'seq', 'head')), parts along dimension 0, may hold values from -12 to 12
- key_rows: bfloat16 [6144, 4096], P(('parts', 'seq', 'head')), parts along dimension 0, may hold values from -12 to 12
- value_rows: bfloat16 [6144, 4096], P(('parts', 'seq', 'head')), parts along dimension 0, may hold values from -6 to 6
- block_lists: int32 [64, 4, 4, 3], P('parts', 'seq'), parts along dimension 0, may hold values from 0 to 5, as said below
- block_counts: int32 [64, 4, 4], P('parts'), parts along dimension 0, may hold values from 0 to 3, as said below
Outputs:
- attended: bfloat16 [6144, 4096], P(('parts', 'seq', 'head')), parts along dimension 0
There are 2 independent parts, one for each index of `parts`. A program takes and returns all parts, laid end to end along the dimension named above; each array names one. Nothing has to cross between parts.
Inputs may be any that keep to these rules, and one draw needn't show every extreme that they name: `block_lists`: for one head, query tile and key tile the 3 entries are distinct block numbers of the key tile; only the first block_counts of them are listed. `block_counts`: 0 where the key tile is the query tile; some entries of every draw equal 3; for every k, query tile and key tile, the counts of heads 2k and 2k+1 sum to at most 4, and exactly 4 for some k in every draw.
All inputs are finite; a program needn't handle non-finite values.
Results may differ from a plain program's by a relative error of at most 0.0034.
Values may be sent and summed in bfloat16 or wider, within the bound.
No kernel may reach another device: no remote copies, remote signals or barrier semaphores. Data moves between devices by JAX's collectives and lax.ppermute only.
A program may use at most 64 MiB of HBM per device.

v0:
```python
import math

import jax
import jax.numpy as jnp
from jax import lax
from jax.sharding import PartitionSpec as P

HEADS = 32
DH = 128
BLOCK = 128
MOST = 3
PAIR_MOST = 4
TILE = 768


def score_block(head_queries, key_block, score_scale):
    products = lax.dot_general(
        head_queries, key_block, (((1,), (1,)), ((), ())), preferred_element_type=jnp.float32
    )
    return products * score_scale


def attend_head(head_queries, own_keys, own_values, flat_blocks, valid_slots, score_scale):
    scores = score_block(head_queries, own_keys, score_scale)
    run_max = jnp.max(scores, axis=1, keepdims=True)
    weights = jnp.exp(scores - run_max)
    run_sum = jnp.sum(weights, axis=1, keepdims=True)
    accum = jnp.dot(weights.astype(jnp.bfloat16), own_values, preferred_element_type=jnp.float32)
    group_size = max(1, 512 // BLOCK)
    slot_order = jnp.argsort(jnp.where(valid_slots, 0, 1), stable=True)
    used_count = jnp.sum(valid_slots.astype(jnp.int32))
    trip_count = (used_count + group_size - 1) // group_size

    def visit(turn_index, state_tuple):
        old_max, old_sum, old_accum = state_tuple
        picked = lax.dynamic_slice_in_dim(slot_order, turn_index * group_size, group_size)
        blocks = flat_blocks[picked].reshape(group_size * BLOCK, 2 * DH)
        live_keys = jnp.repeat(
            turn_index * group_size + jnp.arange(group_size, dtype=jnp.int32) < used_count, BLOCK
        )
        block_scores = score_block(head_queries, blocks[:, :DH], score_scale)
        block_scores = jnp.where(live_keys[None, :], block_scores, -jnp.inf)
        new_max = jnp.maximum(old_max, jnp.max(block_scores, axis=1, keepdims=True))
        block_weights = jnp.exp(block_scores - new_max)
        rescale = jnp.exp(old_max - new_max)
        new_sum = old_sum * rescale + jnp.sum(block_weights, axis=1, keepdims=True)
        new_accum = old_accum * rescale + jnp.dot(
            block_weights.astype(jnp.bfloat16), blocks[:, DH:], preferred_element_type=jnp.float32
        )
        return (new_max, new_sum, new_accum)

    run_max, run_sum, accum = lax.fori_loop(0, trip_count, visit, (run_max, run_sum, accum))
    return (accum / run_sum).astype(jnp.bfloat16)


def on_device(query_rows, key_rows, value_rows, block_lists, block_counts):
    head_count = lax.axis_size("head")
    seq_count = lax.axis_size("seq")
    seq_rank = lax.axis_index("seq")
    head_rank = lax.axis_index("head")
    local_heads = HEADS // head_count
    local_pairs = local_heads // 2
    score_scale = 1.0 / math.sqrt(DH)
    placed = jnp.arange(HEADS, dtype=jnp.int32)
    tile_queries, tile_keys, tile_values = (
        lax.all_to_all(query_rows, "head", split_axis=1, concat_axis=0, tiled=True),
        lax.all_to_all(key_rows, "head", split_axis=1, concat_axis=0, tiled=True),
        lax.all_to_all(value_rows, "head", split_axis=1, concat_axis=0, tiled=True),
    )
    my_heads = lax.dynamic_slice_in_dim(placed, head_rank * local_heads, local_heads)
    my_lists = block_lists[my_heads, 0]
    my_counts = jnp.take(block_counts[my_heads], seq_rank, axis=1)
    wanted = lax.all_to_all(
        jnp.transpose(my_lists, (1, 0, 2)), "seq", split_axis=0, concat_axis=0, tiled=True
    )
    block_total = TILE // BLOCK
    paired = jnp.concatenate(
        [
            tile_keys.reshape(block_total, BLOCK, local_heads, DH),
            tile_values.reshape(block_total, BLOCK, local_heads, DH),
        ],
        axis=3,
    )
    paired = jnp.transpose(paired, (2, 0, 1, 3))
    capacity_index = jnp.arange(PAIR_MOST, dtype=jnp.int32)
    asked_counts = jnp.take(block_counts[my_heads], seq_rank, axis=2)
    first_asked = jnp.transpose(asked_counts[0::2], (1, 0))[:, :, None]
    in_first = capacity_index[None, None, :] < first_asked
    slot_pick = jnp.clip(
        jnp.where(
            in_first, capacity_index[None, None, :], capacity_index[None, None, :] - first_asked
        ),
        0,
        MOST - 1,
    )
    head_pick = 2 * jnp.arange(local_pairs, dtype=jnp.int32)[None, :, None] + jnp.where(
        in_first, 0, 1
    )
    tile_pick = jnp.arange(seq_count, dtype=jnp.int32)[:, None, None]
    block_pick = wanted[tile_pick, head_pick, slot_pick]
    packed = paired[head_pick, block_pick]
    received = lax.all_to_all(packed, "seq", split_axis=0, concat_axis=0, tiled=True)
    outputs = []
    for head_slot in range(local_heads):
        head_queries = tile_queries[:, head_slot * DH : (head_slot + 1) * DH]
        own_keys = tile_keys[:, head_slot * DH : (head_slot + 1) * DH]
        own_values = tile_values[:, head_slot * DH : (head_slot + 1) * DH]
        pair_slot = head_slot // 2
        flat_blocks = received[:, pair_slot].reshape(seq_count * PAIR_MOST, BLOCK, 2 * DH)
        first_have = my_counts[2 * pair_slot][:, None]
        second_have = my_counts[2 * pair_slot + 1][:, None]
        if head_slot % 2 == 0:
            valid_grid = capacity_index[None, :] < first_have
        else:
            valid_grid = (capacity_index[None, :] >= first_have) & (
                capacity_index[None, :] < first_have + second_have
            )
        valid_slots = valid_grid.reshape(-1)
        outputs.append(
            attend_head(head_queries, own_keys, own_values, flat_blocks, valid_slots, score_scale)
        )
    tile_output = jnp.concatenate(outputs, axis=1)
    attended = lax.all_to_all(tile_output, "head", split_axis=0, concat_axis=1, tiled=True)
    return attended


def solution(mesh):
    in_specs = (
        P(("parts", "seq", "head"), None),
        P(("parts", "seq", "head"), None),
        P(("parts", "seq", "head"), None),
        P("parts", "seq", None, None),
        P("parts", None, None),
    )
    out_specs = P(("parts", "seq", "head"), None)
    return jax.shard_map(
        on_device, mesh=mesh, in_specs=in_specs, out_specs=out_specs, check_vma=False
    )
```

profile of v0, /device:TPU:0, one launch (start us, length us, event | category | flops | bytes accessed | tf_op | source)
XLA Modules:
  0.0 289.2 jit_solution(16236335125974565042)
XLA Ops:
  2.2 6.3 %all-to-all-start.3 = ((s32[4,8,3]{1,2,0:T(4,128)}), s32[4,8,3]{1,2,0:T(4,128)S(1)}, u32[]{:S(2)}, u32[]{:S(2)}) async-start(s32[4,8,3]{1,2,0:T(4,128)} %copy.49), calls=%async_computation.3 | async-start | bytes 16384 | tf_op jit(solution)/shard_map/all_to_all | solution.py:73
  8.5 2.7 copy.61
  11.2 2.9 all-to-all-done.3
  14.1 3.6 %all-to-all-start.1 = ((bf16[192,4,1024]{2,0,1:T(8,128)(2,1)}), bf16[192,4,1024]{2,0,1:T(8,128)(2,1)S(1)}, u32[]{:S(2)}, u32[]{:S(2)}) async-start(bf16[192,4,1024]{2,0,1:T(8,128)(2,1)} %bitcast.169), calls=%async_computation.1 | async-start | bytes 3145728 | tf_op jit(solution)/shard_map/all_to_all | solution.py:67
  17.6 2.7 copy.60
  20.4 17.3 %all-to-all-done.1 = bf16[192,4,1024]{2,0,1:T(8,128)(2,1)S(1)} async-done(((bf16[192,4,1024]{2,0,1:T(8,128)(2,1)}), bf16[192,4,1024]{2,0,1:T(8,128)(2,1)S(1)}, u32[]{:S(2)}, u32[]{:S(2)}) %all-to-all-start.1) | async-done | bytes 1572896 | tf_op jit(solution)/shard_map/all_to_all | solution.py:67
  38.8 3.6 %all-to-all-start.2 = ((bf16[192,4,1024]{2,0,1:T(8,128)(2,1)}), bf16[192,4,1024]{2,0,1:T(8,128)(2,1)S(1)}, u32[]{:S(2)}, u32[]{:S(2)}) async-start(bf16[192,4,1024]{2,0,1:T(8,128)(2,1)} %bitcast.168), calls=%async_computation.2 | async-start | bytes 3145728 | tf_op jit(solution)/shard_map/all_to_all | solution.py:68
  43.2 2.7 copy.62
  46.3 16.2 %all-to-all-done.2 = bf16[192,4,1024]{2,0,1:T(8,128)(2,1)S(1)} async-done(((bf16[192,4,1024]{2,0,1:T(8,128)(2,1)}), bf16[192,4,1024]{2,0,1:T(8,128)(2,1)S(1)}, u32[]{:S(2)}, u32[]{:S(2)}) %all-to-all-start.2) | async-done | bytes 1572896 | tf_op jit(solution)/shard_map/all_to_all | solution.py:68
  62.5 4.3 %all-to-all-start = ((bf16[192,4,1024]{2,0,1:T(8,128)(2,1)}), bf16[192,4,1024]{2,0,1:T(8,128)(2,1)}, u32[]{:S(2)}, u32[]{:S(2)}) async-start(bf16[192,4,1024]{2,0,1:T(8,128)(2,1)} %bitcast.167), calls=%async_computation | async-start | bytes 3145728 | tf_op jit(solution)/shard_map/all_to_all | solution.py:66
  74.7 1.3 sort.122
  86.4 1.8 copy.55
  90.0 2.8 gather_fusion.11
  92.8 5.0 %all-to-all-start.4 = ((bf16[4,4,4,128,256]{4,3,2,1,0:T(8,128)(2,1)}), bf16[4,4,4,128,256]{4,3,2,1,0:T(8,128)(2,1)}, u32[]{:S(2)}, u32[]{:S(2)}) async-start(bf16[4,4,4,128,256]{4,3,2,1,0:T(8,128)(2,1)} %bitcast.144), calls=%async_computation.4 | async-start | bytes 8388608 | tf_op jit(solution)/shard_map/all_to_all | solution.py:102
  97.8 1.5 multiply_reduce_fusion
  99.8 1.5 multiply_reduce_fusion.1
  101.7 1.5 multiply_reduce_fusion.2
  103.7 1.5 multiply_reduce_fusion.3
  105.6 1.5 multiply_reduce_fusion.4
  107.6 1.5 multiply_reduce_fusion.5
  109.5 1.5 multiply_reduce_fusion.6
  111.5 1.5 multiply_reduce_fusion.7
  113.4 2.8 fusion.176
  120.7 71.0 %all-to-all-done.4 = bf16[4,4,4,128,256]{4,3,2,1,0:T(8,128)(2,1)} async-done(((bf16[4,4,4,128,256]{4,3,2,1,0:T(8,128)(2,1)}), bf16[4,4,4,128,256]{4,3,2,1,0:T(8,128)(2,1)}, u32[]{:S(2)}, u32[]{:S(2)}) %all-to-all-start.4) | async-done | bytes 4194336 | tf_op jit(solution)/shard_map/all_to_all | solution.py:102
  191.7 4.3 %fusion.175 = (bf16[4,1,4,128,256]{4,3,2,1,0:T(8,128)(2,1)}, bf16[4,1,4,128,256]{4,3,2,1,0:T(8,128)(2,1)}, bf16[4,1,4,128,256]{4,3,2,1,0:T(8,128)(2,1)}, bf16[4,1,4,128,256]{4,3,2,1,0:T(8,128)(2,1)}) fusion(bf16[4,4,4,128,256]{4,3,2,1,0:T(8,128)(2,1)} %all-to-all-done.4), kind=kLoop, calls=%fused_computation.321 | loop fusion | bytes 8388608 | tf_op jit(solution)/shard_map/slice | solution.py:109
  196.0 4.8 %while.121 = (s32[]{:T(128)}, f32[768,1]{0,1:T(1,128)S(1)}, f32[768,1]{0,1:T(1,128)S(1)}, f32[768,128]{1,0:T(8,128)S(1)}, s32[]{:T(128)}, /*index=5*/s32[]{:T(12...) while((s32[]{:T(128)}, f32[768,1]{0,1:T(1,128)S(1)}, ...), condition=%wide.region_63.64_spmd, body=%wide.region_60.63_spmd.sunk | while | flops 204279072 | bytes 6547711 | solution.py:52
  196.1 1.8 gather_fusion.7
  200.8 4.7 %while.120 = (s32[]{:T(128)}, f32[768,1]{0,1:T(1,128)S(1)}, f32[768,1]{0,1:T(1,128)S(1)}, f32[768,128]{1,0:T(8,128)S(1)}, s32[]{:T(128)}, /*index=5*/s32[]{:T(12...) while((s32[]{:T(128)}, f32[768,1]{0,1:T(1,128)S(1)}, ...), condition=%wide.region_55.56_spmd, body=%wide.region_52.55_spmd.sunk | while | flops 204279072 | bytes 6547711 | solution.py:52
  200.9 1.8 gather_fusion.6
  205.6 9.6 %while.119 = (s32[]{:T(128)}, f32[768,1]{0,1:T(1,128)S(1)}, f32[768,1]{0,1:T(1,128)S(1)}, f32[768,128]{1,0:T(8,128)S(1)}, s32[]{:T(128)}, /*index=5*/s32[]{:T(12...) while((s32[]{:T(128)}, f32[768,1]{0,1:T(1,128)S(1)}, ...), condition=%wide.region_47.48_spmd, body=%wide.region_44.47_spmd.sunk | while | flops 204279072 | bytes 6547711 | solution.py:52
  205.7 1.8 gather_fusion.5
  210.5 1.8 gather_fusion.5
  213.0 1.3 fusion.266
  215.2 4.8 %while.118 = (s32[]{:T(128)}, f32[768,1]{0,1:T(1,128)S(1)}, f32[768,1]{0,1:T(1,128)S(1)}, f32[768,128]{1,0:T(8,128)S(1)}, s32[]{:T(128)}, /*index=5*/s32[]{:T(12...) while((s32[]{:T(128)}, f32[768,1]{0,1:T(1,128)S(1)}, ...), condition=%wide.region_39.40_spmd, body=%wide.region_36.39_spmd.sunk | while | flops 204279072 | bytes 6547711 | solution.py:52
  215.3 1.8 gather_fusion.4
  217.8 1.3 fusion.260
  220.0 9.7 %while.117 = (s32[]{:T(128)}, f32[768,1]{0,1:T(1,128)S(1)}, f32[768,1]{0,1:T(1,128)S(1)}, f32[768,128]{1,0:T(8,128)S(1)}, s32[]{:T(128)}, /*index=5*/s32[]{:T(12...) while((s32[]{:T(128)}, f32[768,1]{0,1:T(1,128)S(1)}, ...), condition=%wide.region_31.32_spmd, body=%wide.region_28.31_spmd.sunk | while | flops 204279072 | bytes 6547711 | solution.py:52
  220.1 1.8 gather_fusion.3
  222.7 1.3 fusion.254
  225.0 1.8 gather_fusion.3
  227.5 1.3 fusion.254
  229.7 4.9 %while.116 = (s32[]{:T(128)}, f32[768,1]{0,1:T(1,128)S(1)}, f32[768,1]{0,1:T(1,128)S(1)}, f32[768,128]{1,0:T(8,128)S(1)}, s32[]{:T(128)}, /*index=5*/s32[]{:T(12...) while((s32[]{:T(128)}, f32[768,1]{0,1:T(1,128)S(1)}, ...), condition=%wide.region_23.24_spmd, body=%wide.region_20.23_spmd.sunk | while | flops 204279072 | bytes 6547711 | solution.py:52
  229.9 1.8 gather_fusion.2
  234.7 4.8 %while.114 = (s32[]{:T(128)}, f32[768,1]{0,1:T(1,128)S(1)}, f32[768,1]{0,1:T(1,128)S(1)}, f32[768,128]{1,0:T(8,128)S(1)}, s32[]{:T(128)}, /*index=5*/s32[]{:T(12...) while((s32[]{:T(128)}, f32[768,1]{0,1:T(1,128)S(1)}, ...), condition=%wide.region_7.8_spmd, body=%wide.region_4.7_spmd.sunk | while | flops 204279072 | bytes 6547711 | solution.py:52
  234.8 1.8 gather_fusion
  237.3 1.3 fusion.236
  241.2 46.7 %all_to_all.86 = bf16[4,192,1024]{2,1,0:T(8,128)(2,1)S(1)} all-to-all(bf16[4,192,1024]{2,1,0:T(8,128)(2,1)S(1)} %bitcast.173), channel_id=1, replica_groups=mesh['parts'=2,'seq'=4,'head'=4] {'head'}, dimensions={0} | all-to-all | bytes 3145728 | tf_op jit(solution)/shard_map/all_to_all | solution.py:123
  287.9 1.3 copy.54
  (197 shorter events, 48.9 us)
Async XLA Ops:
  2.2 11.9 %all-to-all-start.3 = ((s32[4,8,3]{1,2,0:T(4,128)}), s32[4,8,3]{1,2,0:T(4,128)S(1)}, u32[]{:S(2)}, u32[]{:S(2)}) async-start(s32[4,8,3]{1,2,0:T(4,128)} %copy.49), calls=%async_computation.3 | async-start | bytes 16384 | tf_op jit(solution)/shard_map/all_to_all | solution.py:73
  14.1 23.6 %all-to-all-start.1 = ((bf16[192,4,1024]{2,0,1:T(8,128)(2,1)}), bf16[192,4,1024]{2,0,1:T(8,128)(2,1)S(1)}, u32[]{:S(2)}, u32[]{:S(2)}) async-start(bf16[192,4,1024]{2,0,1:T(8,128)(2,1)} %bitcast.169), calls=%async_computation.1 | async-start | bytes 3145728 | tf_op jit(solution)/shard_map/all_to_all | solution.py:67
  37.7 1.1 copy-start.2
  37.7 4.7 %copy-start.3 = (s32[32,4,4]{0,2,1:T(4,128)S(1)}, s32[32,4,4]{0,2,1:T(4,128)}, u32[]{:S(2)}) copy-start(s32[32,4,4]{0,2,1:T(4,128)} %param.25) | copy-start | bytes 6148
  38.8 23.6 %all-to-all-start.2 = ((bf16[192,4,1024]{2,0,1:T(8,128)(2,1)}), bf16[192,4,1024]{2,0,1:T(8,128)(2,1)S(1)}, u32[]{:S(2)}, u32[]{:S(2)}) async-start(bf16[192,4,1024]{2,0,1:T(8,128)(2,1)} %bitcast.168), calls=%async_computation.2 | async-start | bytes 3145728 | tf_op jit(solution)/shard_map/all_to_all | solution.py:68
  62.5 26.2 %copy-start = (bf16[192,4,1024]{2,0,1:T(8,128)(2,1)}, bf16[192,4,1024]{2,0,1:T(8,128)(2,1)S(1)}, u32[]{:S(2)}) copy-start(bf16[192,4,1024]{2,0,1:T(8,128)(2,1)S(1)} %all-to-all-done.2) | copy-start | bytes 4718596
  62.5 30.3 %all-to-all-start = ((bf16[192,4,1024]{2,0,1:T(8,128)(2,1)}), bf16[192,4,1024]{2,0,1:T(8,128)(2,1)}, u32[]{:S(2)}, u32[]{:S(2)}) async-start(bf16[192,4,1024]{2,0,1:T(8,128)(2,1)} %bitcast.167), calls=%async_computation | async-start | bytes 3145728 | tf_op jit(solution)/shard_map/all_to_all | solution.py:66
  92.8 99.0 %all-to-all-start.4 = ((bf16[4,4,4,128,256]{4,3,2,1,0:T(8,128)(2,1)}), bf16[4,4,4,128,256]{4,3,2,1,0:T(8,128)(2,1)}, u32[]{:S(2)}, u32[]{:S(2)}) async-start(bf16[4,4,4,128,256]{4,3,2,1,0:T(8,128)(2,1)} %bitcast.144), calls=%async_computation.4 | async-start | bytes 8388608 | tf_op jit(solution)/shard_map/all_to_all | solution.py:102
  113.4 2.8 copy-start.1
where the time goes:
time: 294 us; the launch traced here: 289 us
  waiting for transfers between devices  107 us (36%)
  blocking collectives  46.7 us (16%)
  local copies, waits for them, and re-layouts  45.6 us (16%)
  matrix products  33.1 us (11%)
  other arithmetic  27.3 us (9%)
  starting transfers between devices  22.8 us (8%)
  between operations  5.66 us (2%)
    all_to_all x1, waiting for transfers between devices, on_device(): lax.all_to_all(packed, 'seq', split_axis=0, concat_axis=0, tiled=True)  71 us
    all_to_all x1, blocking collectives, on_device(): lax.all_to_all(tile_output, 'head', split_axis=0, concat_axis=1, tiled=True)  46.7 us
    dot_general x17, matrix products, score_block(): lax.dot_general(head_queries, key_block, (((1,), (1,)), ((), ())), prefer...  23.8 us
    all_to_all x1, waiting for transfers between devices, on_device(): lax.all_to_all(key_rows, 'head', split_axis=1, concat_axis=0, tiled=True)  17.3 us
    all_to_all x1, waiting for transfers between devices, on_device(): lax.all_to_all(value_rows, 'head', split_axis=1, concat_axis=0, tiled=True)  16.2 us
    gather x9, local copies, waits for them, and re-layouts, visit(): blocks = flat_blocks[picked].reshape(group_size * BLOCK, 2 * DH)  16.1 us
    sort x8, other arithmetic, attend_head(): slot_order = jnp.argsort(jnp.where(valid_slots, 0, 1), stable=True)  10.4 us
    all_to_all x1, starting transfers between devices, on_device(): lax.all_to_all(jnp.transpose(my_lists, (1, 0, 2)), 'seq', split_axis=0, c...  6.32 us
  transfers between devices with their start and end apart: 5, of which 4 were waited for; matrix products, arithmetic and copies ran while one was open for 18% of the time, Pallas kernels for 0%

commit v1 on v0

v1 whole, which is shorter than its diff:
```python
import functools
import math

import jax
import jax.numpy as jnp
from jax import lax
from jax.experimental import pallas as pl
from jax.experimental.pallas import tpu as pltpu
from jax.sharding import PartitionSpec as P

HEADS = 32
DH = 128
BLOCK = 128
MOST = 3
PAIR_MOST = 4
TILE = 768
PAIR = 2 * DH
OWN_BLOCKS = TILE // BLOCK
VMEM_LIMIT = 32 * 1024 * 1024
SMEM = pltpu.SMEM


def shifted(array, axis, step):
    size = lax.axis_size(axis)
    return lax.ppermute(array, axis, [(i, (i + step) % size) for i in range(size)])


def vmem_spec():
    return pl.BlockSpec(memory_space=pltpu.VMEM)


def smem_spec():
    return pl.BlockSpec(memory_space=SMEM)


def pick_kernel(head_count, seq_count, slots, place_ref, counts_ref, *refs):
    want_refs = refs[: seq_count - 1]
    rows_refs = refs[seq_count - 1 : seq_count - 1 + head_count]
    tile_ref = refs[seq_count - 1 + head_count]
    send_refs = refs[seq_count + head_count :]
    my_seq, my_head = place_ref[0], place_ref[1]
    rows = TILE // head_count
    for step in range(head_count):
        rank = lax.rem(my_head - step + head_count, head_count)
        place = pl.ds(pl.multiple_of(rank * rows, 16), rows)
        for pair in range(slots):
            for half in range(2):
                base = pair * 2 * PAIR + half * DH
                tile_ref[2 * pair + half, place, :DH] = rows_refs[step][:, base : base + DH]
                tile_ref[2 * pair + half, place, DH:] = rows_refs[step][
                    :, base + PAIR : base + PAIR + DH
                ]
    for step in range(1, seq_count):
        asker = lax.rem(my_seq + step, seq_count)
        for pair in range(slots):
            first = 2 * place_ref[2 + pair]
            first_count = counts_ref[(first * seq_count + asker) * seq_count + my_seq]
            both = first_count + counts_ref[((first + 1) * seq_count + asker) * seq_count + my_seq]
            for slot in range(PAIR_MOST):

                @pl.when(slot < both)
                def _():
                    half = jnp.where(slot < first_count, 0, 1)
                    entry = jnp.where(slot < first_count, slot, slot - first_count)
                    entry = jnp.clip(entry, 0, MOST - 1)
                    block = want_refs[step - 1][
                        ((first + half) * seq_count + my_seq) * MOST + entry
                    ]
                    send_refs[step - 1][pair * PAIR_MOST + slot] = tile_ref[
                        2 * pair + half, pl.ds(pl.multiple_of(block * BLOCK, BLOCK), BLOCK), :
                    ]


def pick_blocks(places, counts, wanted, pieces, slots):
    head_count, seq_count = len(pieces), len(wanted) + 1
    out_shape = [jax.ShapeDtypeStruct((2 * slots, TILE, 2 * DH), jnp.bfloat16)]
    out_shape += [
        jax.ShapeDtypeStruct((slots * PAIR_MOST, BLOCK, 2 * DH), jnp.bfloat16)
    ] * (seq_count - 1)
    outs = pl.pallas_call(
        functools.partial(pick_kernel, head_count, seq_count, slots),
        out_shape=out_shape,
        in_specs=[smem_spec()] * (seq_count + 1) + [vmem_spec()] * head_count,
        out_specs=[vmem_spec()] * seq_count,
        compiler_params=pltpu.CompilerParams(vmem_limit_bytes=VMEM_LIMIT),
        cost_estimate=pl.CostEstimate(
            flops=0, bytes_accessed=slots * 5 * 1024 * 1024, transcendentals=0
        ),
        name="pick_blocks",
    )(places, counts, *wanted, *pieces)
    return outs[0], outs[1:]


GROUP = 3 * BLOCK
QUERIES = 256


def fold(values, combine):
    total = values[:, :DH]
    for start in range(DH, values.shape[1], DH):
        total = combine(total, values[:, start : start + DH])
    return total


def row_top(scores):
    top = jnp.max(fold(scores, jnp.maximum), axis=1, keepdims=True)
    return jnp.broadcast_to(top, (scores.shape[0], DH))


def weigh(scores, top):
    return jnp.concatenate(
        [jnp.exp2(scores[:, at : at + DH] - top) for at in range(0, scores.shape[1], DH)], axis=1
    )


def attend_kernel(head_count, seq_count, place_ref, counts_ref, tile_ref, *refs):
    query_refs = refs[:head_count]
    block_refs = refs[head_count : head_count + seq_count - 1]
    out_refs = refs[head_count + seq_count - 1 : 2 * head_count + seq_count - 1]
    q_ref, k_ref, v_ref, top_ref, sum_ref, mix_ref = refs[2 * head_count + seq_count - 1 :]
    my_seq = place_ref[0]
    turn = pl.program_id(0)
    half = lax.rem(turn, 2)
    first = 2 * place_ref[2 + turn // 2]
    rows = TILE // head_count
    scale = math.log2(math.e) / math.sqrt(DH)

    @pl.when(turn == 0)
    def _():
        k_ref[...] = jnp.zeros_like(k_ref)
        v_ref[...] = jnp.zeros_like(v_ref)

    for step in range(head_count):
        q_ref[step * rows : (step + 1) * rows, :] = query_refs[step][...]

    used = jnp.int32(0)
    for step in range(1, seq_count):
        holder = lax.rem(my_seq - step + seq_count, seq_count)
        first_count = counts_ref[(first * seq_count + my_seq) * seq_count + holder]
        second_count = counts_ref[((first + 1) * seq_count + my_seq) * seq_count + holder]
        count = jnp.where(half == 0, first_count, second_count)
        start = jnp.where(half == 0, 0, first_count)
        for entry in range(MOST):

            @pl.when(entry < count)
            def _():
                place = pl.ds(pl.multiple_of((used + entry) * BLOCK, BLOCK), BLOCK)
                slot = jnp.minimum(start + entry, PAIR_MOST - 1)
                k_ref[place, :] = block_refs[step - 1][slot, :, :DH]
                v_ref[place, :] = block_refs[step - 1][slot, :, DH:]

        used = used + count

    def score(queries, keys):
        return (
            lax.dot_general(
                queries, keys, (((1,), (1,)), ((), ())), preferred_element_type=jnp.float32
            )
            * scale
        )

    own_keys = tile_ref[0, :, :DH]
    own_values = tile_ref[0, :, DH:]
    for at in range(0, TILE, QUERIES):
        span = slice(at, at + QUERIES)
        scores = score(q_ref[span, :], own_keys)
        top = row_top(scores)
        weights = weigh(scores, top)
        top_ref[span, :] = top
        sum_ref[span, :] = fold(weights, jnp.add)
        mix_ref[span, :] = jnp.dot(
            weights.astype(jnp.bfloat16), own_values, preferred_element_type=jnp.float32
        )

    def visit(group, carry):
        place = pl.ds(pl.multiple_of(group * GROUP, GROUP), GROUP)
        keys = k_ref[place, :]
        values = v_ref[place, :]
        column = lax.broadcasted_iota(jnp.int32, (1, GROUP), 1) + group * GROUP
        bias = jnp.where(column < used * BLOCK, 0.0, -jnp.inf)
        for at in range(0, TILE, QUERIES):
            span = slice(at, at + QUERIES)
            scores = score(q_ref[span, :], keys) + bias
            old_top = top_ref[span, :]
            top = jnp.maximum(old_top, row_top(scores))
            weights = weigh(scores, top)
            rescale = jnp.exp2(old_top - top)
            top_ref[span, :] = top
            sum_ref[span, :] = sum_ref[span, :] * rescale + fold(weights, jnp.add)
            mix_ref[span, :] = mix_ref[span, :] * rescale + jnp.dot(
                weights.astype(jnp.bfloat16), values, preferred_element_type=jnp.float32
            )
        return carry

    lax.fori_loop(0, (used + 2) // 3, visit, 0)
    for step in range(head_count):
        span = slice(step * rows, (step + 1) * rows)
        total = jnp.sum(sum_ref[span, :], axis=1, keepdims=True)
        out_refs[step][...] = (mix_ref[span, :] / total).astype(jnp.bfloat16)


def attend(places, counts, tile_pairs, queries, blocks, first_pair, slots):
    head_count, seq_count = len(queries), len(blocks) + 1
    rows = TILE // head_count
    most_blocks = -(-(seq_count - 1) * MOST // 3) * 3
    return pl.pallas_call(
        functools.partial(attend_kernel, head_count, seq_count),
        grid=(2 * slots,),
        out_shape=[jax.ShapeDtypeStruct((rows, slots * PAIR), jnp.bfloat16)] * head_count,
        in_specs=[smem_spec()] * 2
        + [pl.BlockSpec((1, TILE, 2 * DH), lambda i: (i, 0, 0))]
        + [pl.BlockSpec((rows, DH), lambda i: (0, 2 * first_pair + i))] * head_count
        + [pl.BlockSpec((PAIR_MOST, BLOCK, 2 * DH), lambda i: (i // 2, 0, 0))] * (seq_count - 1),
        out_specs=[pl.BlockSpec((rows, DH), lambda i: (0, i))] * head_count,
        scratch_shapes=[
            pltpu.VMEM((TILE, DH), jnp.bfloat16),
            pltpu.VMEM((most_blocks * BLOCK, DH), jnp.bfloat16),
            pltpu.VMEM((most_blocks * BLOCK, DH), jnp.bfloat16),
            pltpu.VMEM((TILE, DH), jnp.float32),
            pltpu.VMEM((TILE, DH), jnp.float32),
            pltpu.VMEM((TILE, DH), jnp.float32),
        ],
        compiler_params=pltpu.CompilerParams(vmem_limit_bytes=VMEM_LIMIT),
        cost_estimate=pl.CostEstimate(
            flops=slots * 2 * TILE * 2 * TILE * DH * 4,
            bytes_accessed=slots * 3 * 1024 * 1024,
            transcendentals=slots * 2 * TILE * 2 * TILE,
        ),
        name="attend",
    )(places, counts, tile_pairs, *queries, *blocks)


def lay_kernel(head_count, groups, place_ref, *refs):
    piece_refs = refs[: head_count * len(groups)]
    out_ref = refs[head_count * len(groups)]
    sems = refs[head_count * len(groups) + 1]
    my_head = place_ref[0]
    local_pairs = sum(len(group) for group in groups)
    copies = []
    for number, group in enumerate(groups):
        for step in range(head_count):
            rank = lax.rem(my_head - step + head_count, head_count)
            for at, pair in enumerate(group):
                column = place_ref[1 + rank * local_pairs + pair] * PAIR
                copy = pltpu.make_async_copy(
                    piece_refs[number * head_count + step].at[:, at * PAIR : (at + 1) * PAIR],
                    out_ref.at[:, pl.ds(pl.multiple_of(column, PAIR), PAIR)],
                    sems.at[len(copies)],
                )
                copy.start()
                copies.append(copy)
    for copy in copies:
        copy.wait()


def lay_out(places, pieces, groups, rows):
    head_count = len(pieces[0])
    flat = [piece for stage in pieces for piece in stage]
    copies = head_count * sum(len(group) for group in groups)
    return pl.pallas_call(
        functools.partial(lay_kernel, head_count, groups),
        out_shape=jax.ShapeDtypeStruct((rows, HEADS * DH), jnp.bfloat16),
        in_specs=[smem_spec()] + [pl.BlockSpec(memory_space=pl.ANY)] * len(flat),
        out_specs=pl.BlockSpec(memory_space=pl.ANY),
        scratch_shapes=[pltpu.SemaphoreType.DMA((copies,))],
        name="lay_out",
    )(places, *flat)


def on_device(query_rows, key_rows, value_rows, block_lists, block_counts):
    head_count = lax.axis_size("head")
    seq_count = lax.axis_size("seq")
    seq_rank = lax.axis_index("seq")
    head_rank = lax.axis_index("head")
    rows = query_rows.shape[0]
    local_pairs = HEADS // 2 // head_count
    pair_table = jnp.arange(HEADS // 2, dtype=jnp.int32)
    groups = [[0], list(range(1, local_pairs - 1)), [local_pairs - 1]]
    groups = [group for group in groups if group] if local_pairs > 1 else [[0]]

    lists = block_lists.reshape(-1)
    counts = block_counts.reshape(-1)
    wanted = [shifted(lists, "seq", (seq_count - step) % seq_count) for step in range(1, seq_count)]

    def columns(array, rank, pair):
        at = lax.dynamic_slice_in_dim(pair_table, rank * local_pairs + pair, 1)[0] * PAIR
        return lax.dynamic_slice(array, (0, at), (rows, PAIR))

    def gathered(parts):
        pieces = []
        for step in range(head_count):
            rank = (head_rank + step) % head_count
            piece = jnp.concatenate([columns(array, rank, pair) for array, pair in parts], axis=1)
            pieces.append(piece if step == 0 else shifted(piece, "head", step))
        return pieces

    tiles, sends = [], []
    for number, group in enumerate(groups):
        parts = [(array, pair) for pair in group for array in (key_rows, value_rows)]
        pieces = gathered(parts)
        mine = lax.dynamic_slice_in_dim(pair_table, head_rank * local_pairs + group[0], len(group))
        places = jnp.concatenate([jnp.stack([seq_rank, head_rank]).astype(jnp.int32), mine])
        tile_pairs, picked = pick_blocks(places, counts, wanted, pieces, len(group))
        blocks = [shifted(picked[step - 1], "seq", step) for step in range(1, seq_count)]
        tiles.append((places, tile_pairs, blocks))
    queries = gathered([(query_rows, pair) for pair in range(local_pairs)])

    results = []
    for group, (places, tile_pairs, blocks) in zip(groups, tiles):
        outs = attend(places, counts, tile_pairs, queries, blocks, group[0], len(group))
        results.append(
            [outs[0]]
            + [shifted(outs[head_count - step], "head", step) for step in range(1, head_count)]
        )
    places = jnp.concatenate([head_rank.astype(jnp.int32)[None], pair_table])
    return lay_out(places, results, groups, rows)


def solution(mesh):
    in_specs = (
        P(("parts", "seq", "head"), None),
        P(("parts", "seq", "head"), None),
        P(("parts", "seq", "head"), None),
        P("parts", "seq", None, None),
        P("parts", None, None),
    )
    out_specs = P(("parts", "seq", "head"), None)
    return jax.shard_map(
        on_device, mesh=mesh, in_specs=in_specs, out_specs=out_specs, check_vma=False
    )
```

time: 294 us -> 232 us (0.79)
  the two profiles are of different devices: /device:TPU:0 before, /device:TPU:13 now
where the time goes in v1:
time: 232 us; the launch traced here: 231 us
  waiting for transfers between devices  95.5 us (41%)
  Pallas kernels  84.1 us (36%)
  starting transfers between devices  32.8 us (14%)
  local copies, waits for them, and re-layouts  10.3 us (4%)
  other arithmetic  7.92 us (3%)
    ppermute x33, waiting for transfers between devices, shifted(): lax.ppermute(array, axis, [(i, (i + step) % size) for i in range(size)])  95.5 us
    pallas_call x1, Pallas kernels, lay_out(): pl.pallas_call(functools.partial(lay_kernel, head_count, groups), out_sha...  49.6 us
    ppermute x33, starting transfers between devices, shifted(): lax.ppermute(array, axis, [(i, (i + step) % size) for i in range(size)])  32.8 us
    pallas_call x3, Pallas kernels, attend(): pl.pallas_call(functools.partial(attend_kernel, head_count, seq_count), g...  29.9 us
    concatenate x16, other arithmetic, gathered(): jnp.concatenate([columns(array, rank, pair) for array, pair in parts], ax...  7.04 us
    unnamed x52, local copies, waits for them, and re-layouts  5.98 us
    pallas_call x3, Pallas kernels, pick_blocks(): pl.pallas_call(functools.partial(pick_kernel, head_count, seq_count, slot...  4.69 us
  transfers between devices with their start and end apart: 33, of which 11 were waited for; matrix products, arithmetic and copies ran while one was open for 5% of the time, Pallas kernels for 15%

profile of v1, /device:TPU:13, one launch (start us, length us, event | category | flops | bytes accessed | tf_op | source)
XLA Modules:
  0.0 231.2 jit_solution(17664522498301892442)
XLA Ops:
  0.0 0.8 copy.7
  1.0 1.3 collective-permute-start.2
  2.4 1.1 collective-permute-start.1
  3.5 1.4 collective-permute-start
  4.8 3.0 %constant_dynamic-slice_fusion = (bf16[192,256]{1,0:T(8,128)(2,1)S(1)}, bf16[192,256]{1,0:T(8,128)(2,1)S(1)}, bf16[192,256]{1,0:T(8,128)(2,1)S(1)}, bf16[192,256...) fusion(bf16[192,4096]{1,0:T(8,128)(2,1)} %param.7, ...), kind=kLoop, calls=%fused_computation.16 | loop fusion | bytes 6291520 | tf_op jit(solution)/shard_map/dynamic_slice | solution.py:287
  7.9 1.3 collective-permute-start.25
  9.2 2.0 collective-permute-start.3
  11.2 0.9 constant_dynamic-slice_fusion.27
  12.1 0.8 pad_maximum_fusion.2
  12.9 0.8 pad_maximum_fusion.1
  13.7 0.8 pad_maximum_fusion.7
  14.5 0.8 pad_maximum_fusion.6
  15.4 1.3 collective-permute-start.4
  16.7 1.8 collective-permute-start.6
  19.0 0.8 pad_maximum_fusion.5
  19.8 2.3 collective-permute-done.4.refs_5_
  22.0 1.2 collective-permute-start.7
  23.2 3.7 %collective-permute-done.5.refs_6_ = bf16[192,512]{1,0:T(8,128)(2,1)S(1)} collective-permute-done((bf16[192,512]{1,0:T(8,128)(2,1)S(1)}, bf16[192,512]{1,0:T(8,128)(2,1)S(1)}, u32[]{:S(2)}, u32[]{:S(2)}) %collective-permute-start.5) | collective-permute-done | bytes 196640 | tf_op jit(solution)/shard_map/ppermute | solution.py:25
  26.9 7.0 %collective-permute-done.24.refs_4_ = bf16[192,512]{1,0:T(8,128)(2,1)S(1)} collective-permute-done((bf16[192,512]{1,0:T(8,128)(2,1)S(1)}, bf16[192,512]{1,0:T(8,128)(2,1)S(1)}, u32[]{:S(2)}, u32[]{:S(2)}) %collective-permute-start.24) | collective-permute-done | bytes 196640 | tf_op jit(solution)/shard_map/ppermute | solution.py:25
  33.9 2.9 %collective-permute-start.17 = (bf16[192,1024]{1,0:T(8,128)(2,1)}, bf16[192,1024]{1,0:T(8,128)(2,1)S(1)}, u32[]{:S(2)}, u32[]{:S(2)}) collective-permute-start(bf16[192,1024]{1,0:T(8,128)(2,1)} %pad_maximum_fusion.7), channel_id=1, source_target_pairs={{0,3},{1,0},{2,1},{3,2},{4,7},{5,4},{6,5},{7,6},{8,11},{9,8},{10,9... | collective-permute-start | bytes 1179656 | tf_op jit(solution)/shard_map/ppermute | solution.py:25
  36.8 1.7 pad_maximum_fusion.3
  38.9 1.9 pick_blocks.5
  40.8 2.3 %collective-permute-done.7.refs_2_ = bf16[192,1024]{1,0:T(8,128)(2,1)} collective-permute-done((bf16[192,1024]{1,0:T(8,128)(2,1)}, bf16[192,1024]{1,0:T(8,128)(2,1)}, u32[]{:S(2)}, u32[]{:S(2)}) %collective-permute-start.7) | collective-permute-done | bytes 393248 | tf_op jit(solution)/shard_map/ppermute | solution.py:25
  43.1 7.2 %collective-permute-done.15.refs_4_ = bf16[192,1024]{1,0:T(8,128)(2,1)S(1)} collective-permute-done((bf16[192,1024]{1,0:T(8,128)(2,1)}, bf16[192,1024]{1,0:T(8,128)(2,1)S(1)}, u32[]{:S(2)}, u32[]{:S(2)}) %collective-permute-start.15) | collective-permute-done | bytes 393248 | tf_op jit(solution)/shard_map/ppermute | solution.py:25
  50.4 1.7 pick_blocks.3
  52.1 0.9 copy-done.5
  53.0 0.7 copy-done.7
  53.7 0.7 copy-done.9
  54.4 5.4 %collective-permute-done.16.refs_5_ = bf16[192,1024]{1,0:T(8,128)(2,1)S(1)} collective-permute-done((bf16[192,1024]{1,0:T(8,128)(2,1)}, bf16[192,1024]{1,0:T(8,128)(2,1)S(1)}, u32[]{:S(2)}, u32[]{:S(2)}) %collective-permute-start.16) | collective-permute-done | bytes 393248 | tf_op jit(solution)/shard_map/ppermute | solution.py:25
  59.9 1.2 collective-permute-start.29
  61.4 1.2 pad_maximum_fusion.4.refs_3_
  62.7 1.1 pick_blocks.4
  63.9 3.3 %collective-permute-start.19 = (bf16[8,128,256]{2,1,0:T(8,128)(2,1)S(1)}, bf16[8,128,256]{2,1,0:T(8,128)(2,1)S(1)}, u32[]{:S(2)}, u32[]{:S(2)}) collective-permute-start(bf16[8,128,256]{2,1,0:T(8,128)(2,1)S(1)} %get-tuple-element.39), channel_id=1, source_target_pairs={{0,8},{4,12},{8,0},{12,4},{1,9},{5,13},{9,1},{13,5},{2,10},{6,14},... | collective-permute-start | bytes 1572872 | tf_op jit(solution)/shard_map/ppermute | solution.py:25
  67.3 31.6 %collective-permute-done.29.refs_6_ = bf16[4,128,256]{2,1,0:T(8,128)(2,1)} collective-permute-done((bf16[4,128,256]{2,1,0:T(8,128)(2,1)}, bf16[4,128,256]{2,1,0:T(8,128)(2,1)}, u32[]{:S(2)}, u32[]{:S(2)}) %collective-permute-start.29) | collective-permute-done | bytes 262176 | tf_op jit(solution)/shard_map/ppermute | solution.py:25
  99.4 10.0 %attend.5 = (bf16[192,256]{1,0:T(8,128)(2,1)S(1)}, bf16[192,256]{1,0:T(8,128)(2,1)S(1)}, bf16[192,256]{1,0:T(8,128)(2,1)S(1)}, bf16[192,256]{1,0:T(8,128)(2,1)S(1)}) custom-call(s32[3]{0:T(128)S(1)} %pad_add_fusion.4.place_ref, s32[512]{0:T(512)S(1)} %reshape.40.counts_ref, bf16[2,768,256]{2,1,0:T(8,128)(2,1)S(1)} %copy-done.4, ...), custom_call_target="tpu_custom_call" | custom-call | flops 1207959552 | bytes 3145728 | tf_op jit(solution)/shard_map/attend/pallas_call | solution.py:206
  110.1 24.4 %collective-permute-done.10.refs_5_ = bf16[4,128,256]{2,1,0:T(8,128)(2,1)S(1)} collective-permute-done((bf16[4,128,256]{2,1,0:T(8,128)(2,1)S(1)}, bf16[4,128,256]{2,1,0:T(8,128)(2,1)S(1)}, u32[]{:S(2)}, u32[]{:S(2)}) %collective-permute-start.10) | collective-permute-done | bytes 262176 | tf_op jit(solution)/shard_map/ppermute | solution.py:25
  134.4 1.8 collective-permute-start.30
  136.3 1.9 collective-permute-done.11.refs_6_
  138.7 8.8 %attend.3 = (bf16[192,256]{1,0:T(8,128)(2,1)S(1)}, bf16[192,256]{1,0:T(8,128)(2,1)S(1)}, bf16[192,256]{1,0:T(8,128)(2,1)S(1)}, bf16[192,256]{1,0:T(8,128)(2,1)S(1)}) custom-call(s32[3]{0:T(128)S(1)} %pad_add_fusion.1.place_ref, s32[512]{0:T(512)S(1)} %reshape.40.counts_ref, bf16[2,768,256]{2,1,0:T(8,128)(2,1)S(1)} %copy-done.6, ...), custom_call_target="tpu_custom_call" | custom-call | flops 1207959552 | bytes 3145728 | tf_op jit(solution)/shard_map/attend/pallas_call | solution.py:206
  148.2 0.9 collective-permute-start.32
  149.1 1.0 collective-permute-start.12
  150.1 11.0 %attend.4 = (bf16[192,512]{1,0:T(8,128)(2,1)S(1)}, bf16[192,512]{1,0:T(8,128)(2,1)S(1)}, bf16[192,512]{1,0:T(8,128)(2,1)S(1)}, bf16[192,512]{1,0:T(8,128)(2,1)S(1)}) custom-call(s32[4]{0:T(128)S(1)} %pad_add_fusion.3.place_ref, s32[512]{0:T(512)S(1)} %reshape.40.counts_ref, bf16[4,768,256]{2,1,0:T(8,128)(2,1)S(1)} %get-tuple-element.37.tile_ref, ...), custom_call_target="tpu_custom_call" | custom-call | flops 2415919104 | bytes 6291456 | tf_op jit(solution)/shard_map/attend/pallas_call | solution.py:206
  161.8 2.4 %collective-permute-start.21 = (bf16[192,512]{1,0:T(8,128)(2,1)S(1)}, bf16[192,512]{1,0:T(8,128)(2,1)S(1)}, u32[]{:S(2)}, u32[]{:S(2)}) collective-permute-start(bf16[192,512]{1,0:T(8,128)(2,1)S(1)} %get-tuple-element.42), channel_id=1, source_target_pairs={{0,1},{1,2},{2,3},{3,0},{4,5},{5,6},{6,7},{7,4},{8,9},{9,10},{10,1... | collective-permute-start | bytes 589832 | tf_op jit(solution)/shard_map/ppermute | solution.py:25
  164.2 3.8 %collective-permute-start.22 = (bf16[192,512]{1,0:T(8,128)(2,1)S(1)}, bf16[192,512]{1,0:T(8,128)(2,1)S(1)}, u32[]{:S(2)}, u32[]{:S(2)}) collective-permute-start(bf16[192,512]{1,0:T(8,128)(2,1)S(1)} %get-tuple-element.43), channel_id=1, source_target_pairs={{0,2},{1,3},{2,0},{3,1},{4,6},{5,7},{6,4},{7,5},{8,10},{9,11},{10,... | collective-permute-start | bytes 589832 | tf_op jit(solution)/shard_map/ppermute | solution.py:25
  168.5 1.7 collective-permute-start.14
  170.9 8.4 %collective-permute-done.13.refs_2_ = bf16[192,256]{1,0:T(8,128)(2,1)S(1)} collective-permute-done((bf16[192,256]{1,0:T(8,128)(2,1)S(1)}, bf16[192,256]{1,0:T(8,128)(2,1)S(1)}, u32[]{:S(2)}, u32[]{:S(2)}) %collective-permute-start.13) | collective-permute-done | bytes 98336 | tf_op jit(solution)/shard_map/ppermute | solution.py:25
  179.2 1.4 collective-permute-done.14.refs_3_
  181.5 49.6 %lay_out.1 = bf16[192,4096]{1,0:T(8,128)(2,1)} custom-call(s32[17]{0:T(128)} %pad_add_fusion.place_ref, bf16[192,256]{1,0:T(8,128)(2,1)} %copy-done.2, bf16[192,256]{1,0:T(8,128)(2,1)} %copy-done.21, bf16[192,256]{1,0:T(8,128)(2,1)} %copy-done.22, bf16[192,256]{1,0:T(8,128)(2,1)} %copy-done.23, bf16[192,512]{1,0:T(8,128)(2,1)} %copy-done, ...), custom_call_target="tpu_custom_call" | custom-call | tf_op jit(solution)/shard_map/lay_out/pallas_call | solution.py:260
  (104 shorter events, 6.8 us)
Async XLA Ops:
  1.0 14.3 %collective-permute-start.2 = (s32[384]{0:T(512)S(1)}, s32[384]{0:T(512)S(1)}, u32[]{:S(2)}, u32[]{:S(2)}) collective-permute-start(s32[384]{0:T(512)S(1)} %reshape.41), channel_id=1, source_target_pairs={{0,4},{4,8},{8,12},{12,0},{1,5},{5,9},{9,13},{13,1},{2,6},{6,10},{... | collective-permute-start | bytes 4616 | tf_op jit(solution)/shard_map/ppermute | solution.py:25
  2.4 14.3 %collective-permute-start.1 = (s32[384]{0:T(512)S(1)}, s32[384]{0:T(512)S(1)}, u32[]{:S(2)}, u32[]{:S(2)}) collective-permute-start(s32[384]{0:T(512)S(1)} %reshape.41), channel_id=1, source_target_pairs={{0,8},{4,12},{8,0},{12,4},{1,9},{5,13},{9,1},{13,5},{2,10},{6,14},... | collective-permute-start | bytes 4616 | tf_op jit(solution)/shard_map/ppermute | solution.py:25
  3.5 13.2 %collective-permute-start = (s32[384]{0:T(512)S(1)}, s32[384]{0:T(512)S(1)}, u32[]{:S(2)}, u32[]{:S(2)}) collective-permute-start(s32[384]{0:T(512)S(1)} %reshape.41), channel_id=1, source_target_pairs={{0,12},{4,0},{8,4},{12,8},{1,13},{5,1},{9,5},{13,9},{2,14},{6,2},{... | collective-permute-start | bytes 4616 | tf_op jit(solution)/shard_map/ppermute | solution.py:25
  4.8 6.3 %copy-start.11 = (bf16[192,4096]{1,0:T(8,128)(2,1)S(1)}, bf16[192,4096]{1,0:T(8,128)(2,1)}, u32[]{:S(2)}) copy-start(bf16[192,4096]{1,0:T(8,128)(2,1)} %param.5) | copy-start | bytes 4718596
  7.9 10.6 %collective-permute-start.25 = (bf16[192,512]{1,0:T(8,128)(2,1)S(1)}, bf16[192,512]{1,0:T(8,128)(2,1)S(1)}, u32[]{:S(2)}, u32[]{:S(2)}) collective-permute-start(bf16[192,512]{1,0:T(8,128)(2,1)S(1)} %pad_maximum_fusion.14), channel_id=1, source_target_pairs={{0,2},{1,3},{2,0},{3,1},{4,6},{5,7},{6,4},{7,5},{8,10},{9,11},{10,... | collective-permute-start | bytes 589832 | tf_op jit(solution)/shard_map/ppermute | solution.py:25
  9.2 9.4 %collective-permute-start.3 = (bf16[192,512]{1,0:T(8,128)(2,1)S(1)}, bf16[192,512]{1,0:T(8,128)(2,1)S(1)}, u32[]{:S(2)}, u32[]{:S(2)}) collective-permute-start(bf16[192,512]{1,0:T(8,128)(2,1)S(1)} %pad_maximum_fusion.9), channel_id=1, source_target_pairs={{0,1},{1,2},{2,3},{3,0},{4,5},{5,6},{6,7},{7,4},{8,9},{9,10},{10,1... | collective-permute-start | bytes 589832 | tf_op jit(solution)/shard_map/ppermute | solution.py:25
  15.3 23.3 %copy-start.24 = (s32[32,4,4]{0,2,1:T(4,128)S(1)}, s32[32,4,4]{0,2,1:T(4,128)}, u32[]{:S(2)}) copy-start(s32[32,4,4]{0,2,1:T(4,128)} %param.9) | copy-start | bytes 6148
  15.4 6.7 %collective-permute-start.4 = (bf16[192,512]{1,0:T(8,128)(2,1)S(1)}, bf16[192,512]{1,0:T(8,128)(2,1)S(1)}, u32[]{:S(2)}, u32[]{:S(2)}) collective-permute-start(bf16[192,512]{1,0:T(8,128)(2,1)S(1)} %pad_maximum_fusion.10), channel_id=1, source_target_pairs={{0,2},{1,3},{2,0},{3,1},{4,6},{5,7},{6,4},{7,5},{8,10},{9,11},{10,... | collective-permute-start | bytes 589832 | tf_op jit(solution)/shard_map/ppermute | solution.py:25
  16.6 10.2 %collective-permute-start.5 = (bf16[192,512]{1,0:T(8,128)(2,1)S(1)}, bf16[192,512]{1,0:T(8,128)(2,1)S(1)}, u32[]{:S(2)}, u32[]{:S(2)}) collective-permute-start(bf16[192,512]{1,0:T(8,128)(2,1)S(1)} %pad_maximum_fusion.11), channel_id=1, source_target_pairs={{0,3},{1,0},{2,1},{3,2},{4,7},{5,4},{6,5},{7,6},{8,11},{9,8},{10,9... | collective-permute-start | bytes 589832 | tf_op jit(solution)/shard_map/ppermute | solution.py:25
  16.7 21.9 %collective-permute-start.6 = (bf16[192,1024]{1,0:T(8,128)(2,1)}, bf16[192,1024]{1,0:T(8,128)(2,1)S(1)}, u32[]{:S(2)}, u32[]{:S(2)}) collective-permute-start(bf16[192,1024]{1,0:T(8,128)(2,1)} %pad_maximum_fusion.1), channel_id=1, source_target_pairs={{0,1},{1,2},{2,3},{3,0},{4,5},{5,6},{6,7},{7,4},{8,9},{9,10},{10,1... | collective-permute-start | bytes 1179656 | tf_op jit(solution)/shard_map/ppermute | solution.py:25
  18.5 15.5 %collective-permute-start.24 = (bf16[192,512]{1,0:T(8,128)(2,1)S(1)}, bf16[192,512]{1,0:T(8,128)(2,1)S(1)}, u32[]{:S(2)}, u32[]{:S(2)}) collective-permute-start(bf16[192,512]{1,0:T(8,128)(2,1)S(1)} %pad_maximum_fusion.13), channel_id=1, source_target_pairs={{0,1},{1,2},{2,3},{3,0},{4,5},{5,6},{6,7},{7,4},{8,9},{9,10},{10,1... | collective-permute-start | bytes 589832 | tf_op jit(solution)/shard_map/ppermute | solution.py:25
  18.5 15.4 %collective-permute-start.26 = (bf16[192,512]{1,0:T(8,128)(2,1)S(1)}, bf16[192,512]{1,0:T(8,128)(2,1)S(1)}, u32[]{:S(2)}, u32[]{:S(2)}) collective-permute-start(bf16[192,512]{1,0:T(8,128)(2,1)S(1)} %pad_maximum_fusion.15), channel_id=1, source_target_pairs={{0,3},{1,0},{2,1},{3,2},{4,7},{5,4},{6,5},{7,6},{8,11},{9,8},{10,9... | collective-permute-start | bytes 589832 | tf_op jit(solution)/shard_map/ppermute | solution.py:25
  22.0 21.1 %collective-permute-start.7 = (bf16[192,1024]{1,0:T(8,128)(2,1)}, bf16[192,1024]{1,0:T(8,128)(2,1)}, u32[]{:S(2)}, u32[]{:S(2)}) collective-permute-start(bf16[192,1024]{1,0:T(8,128)(2,1)} %pad_maximum_fusion.2), channel_id=1, source_target_pairs={{0,2},{1,3},{2,0},{3,1},{4,6},{5,7},{6,4},{7,5},{8,10},{9,11},{10,... | collective-permute-start | bytes 1179656 | tf_op jit(solution)/shard_map/ppermute | solution.py:25
  26.9 23.4 %collective-permute-start.15 = (bf16[192,1024]{1,0:T(8,128)(2,1)}, bf16[192,1024]{1,0:T(8,128)(2,1)S(1)}, u32[]{:S(2)}, u32[]{:S(2)}) collective-permute-start(bf16[192,1024]{1,0:T(8,128)(2,1)} %pad_maximum_fusion.5), channel_id=1, source_target_pairs={{0,1},{1,2},{2,3},{3,0},{4,5},{5,6},{6,7},{7,4},{8,9},{9,10},{10,1... | collective-permute-start | bytes 1179656 | tf_op jit(solution)/shard_map/ppermute | solution.py:25
  33.9 25.9 %collective-permute-start.16 = (bf16[192,1024]{1,0:T(8,128)(2,1)}, bf16[192,1024]{1,0:T(8,128)(2,1)S(1)}, u32[]{:S(2)}, u32[]{:S(2)}) collective-permute-start(bf16[192,1024]{1,0:T(8,128)(2,1)} %pad_maximum_fusion.6), channel_id=1, source_target_pairs={{0,2},{1,3},{2,0},{3,1},{4,6},{5,7},{6,4},{7,5},{8,10},{9,11},{10,... | collective-permute-start | bytes 1179656 | tf_op jit(solution)/shard_map/ppermute | solution.py:25
  33.9 27.2 %collective-permute-start.17 = (bf16[192,1024]{1,0:T(8,128)(2,1)}, bf16[192,1024]{1,0:T(8,128)(2,1)S(1)}, u32[]{:S(2)}, u32[]{:S(2)}) collective-permute-start(bf16[192,1024]{1,0:T(8,128)(2,1)} %pad_maximum_fusion.7), channel_id=1, source_target_pairs={{0,3},{1,0},{2,1},{3,2},{4,7},{5,4},{6,5},{7,6},{8,11},{9,8},{10,9... | collective-permute-start | bytes 1179656 | tf_op jit(solution)/shard_map/ppermute | solution.py:25
  38.6 25.2 %collective-permute-start.8 = (bf16[192,1024]{1,0:T(8,128)(2,1)}, bf16[192,1024]{1,0:T(8,128)(2,1)}, u32[]{:S(2)}, u32[]{:S(2)}) collective-permute-start(bf16[192,1024]{1,0:T(8,128)(2,1)} %pad_maximum_fusion.3), channel_id=1, source_target_pairs={{0,3},{1,0},{2,1},{3,2},{4,7},{5,4},{6,5},{7,6},{8,11},{9,8},{10,9... | collective-permute-start | bytes 1179656 | tf_op jit(solution)/shard_map/ppermute | solution.py:25
  40.8 20.6 %copy-start.3 = (bf16[2,768,256]{2,1,0:T(8,128)(2,1)}, bf16[2,768,256]{2,1,0:T(8,128)(2,1)S(1)}, u32[]{:S(2)}) copy-start(bf16[2,768,256]{2,1,0:T(8,128)(2,1)S(1)} %get-tuple-element.45.tile_ref) | copy-start | bytes 2359300
  43.1 20.8 %collective-permute-start.27 = (bf16[4,128,256]{2,1,0:T(8,128)(2,1)}, bf16[4,128,256]{2,1,0:T(8,128)(2,1)S(1)}, u32[]{:S(2)}, u32[]{:S(2)}) collective-permute-start(bf16[4,128,256]{2,1,0:T(8,128)(2,1)} %get-tuple-element.46), channel_id=1, source_target_pairs={{0,4},{4,8},{8,12},{12,0},{1,5},{5,9},{9,13},{13,1},{2,6},{6,10},{... | collective-permute-start | bytes 786440 | tf_op jit(solution)/shard_map/ppermute | solution.py:25
  50.3 16.9 %collective-permute-start.28 = (bf16[4,128,256]{2,1,0:T(8,128)(2,1)}, bf16[4,128,256]{2,1,0:T(8,128)(2,1)}, u32[]{:S(2)}, u32[]{:S(2)}) collective-permute-start(bf16[4,128,256]{2,1,0:T(8,128)(2,1)} %get-tuple-element.47), channel_id=1, source_target_pairs={{0,8},{4,12},{8,0},{12,4},{1,9},{5,13},{9,1},{13,5},{2,10},{6,14},... | collective-permute-start | bytes 786440 | tf_op jit(solution)/shard_map/ppermute | solution.py:25
  50.4 48.9 %copy-start.12 = (bf16[192,256]{1,0:T(8,128)(2,1)S(1)}, bf16[192,256]{1,0:T(8,128)(2,1)}, u32[]{:S(2)}) copy-start(bf16[192,256]{1,0:T(8,128)(2,1)} %get-tuple-element.96) | copy-start | bytes 294916
  54.4 44.9 %copy-start.13 = (bf16[192,256]{1,0:T(8,128)(2,1)S(1)}, bf16[192,256]{1,0:T(8,128)(2,1)}, u32[]{:S(2)}) copy-start(bf16[192,256]{1,0:T(8,128)(2,1)} %get-tuple-element.97) | copy-start | bytes 294916
  54.4 44.9 %copy-start.14 = (bf16[192,256]{1,0:T(8,128)(2,1)S(1)}, bf16[192,256]{1,0:T(8,128)(2,1)}, u32[]{:S(2)}) copy-start(bf16[192,256]{1,0:T(8,128)(2,1)} %get-tuple-element.98) | copy-start | bytes 294916
  59.9 39.0 %collective-permute-start.29 = (bf16[4,128,256]{2,1,0:T(8,128)(2,1)}, bf16[4,128,256]{2,1,0:T(8,128)(2,1)}, u32[]{:S(2)}, u32[]{:S(2)}) collective-permute-start(bf16[4,128,256]{2,1,0:T(8,128)(2,1)} %get-tuple-element.48), channel_id=1, source_target_pairs={{0,12},{4,0},{8,4},{12,8},{1,13},{5,1},{9,5},{13,9},{2,14},{6,2},{... | collective-permute-start | bytes 786440 | tf_op jit(solution)/shard_map/ppermute | solution.py:25
  61.1 37.8 %collective-permute-start.9 = (bf16[4,128,256]{2,1,0:T(8,128)(2,1)}, bf16[4,128,256]{2,1,0:T(8,128)(2,1)}, u32[]{:S(2)}, u32[]{:S(2)}) collective-permute-start(bf16[4,128,256]{2,1,0:T(8,128)(2,1)} %get-tuple-element.30), channel_id=1, source_target_pairs={{0,4},{4,8},{8,12},{12,0},{1,5},{5,9},{9,13},{13,1},{2,6},{6,10},{... | collective-permute-start | bytes 786440 | tf_op jit(solution)/shard_map/ppermute | solution.py:25
  61.4 38.0 %copy-start.4 = (bf16[2,768,256]{2,1,0:T(8,128)(2,1)S(1)}, bf16[2,768,256]{2,1,0:T(8,128)(2,1)}, u32[]{:S(2)}) copy-start(bf16[2,768,256]{2,1,0:T(8,128)(2,1)} %copy-done.3) | copy-start | bytes 2359300
  62.5 36.4 %copy-start.10 = (bf16[4,128,256]{2,1,0:T(8,128)(2,1)S(1)}, bf16[4,128,256]{2,1,0:T(8,128)(2,1)}, u32[]{:S(2)}) copy-start(bf16[4,128,256]{2,1,0:T(8,128)(2,1)} %copy-done.9) | copy-start | bytes 786436
  62.5 36.4 %copy-start.8 = (bf16[4,128,256]{2,1,0:T(8,128)(2,1)S(1)}, bf16[4,128,256]{2,1,0:T(8,128)(2,1)}, u32[]{:S(2)}) copy-start(bf16[4,128,256]{2,1,0:T(8,128)(2,1)} %copy-done.7) | copy-start | bytes 786436
  63.8 84.4 %collective-permute-start.18 = (bf16[8,128,256]{2,1,0:T(8,128)(2,1)S(1)}, bf16[8,128,256]{2,1,0:T(8,128)(2,1)S(1)}, u32[]{:S(2)}, u32[]{:S(2)}) collective-permute-start(bf16[8,128,256]{2,1,0:T(8,128)(2,1)S(1)} %get-tuple-element.38), channel_id=1, source_target_pairs={{0,4},{4,8},{8,12},{12,0},{1,5},{5,9},{9,13},{13,1},{2,6},{6,10},{... | collective-permute-start | bytes 1572872 | tf_op jit(solution)/shard_map/ppermute | solution.py:25
  63.9 85.2 %collective-permute-start.19 = (bf16[8,128,256]{2,1,0:T(8,128)(2,1)S(1)}, bf16[8,128,256]{2,1,0:T(8,128)(2,1)S(1)}, u32[]{:S(2)}, u32[]{:S(2)}) collective-permute-start(bf16[8,128,256]{2,1,0:T(8,128)(2,1)S(1)} %get-tuple-element.39), channel_id=1, source_target_pairs={{0,8},{4,12},{8,0},{12,4},{1,9},{5,13},{9,1},{13,5},{2,10},{6,14},... | collective-permute-start | bytes 1572872 | tf_op jit(solution)/shard_map/ppermute | solution.py:25
  67.2 82.9 %collective-permute-start.20 = (bf16[8,128,256]{2,1,0:T(8,128)(2,1)S(1)}, bf16[8,128,256]{2,1,0:T(8,128)(2,1)S(1)}, u32[]{:S(2)}, u32[]{:S(2)}) collective-permute-start(bf16[8,128,256]{2,1,0:T(8,128)(2,1)S(1)} %get-tuple-element.40), channel_id=1, source_target_pairs={{0,12},{4,0},{8,4},{12,8},{1,13},{5,1},{9,5},{13,9},{2,14},{6,2},{... | collective-permute-start | bytes 1572872 | tf_op jit(solution)/shard_map/ppermute | solution.py:25
  98.9 35.5 %collective-permute-start.10 = (bf16[4,128,256]{2,1,0:T(8,128)(2,1)S(1)}, bf16[4,128,256]{2,1,0:T(8,128)(2,1)S(1)}, u32[]{:S(2)}, u32[]{:S(2)}) collective-permute-start(bf16[4,128,256]{2,1,0:T(8,128)(2,1)S(1)} %copy-done.10), channel_id=1, source_target_pairs={{0,8},{4,12},{8,0},{12,4},{1,9},{5,13},{9,1},{13,5},{2,10},{6,14},... | collective-permute-start | bytes 786440 | tf_op jit(solution)/shard_map/ppermute | solution.py:25
  98.9 39.2 %collective-permute-start.11 = (bf16[4,128,256]{2,1,0:T(8,128)(2,1)S(1)}, bf16[4,128,256]{2,1,0:T(8,128)(2,1)S(1)}, u32[]{:S(2)}, u32[]{:S(2)}) collective-permute-start(bf16[4,128,256]{2,1,0:T(8,128)(2,1)S(1)} %copy-done.8), channel_id=1, source_target_pairs={{0,12},{4,0},{8,4},{12,8},{1,13},{5,1},{9,5},{13,9},{2,14},{6,2},{... | collective-permute-start | bytes 786440 | tf_op jit(solution)/shard_map/ppermute | solution.py:25
  99.4 39.3 %copy-start.6 = (bf16[2,768,256]{2,1,0:T(8,128)(2,1)S(1)}, bf16[2,768,256]{2,1,0:T(8,128)(2,1)}, u32[]{:S(2)}) copy-start(bf16[2,768,256]{2,1,0:T(8,128)(2,1)} %copy-done.5) | copy-start | bytes 2359300
  134.4 29.8 %collective-permute-start.30 = (bf16[192,256]{1,0:T(8,128)(2,1)S(1)}, bf16[192,256]{1,0:T(8,128)(2,1)S(1)}, u32[]{:S(2)}, u32[]{:S(2)}) collective-permute-start(bf16[192,256]{1,0:T(8,128)(2,1)S(1)} %get-tuple-element.50), channel_id=1, source_target_pairs={{0,1},{1,2},{2,3},{3,0},{4,5},{5,6},{6,7},{7,4},{8,9},{9,10},{10,1... | collective-permute-start | bytes 294920 | tf_op jit(solution)/shard_map/ppermute | solution.py:25
  138.1 29.9 %collective-permute-start.31 = (bf16[192,256]{1,0:T(8,128)(2,1)S(1)}, bf16[192,256]{1,0:T(8,128)(2,1)S(1)}, u32[]{:S(2)}, u32[]{:S(2)}) collective-permute-start(bf16[192,256]{1,0:T(8,128)(2,1)S(1)} %get-tuple-element.51), channel_id=1, source_target_pairs={{0,2},{1,3},{2,0},{3,1},{4,6},{5,7},{6,4},{7,5},{8,10},{9,11},{10,... | collective-permute-start | bytes 294920 | tf_op jit(solution)/shard_map/ppermute | solution.py:25
  148.2 19.8 %collective-permute-start.32 = (bf16[192,256]{1,0:T(8,128)(2,1)S(1)}, bf16[192,256]{1,0:T(8,128)(2,1)S(1)}, u32[]{:S(2)}, u32[]{:S(2)}) collective-permute-start(bf16[192,256]{1,0:T(8,128)(2,1)S(1)} %get-tuple-element.52), channel_id=1, source_target_pairs={{0,3},{1,0},{2,1},{3,2},{4,7},{5,4},{6,5},{7,6},{8,11},{9,8},{10,9... | collective-permute-start | bytes 294920 | tf_op jit(solution)/shard_map/ppermute | solution.py:25
  149.1 19.4 %collective-permute-start.12 = (bf16[192,256]{1,0:T(8,128)(2,1)S(1)}, bf16[192,256]{1,0:T(8,128)(2,1)S(1)}, u32[]{:S(2)}, u32[]{:S(2)}) collective-permute-start(bf16[192,256]{1,0:T(8,128)(2,1)S(1)} %get-tuple-element.34), channel_id=1, source_target_pairs={{0,1},{1,2},{2,3},{3,0},{4,5},{5,6},{6,7},{7,4},{8,9},{9,10},{10,1... | collective-permute-start | bytes 294920 | tf_op jit(solution)/shard_map/ppermute | solution.py:25
  161.8 18.8 %collective-permute-start.21 = (bf16[192,512]{1,0:T(8,128)(2,1)S(1)}, bf16[192,512]{1,0:T(8,128)(2,1)S(1)}, u32[]{:S(2)}, u32[]{:S(2)}) collective-permute-start(bf16[192,512]{1,0:T(8,128)(2,1)S(1)} %get-tuple-element.42), channel_id=1, source_target_pairs={{0,1},{1,2},{2,3},{3,0},{4,5},{5,6},{6,7},{7,4},{8,9},{9,10},{10,1... | collective-permute-start | bytes 589832 | tf_op jit(solution)/shard_map/ppermute | solution.py:25
  164.2 16.4 %copy-start.18 = (bf16[192,256]{1,0:T(8,128)(2,1)}, bf16[192,256]{1,0:T(8,128)(2,1)S(1)}, u32[]{:S(2)}) copy-start(bf16[192,256]{1,0:T(8,128)(2,1)S(1)} %collective-permute-done.30.refs_9_) | copy-start | bytes 294916
  164.2 16.4 %collective-permute-start.22 = (bf16[192,512]{1,0:T(8,128)(2,1)S(1)}, bf16[192,512]{1,0:T(8,128)(2,1)S(1)}, u32[]{:S(2)}, u32[]{:S(2)}) collective-permute-start(bf16[192,512]{1,0:T(8,128)(2,1)S(1)} %get-tuple-element.43), channel_id=1, source_target_pairs={{0,2},{1,3},{2,0},{3,1},{4,6},{5,7},{6,4},{7,5},{8,10},{9,11},{10,... | collective-permute-start | bytes 589832 | tf_op jit(solution)/shard_map/ppermute | solution.py:25
  168.1 12.6 %copy-start.19 = (bf16[192,256]{1,0:T(8,128)(2,1)}, bf16[192,256]{1,0:T(8,128)(2,1)S(1)}, u32[]{:S(2)}) copy-start(bf16[192,256]{1,0:T(8,128)(2,1)S(1)} %collective-permute-done.31.refs_10_) | copy-start | bytes 294916
  168.1 12.5 %collective-permute-start.23 = (bf16[192,512]{1,0:T(8,128)(2,1)S(1)}, bf16[192,512]{1,0:T(8,128)(2,1)S(1)}, u32[]{:S(2)}, u32[]{:S(2)}) collective-permute-start(bf16[192,512]{1,0:T(8,128)(2,1)S(1)} %get-tuple-element.44), channel_id=1, source_target_pairs={{0,3},{1,0},{2,1},{3,2},{4,7},{5,4},{6,5},{7,6},{8,11},{9,8},{10,9... | collective-permute-start | bytes 589832 | tf_op jit(solution)/shard_map/ppermute | solution.py:25
  168.1 12.6 %copy-start.20 = (bf16[192,256]{1,0:T(8,128)(2,1)}, bf16[192,256]{1,0:T(8,128)(2,1)S(1)}, u32[]{:S(2)}) copy-start(bf16[192,256]{1,0:T(8,128)(2,1)S(1)} %collective-permute-done.32.refs_11_) | copy-start | bytes 294916
  168.1 11.1 %collective-permute-start.13 = (bf16[192,256]{1,0:T(8,128)(2,1)S(1)}, bf16[192,256]{1,0:T(8,128)(2,1)S(1)}, u32[]{:S(2)}, u32[]{:S(2)}) collective-permute-start(bf16[192,256]{1,0:T(8,128)(2,1)S(1)} %get-tuple-element.35), channel_id=1, source_target_pairs={{0,2},{1,3},{2,0},{3,1},{4,6},{5,7},{6,4},{7,5},{8,10},{9,11},{10,... | collective-permute-start | bytes 294920 | tf_op jit(solution)/shard_map/ppermute | solution.py:25
  168.5 12.1 %copy-start.21 = (bf16[192,256]{1,0:T(8,128)(2,1)}, bf16[192,256]{1,0:T(8,128)(2,1)S(1)}, u32[]{:S(2)}) copy-start(bf16[192,256]{1,0:T(8,128)(2,1)S(1)} %collective-permute-done.12.refs_1_) | copy-start | bytes 294916
  168.5 12.0 %collective-permute-start.14 = (bf16[192,256]{1,0:T(8,128)(2,1)S(1)}, bf16[192,256]{1,0:T(8,128)(2,1)S(1)}, u32[]{:S(2)}, u32[]{:S(2)}) collective-permute-start(bf16[192,256]{1,0:T(8,128)(2,1)S(1)} %get-tuple-element.36), channel_id=1, source_target_pairs={{0,3},{1,0},{2,1},{3,2},{4,7},{5,4},{6,5},{7,6},{8,11},{9,8},{10,9... | collective-permute-start | bytes 294920 | tf_op jit(solution)/shard_map/ppermute | solution.py:25
  179.2 1.4 copy-start.22
  (10 other events, 7.2 us)

commit v2 on v1

v2 whole, which is shorter than its diff:
```python
import functools
import math

import jax
import jax.numpy as jnp
from jax import lax
from jax.experimental import pallas as pl
from jax.experimental.pallas import tpu as pltpu
from jax.sharding import PartitionSpec as P

HEADS = 32
DH = 128
BLOCK = 128
MOST = 3
PAIR_MOST = 4
TILE = 768
PAIR = 2 * DH
OWN_BLOCKS = TILE // BLOCK
VMEM_LIMIT = 32 * 1024 * 1024
SMEM = pltpu.SMEM


def shifted(array, axis, step):
    size = lax.axis_size(axis)
    return lax.ppermute(array, axis, [(i, (i + step) % size) for i in range(size)])


def vmem_spec():
    return pl.BlockSpec(memory_space=pltpu.VMEM)


def smem_spec():
    return pl.BlockSpec(memory_space=SMEM)


def gather_kernel(table_ref, *refs):
    out_ref = refs[-1]
    for at, ref in enumerate(refs[:-1]):
        out_ref[0, :, at * PAIR : (at + 1) * PAIR] = ref[...]


def gather_columns(table, parts, head_count, local_pairs):
    rows = parts[0][0].shape[0]

    def column_of(pair):
        return lambda rank, table_ref: (0, table_ref[rank * local_pairs + pair])

    return pl.pallas_call(
        gather_kernel,
        grid_spec=pltpu.PrefetchScalarGridSpec(
            num_scalar_prefetch=1,
            grid=(head_count,),
            in_specs=[pl.BlockSpec((rows, PAIR), column_of(pair)) for _, pair in parts],
            out_specs=pl.BlockSpec((1, rows, len(parts) * PAIR), lambda rank, _: (rank, 0, 0)),
        ),
        out_shape=jax.ShapeDtypeStruct((head_count, rows, len(parts) * PAIR), jnp.bfloat16),
        compiler_params=pltpu.CompilerParams(vmem_limit_bytes=VMEM_LIMIT),
        cost_estimate=pl.CostEstimate(
            flops=0, bytes_accessed=len(parts) * TILE * PAIR * 4, transcendentals=0
        ),
        name="gather_columns",
    )(table, *[array for array, _ in parts])


def pick_kernel(seq_count, slots, place_ref, counts_ref, *refs):
    want_refs = refs[: seq_count - 1]
    tile_ref = refs[seq_count - 1]
    send_refs = refs[seq_count:]
    my_seq = place_ref[0]
    for step in range(1, seq_count):
        asker = lax.rem(my_seq + step, seq_count)
        for pair in range(slots):
            first = 2 * place_ref[2 + pair]
            first_count = counts_ref[(first * seq_count + asker) * seq_count + my_seq]
            both = first_count + counts_ref[((first + 1) * seq_count + asker) * seq_count + my_seq]
            for slot in range(PAIR_MOST):

                @pl.when(slot < both)
                def _():
                    half = jnp.where(slot < first_count, 0, 1)
                    entry = jnp.where(slot < first_count, slot, slot - first_count)
                    entry = jnp.clip(entry, 0, MOST - 1)
                    block = want_refs[step - 1][
                        ((first + half) * seq_count + my_seq) * MOST + entry
                    ]
                    span = pl.ds(pl.multiple_of(block * BLOCK, BLOCK), BLOCK)
                    base = pair * 2 * PAIR + half * DH
                    where = pair * PAIR_MOST + slot
                    send_refs[step - 1][where, :, :DH] = tile_ref[
                        span, pl.ds(pl.multiple_of(base, DH), DH)
                    ]
                    send_refs[step - 1][where, :, DH:] = tile_ref[
                        span, pl.ds(pl.multiple_of(base + PAIR, DH), DH)
                    ]


def pick_blocks(places, counts, wanted, tile, slots):
    seq_count = len(wanted) + 1
    return pl.pallas_call(
        functools.partial(pick_kernel, seq_count, slots),
        grid=(1,),
        out_shape=[jax.ShapeDtypeStruct((slots * PAIR_MOST, BLOCK, 2 * DH), jnp.bfloat16)]
        * (seq_count - 1),
        in_specs=[smem_spec()] * (seq_count + 1)
        + [pl.BlockSpec((TILE, slots * 2 * PAIR), lambda i: (0, 0))],
        out_specs=[pl.BlockSpec((slots * PAIR_MOST, BLOCK, 2 * DH), lambda i: (0, 0, 0))]
        * (seq_count - 1),
        compiler_params=pltpu.CompilerParams(vmem_limit_bytes=VMEM_LIMIT),
        cost_estimate=pl.CostEstimate(
            flops=0, bytes_accessed=slots * 2 * 1024 * 1024, transcendentals=0
        ),
        name="pick_blocks",
    )(places, counts, *wanted, tile)


GROUP = 3 * BLOCK
QUERIES = 256


def fold(values, combine):
    total = values[:, :DH]
    for start in range(DH, values.shape[1], DH):
        total = combine(total, values[:, start : start + DH])
    return total


def row_top(scores):
    top = jnp.max(fold(scores, jnp.maximum), axis=1, keepdims=True)
    return jnp.broadcast_to(top, (scores.shape[0], DH))


def weigh(scores, top):
    return jnp.concatenate(
        [jnp.exp2(scores[:, at : at + DH] - top) for at in range(0, scores.shape[1], DH)], axis=1
    )


def attend_kernel(seq_count, place_ref, counts_ref, q_ref, own_k_ref, own_v_ref, *refs):
    block_refs = refs[: seq_count - 1]
    out_ref, k_ref, v_ref, top_ref, sum_ref, mix_ref = refs[seq_count - 1 :]
    my_seq = place_ref[0]
    turn = pl.program_id(0)
    half = lax.rem(turn, 2)
    first = 2 * place_ref[2 + turn // 2]
    scale = math.log2(math.e) / math.sqrt(DH)

    @pl.when(turn == 0)
    def _():
        k_ref[...] = jnp.zeros_like(k_ref)
        v_ref[...] = jnp.zeros_like(v_ref)

    used = jnp.int32(0)
    for step in range(1, seq_count):
        holder = lax.rem(my_seq - step + seq_count, seq_count)
        first_count = counts_ref[(first * seq_count + my_seq) * seq_count + holder]
        second_count = counts_ref[((first + 1) * seq_count + my_seq) * seq_count + holder]
        count = jnp.where(half == 0, first_count, second_count)
        start = jnp.where(half == 0, 0, first_count)
        for entry in range(MOST):

            @pl.when(entry < count)
            def _():
                place = pl.ds(pl.multiple_of((used + entry) * BLOCK, BLOCK), BLOCK)
                slot = jnp.minimum(start + entry, PAIR_MOST - 1)
                k_ref[place, :] = block_refs[step - 1][slot, :, :DH]
                v_ref[place, :] = block_refs[step - 1][slot, :, DH:]

        used = used + count

    def score(queries, keys):
        return (
            lax.dot_general(
                queries, keys, (((1,), (1,)), ((), ())), preferred_element_type=jnp.float32
            )
            * scale
        )

    own_keys = own_k_ref[...]
    own_values = own_v_ref[...]
    for at in range(0, TILE, QUERIES):
        span = slice(at, at + QUERIES)
        scores = score(q_ref[span, :], own_keys)
        top = row_top(scores)
        weights = weigh(scores, top)
        top_ref[span, :] = top
        sum_ref[span, :] = fold(weights, jnp.add)
        mix_ref[span, :] = jnp.dot(
            weights.astype(jnp.bfloat16), own_values, preferred_element_type=jnp.float32
        )

    def visit(group, carry):
        place = pl.ds(pl.multiple_of(group * GROUP, GROUP), GROUP)
        keys = k_ref[place, :]
        values = v_ref[place, :]
        column = lax.broadcasted_iota(jnp.int32, (1, GROUP), 1) + group * GROUP
        bias = jnp.where(column < used * BLOCK, 0.0, -jnp.inf)
        for at in range(0, TILE, QUERIES):
            span = slice(at, at + QUERIES)
            scores = score(q_ref[span, :], keys) + bias
            old_top = top_ref[span, :]
            top = jnp.maximum(old_top, row_top(scores))
            weights = weigh(scores, top)
            rescale = jnp.exp2(old_top - top)
            top_ref[span, :] = top
            sum_ref[span, :] = sum_ref[span, :] * rescale + fold(weights, jnp.add)
            mix_ref[span, :] = mix_ref[span, :] * rescale + jnp.dot(
                weights.astype(jnp.bfloat16), values, preferred_element_type=jnp.float32
            )
        return carry

    lax.fori_loop(0, (used + 2) // 3, visit, 0)
    for at in range(0, TILE, QUERIES):
        span = slice(at, at + QUERIES)
        total = jnp.sum(sum_ref[span, :], axis=1, keepdims=True)
        out_ref[span, :] = (mix_ref[span, :] / total).astype(jnp.bfloat16)


def attend(places, counts, queries, query_at, tile, blocks, slots):
    seq_count = len(blocks) + 1
    most_blocks = -(-(seq_count - 1) * MOST // 3) * 3

    def head_block(index):
        return pl.BlockSpec((TILE, DH), lambda i: (0, index(i)))

    return pl.pallas_call(
        functools.partial(attend_kernel, seq_count),
        grid=(2 * slots,),
        out_shape=jax.ShapeDtypeStruct((TILE, slots * PAIR), jnp.bfloat16),
        in_specs=[smem_spec()] * 2
        + [
            head_block(lambda i: query_at + i),
            head_block(lambda i: i // 2 * 4 + i % 2),
            head_block(lambda i: i // 2 * 4 + i % 2 + 2),
        ]
        + [pl.BlockSpec((PAIR_MOST, BLOCK, 2 * DH), lambda i: (i // 2, 0, 0))] * (seq_count - 1),
        out_specs=head_block(lambda i: i),
        scratch_shapes=[
            pltpu.VMEM((most_blocks * BLOCK, DH), jnp.bfloat16),
            pltpu.VMEM((most_blocks * BLOCK, DH), jnp.bfloat16),
            pltpu.VMEM((TILE, DH), jnp.float32),
            pltpu.VMEM((TILE, DH), jnp.float32),
            pltpu.VMEM((TILE, DH), jnp.float32),
        ],
        compiler_params=pltpu.CompilerParams(vmem_limit_bytes=VMEM_LIMIT),
        cost_estimate=pl.CostEstimate(
            flops=slots * 2 * TILE * 2 * TILE * DH * 4,
            bytes_accessed=slots * 3 * 1024 * 1024,
            transcendentals=slots * 2 * TILE * 2 * TILE,
        ),
        name="attend",
    )(places, counts, queries, tile, tile, *blocks)


def lay_kernel(groups, table_ref, *refs):
    out_ref = refs[-1]
    rank = pl.program_id(0)
    local_pairs = sum(len(group) for group in groups)
    for group, ref in zip(groups, refs[:-1]):
        for at, pair in enumerate(group):
            column = table_ref[rank * local_pairs + pair] * PAIR
            out_ref[:, pl.ds(pl.multiple_of(column, PAIR), PAIR)] = ref[
                0, :, at * PAIR : (at + 1) * PAIR
            ]


def lay_out(table, stages, groups):
    head_count, rows = stages[0].shape[:2]
    return pl.pallas_call(
        functools.partial(lay_kernel, groups),
        grid=(head_count,),
        out_shape=jax.ShapeDtypeStruct((rows, HEADS * DH), jnp.bfloat16),
        in_specs=[smem_spec()]
        + [pl.BlockSpec((1, rows, len(group) * PAIR), lambda i: (i, 0, 0)) for group in groups],
        out_specs=pl.BlockSpec((rows, HEADS * DH), lambda i: (0, 0)),
        compiler_params=pltpu.CompilerParams(vmem_limit_bytes=VMEM_LIMIT),
        cost_estimate=pl.CostEstimate(
            flops=0, bytes_accessed=rows * HEADS * DH * 4, transcendentals=0
        ),
        name="lay_out",
    )(table, *stages)


def on_device(query_rows, key_rows, value_rows, block_lists, block_counts):
    head_count = lax.axis_size("head")
    seq_count = lax.axis_size("seq")
    seq_rank = lax.axis_index("seq")
    head_rank = lax.axis_index("head")
    rows = query_rows.shape[0]
    local_pairs = HEADS // 2 // head_count
    table = jnp.arange(HEADS // 2, dtype=jnp.int32)
    groups = [[0], list(range(1, local_pairs - 1)), [local_pairs - 1]]
    groups = [group for group in groups if group] if local_pairs > 1 else [[0]]

    lists = block_lists.reshape(-1)
    counts = block_counts.reshape(-1)
    wanted = [shifted(lists, "seq", (seq_count - step) % seq_count) for step in range(1, seq_count)]

    def exchanged(array):
        return lax.all_to_all(array, "head", split_axis=0, concat_axis=0, tiled=True)

    tiles = []
    for group in groups:
        parts = [(array, pair) for pair in group for array in (key_rows, value_rows)]
        query_at = 2 * len(parts)
        if group is groups[-1]:
            parts += [(query_rows, pair) for pair in range(local_pairs)]
        tile = exchanged(gather_columns(table, parts, head_count, local_pairs))
        tile = tile.reshape(TILE, len(parts) * PAIR)
        mine = lax.dynamic_slice_in_dim(table, head_rank * local_pairs + group[0], len(group))
        places = jnp.concatenate([jnp.stack([seq_rank, head_rank]).astype(jnp.int32), mine])
        picked = pick_blocks(places, counts, wanted, tile, len(group))
        blocks = [shifted(picked[step - 1], "seq", step) for step in range(1, seq_count)]
        tiles.append((places, tile, blocks))
    queries = tile

    stages = []
    for group, (places, tile, blocks) in zip(groups, tiles):
        out = attend(
            places, counts, queries, query_at + 2 * group[0], tile, blocks, len(group)
        )
        stages.append(exchanged(out.reshape(head_count, rows, len(group) * PAIR)))
    return lay_out(table, stages, groups)


def solution(mesh):
    in_specs = (
        P(("parts", "seq", "head"), None),
        P(("parts", "seq", "head"), None),
        P(("parts", "seq", "head"), None),
        P("parts", "seq", None, None),
        P("parts", None, None),
    )
    out_specs = P(("parts", "seq", "head"), None)
    return jax.shard_map(
        on_device, mesh=mesh, in_specs=in_specs, out_specs=out_specs, check_vma=False
    )
```

time: 232 us -> 210 us (0.905)
  Pallas kernels: 84.1 us -> 44 us
  blocking collectives: 0 us -> 17.3 us
  starting transfers between devices: 32.8 us -> 48.7 us
  waiting for transfers between devices: 95.5 us -> 87.5 us
  other arithmetic: 7.92 us -> 0.23 us
    ppermute x33 -> x12, waiting for transfers between devices: 95.5 us -> 53.7 us  [shifted(): lax.ppermute(array, axis, [(i, (i + step) % size) for i in range(size)])]
    pallas_call x7 -> x10, Pallas kernels: 84.1 us -> 44 us  [the longest x3 31.6 us: attend(): pl.pallas_call(functools.partial(attend_kernel, seq_count), grid=(2 * slo...]
    all_to_all x0 -> x5, waiting for transfers between devices: none -> 33.8 us  [exchanged(): lax.all_to_all(array, 'head', split_axis=0, concat_axis=0, tiled=True)]
    all_to_all x0 -> x5, starting transfers between devices: none -> 31.9 us  [exchanged(): lax.all_to_all(array, 'head', split_axis=0, concat_axis=0, tiled=True)]
    all_to_all x0 -> x1, blocking collectives: none -> 17.3 us  [exchanged(): lax.all_to_all(array, 'head', split_axis=0, concat_axis=0, tiled=True)]
    ppermute x33 -> x12, starting transfers between devices: 32.8 us -> 16.8 us  [shifted(): lax.ppermute(array, axis, [(i, (i + step) % size) for i in range(size)])]
    concatenate x17 -> x0, other arithmetic: 7.69 us -> none  [the longest x16 7.04 us: gathered(): jnp.concatenate([columns(array, rank, pair) for array, pair in parts], ax...]
    unnamed x52 -> x28, local copies, waits for them, and re-layouts: 5.98 us -> 11.6 us
  transfers between devices with their start and end apart: 33 -> 17, of which waited for: 11 -> 7; matrix products, arithmetic and copies ran while one was open for 5% -> 0% of each run, Pallas kernels for 15% -> 20%
where the time goes in v2:
time: 210 us
  waiting for transfers between devices  87.5 us (42%)
  starting transfers between devices  48.7 us (23%)
  Pallas kernels  44 us (21%)
  blocking collectives  17.3 us (8%)
  local copies, waits for them, and re-layouts  12 us (6%)
    ppermute x12, waiting for transfers between devices, shifted(): lax.ppermute(array, axis, [(i, (i + step) % size) for i in range(size)])  53.7 us
    all_to_all x5, waiting for transfers between devices, exchanged(): lax.all_to_all(array, 'head', split_axis=0, concat_axis=0, tiled=True)  33.8 us
    all_to_all x5, starting transfers between devices, exchanged(): lax.all_to_all(array, 'head', split_axis=0, concat_axis=0, tiled=True)  31.9 us
    pallas_call x3, Pallas kernels, attend(): pl.pallas_call(functools.partial(attend_kernel, seq_count), grid=(2 * slo...  31.6 us
    all_to_all x1, blocking collectives, exchanged(): lax.all_to_all(array, 'head', split_axis=0, concat_axis=0, tiled=True)  17.3 us
    ppermute x12, starting transfers between devices, shifted(): lax.ppermute(array, axis, [(i, (i + step) % size) for i in range(size)])  16.8 us
    unnamed x28, local copies, waits for them, and re-layouts  11.6 us
    pallas_call x3, Pallas kernels, pick_blocks(): pl.pallas_call(functools.partial(pick_kernel, seq_count, slots), grid=(1,...  7.14 us
  transfers between devices with their start and end apart: 17, of which 7 were waited for; matrix products, arithmetic and copies ran while one was open for 0% of the time, Pallas kernels for 20%

profile of v2, /device:TPU:13, one launch (start us, length us, event | category | flops | bytes accessed | tf_op | source)
XLA Modules:
  0.0 209.8 jit_solution(8362114604338073070)
XLA Ops:
  0.0 1.4 copy-done.1
  1.4 1.4 copy-done.4
  2.8 0.9 gather_columns.4
  3.7 0.9 copy-done.9
  4.6 5.0 %all-to-all-start.1 = ((bf16[4,192,512]{2,1,0:T(8,128)(2,1)}), bf16[4,192,512]{2,1,0:T(8,128)(2,1)}, u32[]{:S(2)}, u32[]{:S(2)}) async-start(bf16[4,192,512]{2,1,0:T(8,128)(2,1)} %copy-done.9), calls=%async_computation.1 | async-start | bytes 1572864 | tf_op jit(solution)/shard_map/all_to_all | solution.py:299
  9.6 1.4 copy-done.5
  11.0 1.3 gather_columns.3
  12.3 1.4 copy-done.7
  13.7 6.7 %all-to-all-done.1 = bf16[4,192,512]{2,1,0:T(8,128)(2,1)} async-done(((bf16[4,192,512]{2,1,0:T(8,128)(2,1)}), bf16[4,192,512]{2,1,0:T(8,128)(2,1)}, u32[]{:S(2)}, u32[]{:S(2)}) %all-to-all-start.1) | async-done | bytes 786464 | tf_op jit(solution)/shard_map/all_to_all | solution.py:299
  20.4 4.5 %all-to-all-start = ((bf16[4,192,1536]{2,1,0:T(8,128)(2,1)}), bf16[4,192,1536]{2,1,0:T(8,128)(2,1)S(1)}, u32[]{:S(2)}, u32[]{:S(2)}) async-start(bf16[4,192,1536]{2,1,0:T(8,128)(2,1)} %copy-done.7), calls=%async_computation | async-start | bytes 4718592 | tf_op jit(solution)/shard_map/all_to_all | solution.py:299
  24.9 1.4 copy-done.3
  26.3 1.4 copy-done.6
  27.7 1.1 gather_columns.5
  28.9 1.1 copy-done.8
  30.0 22.5 %all-to-all-done = bf16[4,192,1536]{2,1,0:T(8,128)(2,1)S(1)} async-done(((bf16[4,192,1536]{2,1,0:T(8,128)(2,1)}), bf16[4,192,1536]{2,1,0:T(8,128)(2,1)S(1)}, u32[]{:S(2)}, u32[]{:S(2)}) %all-to-all-start) | async-done | bytes 2359328 | tf_op jit(solution)/shard_map/all_to_all | solution.py:299
  52.6 5.2 %all-to-all-start.3 = ((bf16[4,192,1024]{2,1,0:T(8,128)(2,1)}), bf16[4,192,1024]{2,1,0:T(8,128)(2,1)}, u32[]{:S(2)}, u32[]{:S(2)}) async-start(bf16[4,192,1024]{2,1,0:T(8,128)(2,1)} %copy-done.8), calls=%async_computation.3 | async-start | bytes 3145728 | tf_op jit(solution)/shard_map/all_to_all | solution.py:299
  57.7 0.1 copy.7
  57.8 0.2 reshape.29
  58.1 0.2 collective-permute-start
  58.3 2.3 %collective-permute-start.1 = (s32[384]{0:T(512)S(1)}, s32[384]{0:T(512)S(1)}, u32[]{:S(2)}, u32[]{:S(2)}) collective-permute-start(s32[384]{0:T(512)S(1)} %reshape.29), channel_id=1, source_target_pairs={{0,8},{4,12},{8,0},{12,4},{1,9},{5,13},{9,1},{13,5},{2,10},{6,14},... | collective-permute-start | bytes 4616 | tf_op jit(solution)/shard_map/ppermute | solution.py:25
  60.6 2.2 %collective-permute-start.2 = (s32[384]{0:T(512)S(1)}, s32[384]{0:T(512)S(1)}, u32[]{:S(2)}, u32[]{:S(2)}) collective-permute-start(s32[384]{0:T(512)S(1)} %reshape.29), channel_id=1, source_target_pairs={{0,4},{4,8},{8,12},{12,0},{1,5},{5,9},{9,13},{13,1},{2,6},{6,10},{... | collective-permute-start | bytes 4616 | tf_op jit(solution)/shard_map/ppermute | solution.py:25
  62.8 0.1 pad_add_fusion.place_ref
  62.9 0.1 copy.6
  63.0 0.1 reshape.26.counts_ref
  63.1 0.4 collective-permute-done.2.refs_2_
  63.5 2.4 %pick_blocks.3 = (bf16[4,128,256]{2,1,0:T(8,128)(2,1)}, bf16[4,128,256]{2,1,0:T(8,128)(2,1)}, bf16[4,128,256]{2,1,0:T(8,128)(2,1)}) custom-call(s32[3]{0:T(128)S(1)} %pad_add_fusion.place_ref, s32[512]{0:T(512)S(1)} %reshape.26.counts_ref, s32[384]{0:T(512)S(1)} %collective-permute-done.refs_0_, s32[384]{0:T(512)S(1)} %collective-permute-done.1.refs_1_, ...), custom_call_target="tpu_custom_call" | custom-call | bytes 2097152 | tf_op jit(solution)/shard_map/pick_blocks/pallas_call | solution.py:99
  65.9 2.1 %collective-permute-start.3 = (bf16[4,128,256]{2,1,0:T(8,128)(2,1)}, bf16[4,128,256]{2,1,0:T(8,128)(2,1)S(1)}, u32[]{:S(2)}, u32[]{:S(2)}) collective-permute-start(bf16[4,128,256]{2,1,0:T(8,128)(2,1)} %get-tuple-element.14), channel_id=1, source_target_pairs={{0,4},{4,8},{8,12},{12,0},{1,5},{5,9},{9,13},{13,1},{2,6},{6,10},{... | collective-permute-start | bytes 786440 | tf_op jit(solution)/shard_map/ppermute | solution.py:25
  68.0 2.3 %collective-permute-start.4 = (bf16[4,128,256]{2,1,0:T(8,128)(2,1)}, bf16[4,128,256]{2,1,0:T(8,128)(2,1)S(1)}, u32[]{:S(2)}, u32[]{:S(2)}) collective-permute-start(bf16[4,128,256]{2,1,0:T(8,128)(2,1)} %get-tuple-element.15), channel_id=1, source_target_pairs={{0,8},{4,12},{8,0},{12,4},{1,9},{5,13},{9,1},{13,5},{2,10},{6,14},... | collective-permute-start | bytes 786440 | tf_op jit(solution)/shard_map/ppermute | solution.py:25
  70.4 1.7 pick_blocks.5
  72.1 0.2 collective-permute-start.10
  72.3 0.1 dynamic_slice.15
  72.4 0.1 pad_add_fusion.2.place_ref
  72.5 4.5 %all-to-all-done.3 = bf16[4,192,1024]{2,1,0:T(8,128)(2,1)} async-done(((bf16[4,192,1024]{2,1,0:T(8,128)(2,1)}), bf16[4,192,1024]{2,1,0:T(8,128)(2,1)}, u32[]{:S(2)}, u32[]{:S(2)}) %all-to-all-start.3) | async-done | bytes 1572896 | tf_op jit(solution)/shard_map/all_to_all | solution.py:299
  77.0 3.1 %pick_blocks.4 = (bf16[8,128,256]{2,1,0:T(8,128)(2,1)}, bf16[8,128,256]{2,1,0:T(8,128)(2,1)}, bf16[8,128,256]{2,1,0:T(8,128)(2,1)}) custom-call(s32[4]{0:T(128)S(1)} %pad_add_fusion.2.place_ref, s32[512]{0:T(512)S(1)} %reshape.26.counts_ref, s32[384]{0:T(512)S(1)} %collective-permute-done.refs_0_, s32[384]{0:T(512)S(1)} %collective-permute-done.1.refs_1_, ...), custom_call_target="tpu_custom_call" | custom-call | bytes 4194304 | tf_op jit(solution)/shard_map/pick_blocks/pallas_call | solution.py:99
  80.1 1.3 collective-permute-start.6
  81.4 1.1 collective-permute-start.7
  82.5 12.6 %collective-permute-done.4.refs_1_ = bf16[4,128,256]{2,1,0:T(8,128)(2,1)S(1)} collective-permute-done((bf16[4,128,256]{2,1,0:T(8,128)(2,1)}, bf16[4,128,256]{2,1,0:T(8,128)(2,1)S(1)}, u32[]{:S(2)}, u32[]{:S(2)}) %collective-permute-start.4) | collective-permute-done | bytes 262176 | tf_op jit(solution)/shard_map/ppermute | solution.py:25
  95.1 25.4 %collective-permute-done.5.refs_2_ = bf16[4,128,256]{2,1,0:T(8,128)(2,1)S(1)} collective-permute-done((bf16[4,128,256]{2,1,0:T(8,128)(2,1)}, bf16[4,128,256]{2,1,0:T(8,128)(2,1)S(1)}, u32[]{:S(2)}, u32[]{:S(2)}) %collective-permute-start.5) | collective-permute-done | bytes 262176 | tf_op jit(solution)/shard_map/ppermute | solution.py:25
  120.5 5.0 %collective-permute-start.9 = (bf16[4,128,256]{2,1,0:T(8,128)(2,1)}, bf16[4,128,256]{2,1,0:T(8,128)(2,1)}, u32[]{:S(2)}, u32[]{:S(2)}) collective-permute-start(bf16[4,128,256]{2,1,0:T(8,128)(2,1)} %get-tuple-element.20), channel_id=1, source_target_pairs={{0,4},{4,8},{8,12},{12,0},{1,5},{5,9},{9,13},{13,1},{2,6},{6,10},{... | collective-permute-start | bytes 786440 | tf_op jit(solution)/shard_map/ppermute | solution.py:25
  125.5 9.4 %attend.3 = bf16[768,256]{1,0:T(8,128)(2,1)} custom-call(s32[3]{0:T(128)S(1)} %pad_add_fusion.place_ref, s32[512]{0:T(512)S(1)} %reshape.26.counts_ref, bf16[768,1536]{1,0:T(8,128)(2,1)S(1)} %bitcast.13, bf16[768,512]{1,0:T(8,128)(2,1)} %bitcast.4.refs_3_.own_k_ref.own_v_ref, bf16[768,512]{1,0:T(8,128)(2,1)} %bitcast.4.refs_3_.own_k_ref.own_v_ref, ...), custom_call_target="tpu_custom_call" | custom-call | flops 1207959552 | bytes 3145728 | tf_op jit(solution)/shard_map/attend/pallas_call | solution.py:225
  134.9 9.7 %all-to-all-start.2 = ((bf16[4,192,256]{2,1,0:T(8,128)(2,1)}), bf16[4,192,256]{2,1,0:T(8,128)(2,1)S(1)}, u32[]{:S(2)}, u32[]{:S(2)}) async-start(bf16[4,192,256]{2,1,0:T(8,128)(2,1)} %bitcast.5), calls=%async_computation.2 | async-start | bytes 786432 | tf_op jit(solution)/shard_map/all_to_all | solution.py:299
  144.6 15.3 %collective-permute-done.11.refs_2_ = bf16[4,128,256]{2,1,0:T(8,128)(2,1)} collective-permute-done((bf16[4,128,256]{2,1,0:T(8,128)(2,1)}, bf16[4,128,256]{2,1,0:T(8,128)(2,1)}, u32[]{:S(2)}, u32[]{:S(2)}) %collective-permute-start.11) | collective-permute-done | bytes 262176 | tf_op jit(solution)/shard_map/ppermute | solution.py:25
  159.9 7.4 %attend.5 = bf16[768,256]{1,0:T(8,128)(2,1)} custom-call(s32[3]{0:T(128)S(1)} %pad_add_fusion.3.place_ref, s32[512]{0:T(512)S(1)} %reshape.26.counts_ref, bf16[768,1536]{1,0:T(8,128)(2,1)S(1)} %bitcast.14, bf16[768,1536]{1,0:T(8,128)(2,1)S(1)} %bitcast.15, bf16[768,1536]{1,0:T(8,128)(2,1)S(1)} %bitcast.16, ...), custom_call_target="tpu_custom_call" | custom-call | flops 1207959552 | bytes 3145728 | tf_op jit(solution)/shard_map/attend/pallas_call | solution.py:225
  167.3 7.6 %all-to-all-start.5 = ((bf16[4,192,256]{2,1,0:T(8,128)(2,1)}), bf16[4,192,256]{2,1,0:T(8,128)(2,1)S(1)}, u32[]{:S(2)}, u32[]{:S(2)}) async-start(bf16[4,192,256]{2,1,0:T(8,128)(2,1)} %bitcast.9), calls=%async_computation.5 | async-start | bytes 786432 | tf_op jit(solution)/shard_map/all_to_all | solution.py:299
  174.9 14.8 %attend.4 = bf16[768,512]{1,0:T(8,128)(2,1)S(1)} custom-call(s32[4]{0:T(128)S(1)} %pad_add_fusion.2.place_ref, s32[512]{0:T(512)S(1)} %reshape.26.counts_ref, bf16[768,1536]{1,0:T(8,128)(2,1)S(1)} %bitcast.17, bf16[768,1024]{1,0:T(8,128)(2,1)} %bitcast.6.refs_3_.own_k_ref.own_v_ref, bf16[768,1024]{1,0:T(8,128)(2,1)} %bitcast.6.refs_3_.own_k_ref.own_v_ref, ...), custom_call_target="tpu_custom_call" | custom-call | flops 2415919104 | bytes 6291456 | tf_op jit(solution)/shard_map/attend/pallas_call | solution.py:225
  189.7 0.9 copy-done.10
  190.6 17.3 %all_to_all.30.refs_1_ = bf16[4,192,512]{2,1,0:T(8,128)(2,1)S(1)} all-to-all(bf16[4,192,512]{2,1,0:T(8,128)(2,1)} %bitcast.18), channel_id=1, replica_groups=mesh['parts'=2,'seq'=4,'head'=4] {'head'}, dimensions={0} | all-to-all | bytes 1572864 | tf_op jit(solution)/shard_map/all_to_all | solution.py:299
  207.9 1.9 lay_out.1
  (36 shorter events, 0.2 us)
Async XLA Ops:
  0.0 1.4 copy-start.1
  1.4 1.4 copy-start.4
  2.8 6.7 %copy-start.2 = (bf16[192,4096]{1,0:T(8,128)(2,1)S(1)}, bf16[192,4096]{1,0:T(8,128)(2,1)}, u32[]{:S(2)}) copy-start(bf16[192,4096]{1,0:T(8,128)(2,1)} %refs_2_.3) | copy-start | bytes 4718596
  3.7 0.9 copy-start.9
  4.6 5.0 %copy-start = (bf16[192,4096]{1,0:T(8,128)(2,1)S(1)}, bf16[192,4096]{1,0:T(8,128)(2,1)}, u32[]{:S(2)}) copy-start(bf16[192,4096]{1,0:T(8,128)(2,1)} %refs_5_.1) | copy-start | bytes 4718596
  4.6 15.9 %all-to-all-start.1 = ((bf16[4,192,512]{2,1,0:T(8,128)(2,1)}), bf16[4,192,512]{2,1,0:T(8,128)(2,1)}, u32[]{:S(2)}, u32[]{:S(2)}) async-start(bf16[4,192,512]{2,1,0:T(8,128)(2,1)} %copy-done.9), calls=%async_computation.1 | async-start | bytes 1572864 | tf_op jit(solution)/shard_map/all_to_all | solution.py:299
  9.6 1.4 copy-start.5
  12.3 1.4 copy-start.7
  20.4 32.1 %all-to-all-start = ((bf16[4,192,1536]{2,1,0:T(8,128)(2,1)}), bf16[4,192,1536]{2,1,0:T(8,128)(2,1)S(1)}, u32[]{:S(2)}, u32[]{:S(2)}) async-start(bf16[4,192,1536]{2,1,0:T(8,128)(2,1)} %copy-done.7), calls=%async_computation | async-start | bytes 4718592 | tf_op jit(solution)/shard_map/all_to_all | solution.py:299
  24.9 1.4 copy-start.3
  26.3 1.4 copy-start.6
  28.9 1.1 copy-start.8
  30.0 27.7 %copy-start.12 = (s32[32,1,4,3]{0,2,3,1:T(4,128)S(1)}, s32[32,1,4,3]{0,2,3,1:T(4,128)}, u32[]{:S(2)}) copy-start(s32[32,1,4,3]{0,2,3,1:T(4,128)} %param.8) | copy-start | bytes 4612
  30.0 32.8 %copy-start.11 = (s32[32,4,4]{0,2,1:T(4,128)S(1)}, s32[32,4,4]{0,2,1:T(4,128)}, u32[]{:S(2)}) copy-start(s32[32,4,4]{0,2,1:T(4,128)} %param.9) | copy-start | bytes 6148
  52.6 24.5 %all-to-all-start.3 = ((bf16[4,192,1024]{2,1,0:T(8,128)(2,1)}), bf16[4,192,1024]{2,1,0:T(8,128)(2,1)}, u32[]{:S(2)}, u32[]{:S(2)}) async-start(bf16[4,192,1024]{2,1,0:T(8,128)(2,1)} %copy-done.8), calls=%async_computation.3 | async-start | bytes 3145728 | tf_op jit(solution)/shard_map/all_to_all | solution.py:299
  58.1 5.0 %collective-permute-start = (s32[384]{0:T(512)S(1)}, s32[384]{0:T(512)S(1)}, u32[]{:S(2)}, u32[]{:S(2)}) collective-permute-start(s32[384]{0:T(512)S(1)} %reshape.29), channel_id=1, source_target_pairs={{0,12},{4,0},{8,4},{12,8},{1,13},{5,1},{9,5},{13,9},{2,14},{6,2},{... | collective-permute-start | bytes 4616 | tf_op jit(solution)/shard_map/ppermute | solution.py:25
  58.3 4.8 %collective-permute-start.1 = (s32[384]{0:T(512)S(1)}, s32[384]{0:T(512)S(1)}, u32[]{:S(2)}, u32[]{:S(2)}) collective-permute-start(s32[384]{0:T(512)S(1)} %reshape.29), channel_id=1, source_target_pairs={{0,8},{4,12},{8,0},{12,4},{1,9},{5,13},{9,1},{13,5},{2,10},{6,14},... | collective-permute-start | bytes 4616 | tf_op jit(solution)/shard_map/ppermute | solution.py:25
  60.6 2.9 %collective-permute-start.2 = (s32[384]{0:T(512)S(1)}, s32[384]{0:T(512)S(1)}, u32[]{:S(2)}, u32[]{:S(2)}) collective-permute-start(s32[384]{0:T(512)S(1)} %reshape.29), channel_id=1, source_target_pairs={{0,4},{4,8},{8,12},{12,0},{1,5},{5,9},{9,13},{13,1},{2,6},{6,10},{... | collective-permute-start | bytes 4616 | tf_op jit(solution)/shard_map/ppermute | solution.py:25
  65.9 15.5 %collective-permute-start.3 = (bf16[4,128,256]{2,1,0:T(8,128)(2,1)}, bf16[4,128,256]{2,1,0:T(8,128)(2,1)S(1)}, u32[]{:S(2)}, u32[]{:S(2)}) collective-permute-start(bf16[4,128,256]{2,1,0:T(8,128)(2,1)} %get-tuple-element.14), channel_id=1, source_target_pairs={{0,4},{4,8},{8,12},{12,0},{1,5},{5,9},{9,13},{13,1},{2,6},{6,10},{... | collective-permute-start | bytes 786440 | tf_op jit(solution)/shard_map/ppermute | solution.py:25
  68.0 27.1 %collective-permute-start.4 = (bf16[4,128,256]{2,1,0:T(8,128)(2,1)}, bf16[4,128,256]{2,1,0:T(8,128)(2,1)S(1)}, u32[]{:S(2)}, u32[]{:S(2)}) collective-permute-start(bf16[4,128,256]{2,1,0:T(8,128)(2,1)} %get-tuple-element.15), channel_id=1, source_target_pairs={{0,8},{4,12},{8,0},{12,4},{1,9},{5,13},{9,1},{13,5},{2,10},{6,14},... | collective-permute-start | bytes 786440 | tf_op jit(solution)/shard_map/ppermute | solution.py:25
  70.4 50.1 %collective-permute-start.5 = (bf16[4,128,256]{2,1,0:T(8,128)(2,1)}, bf16[4,128,256]{2,1,0:T(8,128)(2,1)S(1)}, u32[]{:S(2)}, u32[]{:S(2)}) collective-permute-start(bf16[4,128,256]{2,1,0:T(8,128)(2,1)} %get-tuple-element.16), channel_id=1, source_target_pairs={{0,12},{4,0},{8,4},{12,8},{1,13},{5,1},{9,5},{13,9},{2,14},{6,2},{... | collective-permute-start | bytes 786440 | tf_op jit(solution)/shard_map/ppermute | solution.py:25
  72.1 48.4 %collective-permute-start.10 = (bf16[4,128,256]{2,1,0:T(8,128)(2,1)}, bf16[4,128,256]{2,1,0:T(8,128)(2,1)S(1)}, u32[]{:S(2)}, u32[]{:S(2)}) collective-permute-start(bf16[4,128,256]{2,1,0:T(8,128)(2,1)} %get-tuple-element.21), channel_id=1, source_target_pairs={{0,8},{4,12},{8,0},{12,4},{1,9},{5,13},{9,1},{13,5},{2,10},{6,14},... | collective-permute-start | bytes 786440 | tf_op jit(solution)/shard_map/ppermute | solution.py:25
  80.1 94.8 %collective-permute-start.6 = (bf16[8,128,256]{2,1,0:T(8,128)(2,1)}, bf16[8,128,256]{2,1,0:T(8,128)(2,1)}, u32[]{:S(2)}, u32[]{:S(2)}) collective-permute-start(bf16[8,128,256]{2,1,0:T(8,128)(2,1)} %get-tuple-element.17), channel_id=1, source_target_pairs={{0,4},{4,8},{8,12},{12,0},{1,5},{5,9},{9,13},{13,1},{2,6},{6,10},{... | collective-permute-start | bytes 1572872 | tf_op jit(solution)/shard_map/ppermute | solution.py:25
  81.4 93.5 %collective-permute-start.7 = (bf16[8,128,256]{2,1,0:T(8,128)(2,1)}, bf16[8,128,256]{2,1,0:T(8,128)(2,1)}, u32[]{:S(2)}, u32[]{:S(2)}) collective-permute-start(bf16[8,128,256]{2,1,0:T(8,128)(2,1)} %get-tuple-element.18), channel_id=1, source_target_pairs={{0,8},{4,12},{8,0},{12,4},{1,9},{5,13},{9,1},{13,5},{2,10},{6,14},... | collective-permute-start | bytes 1572872 | tf_op jit(solution)/shard_map/ppermute | solution.py:25
  95.1 79.8 %collective-permute-start.8 = (bf16[8,128,256]{2,1,0:T(8,128)(2,1)}, bf16[8,128,256]{2,1,0:T(8,128)(2,1)}, u32[]{:S(2)}, u32[]{:S(2)}) collective-permute-start(bf16[8,128,256]{2,1,0:T(8,128)(2,1)} %get-tuple-element.19), channel_id=1, source_target_pairs={{0,12},{4,0},{8,4},{12,8},{1,13},{5,1},{9,5},{13,9},{2,14},{6,2},{... | collective-permute-start | bytes 1572872 | tf_op jit(solution)/shard_map/ppermute | solution.py:25
  120.5 39.5 %collective-permute-start.11 = (bf16[4,128,256]{2,1,0:T(8,128)(2,1)}, bf16[4,128,256]{2,1,0:T(8,128)(2,1)}, u32[]{:S(2)}, u32[]{:S(2)}) collective-permute-start(bf16[4,128,256]{2,1,0:T(8,128)(2,1)} %get-tuple-element.22), channel_id=1, source_target_pairs={{0,12},{4,0},{8,4},{12,8},{1,13},{5,1},{9,5},{13,9},{2,14},{6,2},{... | collective-permute-start | bytes 786440 | tf_op jit(solution)/shard_map/ppermute | solution.py:25
  120.5 39.5 %collective-permute-start.9 = (bf16[4,128,256]{2,1,0:T(8,128)(2,1)}, bf16[4,128,256]{2,1,0:T(8,128)(2,1)}, u32[]{:S(2)}, u32[]{:S(2)}) collective-permute-start(bf16[4,128,256]{2,1,0:T(8,128)(2,1)} %get-tuple-element.20), channel_id=1, source_target_pairs={{0,4},{4,8},{8,12},{12,0},{1,5},{5,9},{9,13},{13,1},{2,6},{6,10},{... | collective-permute-start | bytes 786440 | tf_op jit(solution)/shard_map/ppermute | solution.py:25
  134.9 32.4 %all-to-all-start.2 = ((bf16[4,192,256]{2,1,0:T(8,128)(2,1)}), bf16[4,192,256]{2,1,0:T(8,128)(2,1)S(1)}, u32[]{:S(2)}, u32[]{:S(2)}) async-start(bf16[4,192,256]{2,1,0:T(8,128)(2,1)} %bitcast.5), calls=%async_computation.2 | async-start | bytes 786432 | tf_op jit(solution)/shard_map/all_to_all | solution.py:299
  167.3 23.3 %all-to-all-start.5 = ((bf16[4,192,256]{2,1,0:T(8,128)(2,1)}), bf16[4,192,256]{2,1,0:T(8,128)(2,1)S(1)}, u32[]{:S(2)}, u32[]{:S(2)}) async-start(bf16[4,192,256]{2,1,0:T(8,128)(2,1)} %bitcast.9), calls=%async_computation.5 | async-start | bytes 786432 | tf_op jit(solution)/shard_map/all_to_all | solution.py:299
  189.7 0.9 copy-start.10

commit v3 on v1

v3 whole, which is shorter than its diff:
```python
import functools
import math

import jax
import jax.numpy as jnp
from jax import lax
from jax.experimental import pallas as pl
from jax.experimental.pallas import tpu as pltpu
from jax.sharding import PartitionSpec as P

HEADS = 32
DH = 128
BLOCK = 128
MOST = 3
PAIR_MOST = 4
TILE = 768
PAIR = 2 * DH
LIGHT_MOST = 1
VMEM_LIMIT = 60 * 1024 * 1024
SMEM = pltpu.SMEM
BRIEF = pl.CostEstimate(flops=1024, bytes_accessed=1024, transcendentals=0)


def shifted(array, axis, step):
    size = lax.axis_size(axis)
    return lax.ppermute(array, axis, [(i, (i + step) % size) for i in range(size)])


def smem_spec():
    return pl.BlockSpec(memory_space=SMEM)


def one_block(shape):
    return pl.BlockSpec(shape, lambda i, *_: (0,) * len(shape))


def gather_kernel(head_count, place_ref, *refs):
    part_count = len(refs) // head_count - 1
    for step in range(head_count):
        for at in range(part_count):
            refs[head_count * part_count + step][:, at * PAIR : (at + 1) * PAIR] = refs[
                step * part_count + at
            ][...]


def gather_columns(places, parts, head_count, local_pairs):
    rows = parts[0][0].shape[0]

    def column_of(step, pair):
        def index(i, place_ref):
            rank = lax.rem(place_ref[1] + step, head_count)
            return 0, place_ref[2 + rank * local_pairs + pair]

        return index

    return pl.pallas_call(
        functools.partial(gather_kernel, head_count),
        grid_spec=pltpu.PrefetchScalarGridSpec(
            num_scalar_prefetch=1,
            grid=(1,),
            in_specs=[
                pl.BlockSpec((rows, PAIR), column_of(step, pair))
                for step in range(head_count)
                for _, pair in parts
            ],
            out_specs=[one_block((rows, len(parts) * PAIR))] * head_count,
        ),
        out_shape=[jax.ShapeDtypeStruct((rows, len(parts) * PAIR), jnp.bfloat16)] * head_count,
        compiler_params=pltpu.CompilerParams(vmem_limit_bytes=VMEM_LIMIT),
        cost_estimate=BRIEF,
        name="gather_columns",
    )(places, *[array for array, _ in parts] * head_count)


def pick_kernel(head_count, seq_count, first_pair, caps, place_ref, counts_ref, *refs):
    want_refs = refs[: seq_count - 1]
    rows_refs = refs[seq_count - 1 : seq_count - 1 + head_count]
    tile_ref = refs[seq_count - 1 + head_count]
    send_refs = refs[seq_count + head_count :]
    my_seq, my_head = place_ref[0], place_ref[1]
    rows = TILE // head_count
    pair_at = 2 + my_head * (HEADS // 2 // head_count) + first_pair
    for step in range(head_count):
        rank = lax.rem(my_head - step + head_count, head_count)
        place = pl.ds(pl.multiple_of(rank * rows, 16), rows)
        for pair in range(len(caps)):
            for half in range(2):
                base = pair * 2 * PAIR + half * DH
                tile_ref[2 * pair + half, place, :DH] = rows_refs[step][:, base : base + DH]
                tile_ref[2 * pair + half, place, DH:] = rows_refs[step][
                    :, base + PAIR : base + PAIR + DH
                ]
    for step in range(1, seq_count):
        asker = lax.rem(my_seq + step, seq_count)
        for pair, cap in enumerate(caps):
            first = 2 * place_ref[pair_at + pair]
            first_count = counts_ref[(first * seq_count + asker) * seq_count + my_seq]
            both = first_count + counts_ref[((first + 1) * seq_count + asker) * seq_count + my_seq]
            for slot in range(cap):

                @pl.when(slot < both)
                def _():
                    half = jnp.where(slot < first_count, 0, 1)
                    entry = jnp.where(slot < first_count, slot, slot - first_count)
                    entry = jnp.clip(entry, 0, MOST - 1)
                    block = want_refs[step - 1][
                        ((first + half) * seq_count + my_seq) * MOST + entry
                    ]
                    send_refs[step - 1][pair * PAIR_MOST + slot] = tile_ref[
                        2 * pair + half, pl.ds(pl.multiple_of(block * BLOCK, BLOCK), BLOCK), :
                    ]


def pick_blocks(places, counts, wanted, pieces, first_pair, caps):
    slots = len(caps)
    head_count, seq_count = len(pieces), len(wanted) + 1
    out_shape = [jax.ShapeDtypeStruct((2 * slots, TILE, 2 * DH), jnp.bfloat16)]
    out_shape += [
        jax.ShapeDtypeStruct((sum(caps), BLOCK, 2 * DH), jnp.bfloat16)
    ] * (seq_count - 1)
    outs = pl.pallas_call(
        functools.partial(pick_kernel, head_count, seq_count, first_pair, caps),
        out_shape=out_shape,
        grid=(1,),
        in_specs=[smem_spec()] * (seq_count + 1) + [one_block((pieces[0].shape[0], slots * 2 * PAIR))]
        * head_count,
        out_specs=[one_block(shape.shape) for shape in out_shape],
        compiler_params=pltpu.CompilerParams(vmem_limit_bytes=VMEM_LIMIT),
        cost_estimate=BRIEF,
        name="pick_blocks",
    )(places, counts, *wanted, *pieces)
    return outs[0], outs[1:]


GROUP = 3 * BLOCK


def fold(values, combine):
    total = values[:, :DH]
    for start in range(DH, values.shape[1], DH):
        total = combine(total, values[:, start : start + DH])
    return total


def row_top(scores):
    top = jnp.max(fold(scores, jnp.maximum), axis=1, keepdims=True)
    return jnp.broadcast_to(top, (scores.shape[0], DH))


def weigh(scores, top):
    return jnp.concatenate(
        [jnp.exp2(scores[:, at : at + DH] - top) for at in range(0, scores.shape[1], DH)], axis=1
    )


def start_state(queries, keys, values, scale):
    scores = score(queries, keys, scale)
    top = row_top(scores)
    weights = weigh(scores, top)
    mixture = jnp.dot(weights.astype(jnp.bfloat16), values, preferred_element_type=jnp.float32)
    return top, fold(weights, jnp.add), mixture


def score(queries, keys, scale):
    products = lax.dot_general(
        queries, keys, (((1,), (1,)), ((), ())), preferred_element_type=jnp.float32
    )
    return products * scale


SCALE = math.log2(math.e) / math.sqrt(DH)


def fetch_blocks(place_ref, counts_ref, block_refs, k_ref, v_ref, head_count, first_pair):
    seq_count = len(block_refs) + 1
    my_seq = place_ref[0]
    turn = pl.program_id(0)
    half = lax.rem(turn, 2)
    pair_at = 2 + place_ref[1] * (HEADS // 2 // head_count) + first_pair
    first = 2 * place_ref[pair_at + turn // 2]
    slot_most = block_refs[0].shape[0] - 1
    used = jnp.int32(0)
    for step in range(1, seq_count):
        holder = lax.rem(my_seq - step + seq_count, seq_count)
        first_count = counts_ref[(first * seq_count + my_seq) * seq_count + holder]
        second_count = counts_ref[((first + 1) * seq_count + my_seq) * seq_count + holder]
        count = jnp.where(half == 0, first_count, second_count)
        start = jnp.where(half == 0, 0, first_count) + turn // 2 * PAIR_MOST
        for entry in range(MOST):

            @pl.when(entry < count)
            def _():
                place = pl.ds(pl.multiple_of((used + entry) * BLOCK, BLOCK), BLOCK)
                slot = jnp.minimum(start + entry, slot_most)
                k_ref[place, :] = block_refs[step - 1][slot, :, :DH]
                v_ref[place, :] = block_refs[step - 1][slot, :, DH:]

        used = used + count
    return used


def visit_blocks(used, q_ref, k_ref, v_ref, top_ref, sum_ref, mix_ref):
    def visit(group, carry):
        place = pl.ds(pl.multiple_of(group * GROUP, GROUP), GROUP)
        column = lax.broadcasted_iota(jnp.int32, (1, GROUP), 1) + group * GROUP
        bias = jnp.where(column < used * BLOCK, 0.0, -jnp.inf)
        scores = score(q_ref[...], k_ref[place, :], SCALE) + bias
        old_top = top_ref[...]
        top = jnp.maximum(old_top, row_top(scores))
        weights = weigh(scores, top)
        rescale = jnp.exp2(old_top - top)
        top_ref[...] = top
        sum_ref[...] = sum_ref[...] * rescale + fold(weights, jnp.add)
        mix_ref[...] = mix_ref[...] * rescale + jnp.dot(
            weights.astype(jnp.bfloat16), v_ref[place, :], preferred_element_type=jnp.float32
        )
        return carry

    lax.fori_loop(0, (used + 2) // 3, visit, 0)


def clear_blocks(k_ref, v_ref):
    @pl.when(pl.program_id(0) == 0)
    def _():
        k_ref[...] = jnp.zeros_like(k_ref)
        v_ref[...] = jnp.zeros_like(v_ref)


def join_pieces(query_refs, q_ref):
    rows = TILE // len(query_refs)
    for step, ref in enumerate(query_refs):
        q_ref[step * rows : (step + 1) * rows, :] = ref[...]


def split_result(out_refs, sum_ref, mix_ref):
    rows = TILE // len(out_refs)
    for step, ref in enumerate(out_refs):
        span = slice(step * rows, (step + 1) * rows)
        total = jnp.sum(sum_ref[span, :], axis=1, keepdims=True)
        ref[...] = (mix_ref[span, :] / total).astype(jnp.bfloat16)


def attend_kernel(head_count, seq_count, first_pair, place_ref, counts_ref, tile_ref, *refs):
    query_refs, refs = refs[:head_count], refs[head_count:]
    block_refs, refs = refs[: seq_count - 1], refs[seq_count - 1 :]
    out_refs, refs = refs[:head_count], refs[head_count:]
    q_ref, k_ref, v_ref, top_ref, sum_ref, mix_ref = refs
    clear_blocks(k_ref, v_ref)
    join_pieces(query_refs, q_ref)
    used = fetch_blocks(place_ref, counts_ref, block_refs, k_ref, v_ref, head_count, first_pair)
    top_ref[...], sum_ref[...], mix_ref[...] = start_state(
        q_ref[...], tile_ref[0, :, :DH], tile_ref[0, :, DH:], SCALE
    )
    visit_blocks(used, q_ref, k_ref, v_ref, top_ref, sum_ref, mix_ref)
    split_result(out_refs, sum_ref, mix_ref)


def own_kernel(head_count, tile_ref, *refs):
    query_refs, (top_ref, sum_ref, mix_ref, q_ref) = refs[:head_count], refs[head_count:]
    join_pieces(query_refs, q_ref)
    top_ref[0], sum_ref[0], mix_ref[0] = start_state(
        q_ref[...], tile_ref[0, :, :DH], tile_ref[0, :, DH:], SCALE
    )


def far_kernel(head_count, seq_count, first_pair, place_ref, counts_ref, *refs):
    old_top_ref, old_sum_ref, old_mix_ref = refs[:3]
    query_refs, refs = refs[3 : 3 + head_count], refs[3 + head_count :]
    block_refs, refs = refs[: seq_count - 1], refs[seq_count - 1 :]
    out_refs, refs = refs[:head_count], refs[head_count:]
    q_ref, k_ref, v_ref, top_ref, sum_ref, mix_ref = refs
    clear_blocks(k_ref, v_ref)
    join_pieces(query_refs, q_ref)
    used = fetch_blocks(place_ref, counts_ref, block_refs, k_ref, v_ref, head_count, first_pair)
    top_ref[...], sum_ref[...], mix_ref[...] = old_top_ref[0], old_sum_ref[0], old_mix_ref[0]
    visit_blocks(used, q_ref, k_ref, v_ref, top_ref, sum_ref, mix_ref)
    split_result(out_refs, sum_ref, mix_ref)


def state_spec():
    return pl.BlockSpec((1, TILE, DH), lambda i: (i, 0, 0))


def tile_spec():
    return pl.BlockSpec((1, TILE, 2 * DH), lambda i: (i, 0, 0))


def query_specs(queries, query_at):
    return [pl.BlockSpec((piece.shape[0], DH), lambda i: (0, query_at + i)) for piece in queries]


def attention_call(kernel, name, slots, seq_count, operands, in_specs, head_count):
    most_blocks = -(-(seq_count - 1) * MOST // 3) * 3
    rows = TILE // head_count
    return pl.pallas_call(
        kernel,
        grid=(2 * slots,),
        out_shape=[jax.ShapeDtypeStruct((rows, slots * PAIR), jnp.bfloat16)] * head_count,
        in_specs=in_specs,
        out_specs=[pl.BlockSpec((rows, DH), lambda i: (0, i))] * head_count,
        scratch_shapes=[
            pltpu.VMEM((TILE, DH), jnp.bfloat16),
            pltpu.VMEM((most_blocks * BLOCK, DH), jnp.bfloat16),
            pltpu.VMEM((most_blocks * BLOCK, DH), jnp.bfloat16),
            pltpu.VMEM((TILE, DH), jnp.float32),
            pltpu.VMEM((TILE, DH), jnp.float32),
            pltpu.VMEM((TILE, DH), jnp.float32),
        ],
        compiler_params=pltpu.CompilerParams(vmem_limit_bytes=VMEM_LIMIT),
        cost_estimate=BRIEF,
        name=name,
    )(*operands)


def attend(places, counts, tile_pairs, queries, query_at, blocks, first_pair, slots):
    head_count, seq_count = len(queries), len(blocks) + 1
    return attention_call(
        functools.partial(attend_kernel, head_count, seq_count, first_pair),
        "attend",
        slots,
        seq_count,
        (places, counts, tile_pairs, *queries, *blocks),
        [smem_spec()] * 2
        + [tile_spec()]
        + query_specs(queries, query_at)
        + [one_block(block.shape) for block in blocks],
        head_count,
    )


def attend_own(tile_pairs, queries, query_at, slots):
    head_count = len(queries)
    return pl.pallas_call(
        functools.partial(own_kernel, head_count),
        grid=(2 * slots,),
        out_shape=[jax.ShapeDtypeStruct((2 * slots, TILE, DH), jnp.float32)] * 3,
        in_specs=[tile_spec()] + query_specs(queries, query_at),
        out_specs=[state_spec()] * 3,
        scratch_shapes=[pltpu.VMEM((TILE, DH), jnp.bfloat16)],
        compiler_params=pltpu.CompilerParams(vmem_limit_bytes=VMEM_LIMIT),
        cost_estimate=BRIEF,
        name="attend_own",
    )(tile_pairs, *queries)


def attend_far(places, counts, state, queries, query_at, blocks, first_pair, slots):
    head_count, seq_count = len(queries), len(blocks) + 1
    return attention_call(
        functools.partial(far_kernel, head_count, seq_count, first_pair),
        "attend_far",
        slots,
        seq_count,
        (places, counts, *state, *queries, *blocks),
        [smem_spec()] * 2
        + [state_spec()] * 3
        + query_specs(queries, query_at)
        + [one_block(block.shape) for block in blocks],
        head_count,
    )


def lay_kernel(groups, head_count, place_ref, *refs):
    out_ref = refs[-1]
    local_pairs = HEADS // 2 // head_count
    for number, group in enumerate(groups):
        for step in range(head_count):
            rank = lax.rem(place_ref[1] - step + head_count, head_count)
            for at, pair in enumerate(group):
                column = place_ref[2 + rank * local_pairs + pair] * PAIR
                out_ref[:, pl.ds(pl.multiple_of(column, PAIR), PAIR)] = refs[
                    number * head_count + step
                ][:, at * PAIR : (at + 1) * PAIR]


def lay_out(places, stages, groups):
    head_count = len(stages[0])
    rows = stages[0][0].shape[0]
    flat = [piece for stage in stages for piece in stage]
    return pl.pallas_call(
        functools.partial(lay_kernel, groups, head_count),
        grid=(1,),
        out_shape=jax.ShapeDtypeStruct((rows, HEADS * DH), jnp.bfloat16),
        in_specs=[smem_spec()] + [one_block(piece.shape) for piece in flat],
        out_specs=one_block((rows, HEADS * DH)),
        compiler_params=pltpu.CompilerParams(vmem_limit_bytes=VMEM_LIMIT),
        cost_estimate=BRIEF,
        name="lay_out",
    )(places, *flat)


def after(value, *others):
    return lax.optimization_barrier((value, others))[0]


def place_pairs(block_counts, head_count, local_pairs):
    pair_count = HEADS // 2
    listed = jnp.sum(block_counts.reshape(pair_count, 2, *block_counts.shape[1:]), axis=1)
    total = jnp.sum(listed, axis=(1, 2))
    most = jnp.max(listed, axis=(1, 2))
    pairs = jnp.arange(pair_count, dtype=jnp.int32)
    ahead = (total[None, :] > total[:, None]) | (
        (total[None, :] == total[:, None]) & (pairs[None, :] < pairs[:, None])
    )
    order = jnp.sum(ahead.astype(jnp.int32), axis=1)
    place = order % head_count * local_pairs + order // head_count
    hit = place[None, :] == pairs[:, None]
    table = jnp.sum(jnp.where(hit, pairs[None, :], 0), axis=1)
    return table, jnp.where(order >= 3 * head_count, most, 0)


def on_device(query_rows, key_rows, value_rows, block_lists, block_counts):
    head_count = lax.axis_size("head")
    seq_count = lax.axis_size("seq")
    part_count = lax.axis_size("parts")
    local_pairs = HEADS // 2 // head_count
    ranks = jnp.stack([lax.axis_index("seq"), lax.axis_index("head")]).astype(jnp.int32)
    table, light_most = place_pairs(block_counts, head_count, local_pairs)
    places = jnp.concatenate([ranks, table])
    groups = [[0], list(range(2, local_pairs)), [1]]
    groups = [group for group in groups if group and group[-1] < local_pairs]

    sources, query_from = [], {}
    for number, group in enumerate(groups):
        parts = [(array, pair) for pair in group for array in (key_rows, value_rows)]
        if len(groups) == 1 or number == 1:
            asked = [0]
        elif number == 0:
            asked = []
        else:
            asked = [1, 2]
        for other in asked:
            query_from[other] = (number, len(parts) * 2)
            parts += [(query_rows, pair) for pair in groups[other]]
        sources.append(gather_columns(places, parts, head_count, local_pairs))

    def spread(source):
        return [source[0]] + [shifted(source[step], "head", step) for step in range(1, head_count)]

    def returned(outs):
        return [outs[0]] + [
            shifted(outs[head_count - step], "head", step) for step in range(1, head_count)
        ]

    def passed_on(picked):
        return [shifted(picked[step - 1], "seq", step) for step in range(1, seq_count)]

    pieces = [spread(sources[0])]
    lists, counts = after((block_lists, block_counts), sources[0])
    lists, counts = lists.reshape(-1), counts.reshape(-1)
    wanted = [shifted(lists, "seq", (seq_count - step) % seq_count) for step in range(1, seq_count)]

    def pick(number, arrived, light):
        caps = [light if pair >= 3 else PAIR_MOST for pair in groups[number]]
        return pick_blocks(places, counts, wanted, arrived, groups[number][0], caps)

    def whole(number, tile_pairs, blocks):
        source, at = query_from[number]
        group = groups[number]
        return attend(
            places, counts, tile_pairs, pieces[source], at, blocks, group[0], len(group)
        )

    if len(groups) == 1:
        tile_pairs, picked = pick(0, pieces[0], PAIR_MOST)
        return lay_out(places, [returned(whole(0, tile_pairs, passed_on(picked)))], groups)

    pieces.append(spread(after(sources[1], pieces[0], wanted, counts)))
    tile_pairs, picked = pick(0, pieces[0], PAIR_MOST)
    blocks = passed_on(picked)
    light_most = after(jnp.max(after(light_most, sources[0])), pieces[1][1])
    for step in range(1, part_count):
        light_most = jnp.maximum(light_most, shifted(light_most[None], "parts", step)[0])
    first = (tile_pairs, blocks)
    light_most, first, arrived, third = lax.optimization_barrier(
        (light_most, first, pieces[1], sources[2])
    )

    def finish(light, first, arrived, third):
        pieces[1] = arrived
        tile_pairs, picked = pick(1, arrived, light)
        pieces[2:] = [spread(after(third, picked))]
        second = (tile_pairs, passed_on(picked))
        outs = whole(0, *after(first, picked))
        arrived = after(pieces[2], outs, second[1])
        tile_pairs, picked = pick(2, arrived, light)
        results = [returned(outs)]
        blocks = passed_on(picked)
        results.append(returned(whole(1, *after(second, picked))))
        source, at = query_from[2]
        state = attend_own(tile_pairs, pieces[source], at, 1)
        state = after(state, results[0], results[1][0])
        outs = attend_far(places, counts, state, pieces[source], at, blocks, groups[2][0], 1)
        results.append(returned(outs))
        return lay_out(places, results, groups)

    if max(max(group) for group in groups) < 3:
        return finish(PAIR_MOST, first, arrived, third)
    return lax.cond(
        light_most > LIGHT_MOST,
        functools.partial(finish, PAIR_MOST),
        functools.partial(finish, LIGHT_MOST),
        first,
        arrived,
        third,
    )


def solution(mesh):
    in_specs = (
        P(("parts", "seq", "head"), None),
        P(("parts", "seq", "head"), None),
        P(("parts", "seq", "head"), None),
        P("parts", "seq", None, None),
        P("parts", None, None),
    )
    out_specs = P(("parts", "seq", "head"), None)
    return jax.shard_map(
        on_device, mesh=mesh, in_specs=in_specs, out_specs=out_specs, check_vma=False
    )
```

time: 232 us -> 134 us (0.58)
  waiting for transfers between devices: 95.5 us -> 38.8 us
  Pallas kernels: 84.1 us -> 49.6 us
  other arithmetic: 7.92 us -> 2.04 us
  local copies, waits for them, and re-layouts: 10.3 us -> 5.7 us
    ppermute x33 -> x31, waiting for transfers between devices: 95.5 us -> 38.8 us  [shifted(): lax.ppermute(array, axis, [(i, (i + step) % size) for i in range(size)])]
    pallas_call x7 -> x11, Pallas kernels: 84.1 us -> 49.6 us  [the longest x3 25.8 us: attention_call(): pl.pallas_call(kernel, grid=(2 * slots,), out_shape=[jax.ShapeDtypeStruct...]
    concatenate x20 -> x1, other arithmetic: 7.92 us -> 0.08 us  [on_device(): places = jnp.concatenate([ranks, table])]
    unnamed x52 -> x13, local copies, waits for them, and re-layouts: 5.98 us -> 1.95 us
    dynamic_slice x3 -> x0, local copies, waits for them, and re-layouts: 4.01 us -> none  [the longest x2 3.93 us: columns(): return lax.dynamic_slice(array, (0, at), (rows, PAIR))]
    cond x0 -> x42, local copies, waits for them, and re-layouts: none -> 3.1 us
    ppermute x33 -> x31, starting transfers between devices: 32.8 us -> 34.2 us  [shifted(): lax.ppermute(array, axis, [(i, (i + step) % size) for i in range(size)])]
  transfers between devices with their start and end apart: 33 -> 31, of which waited for: 11 -> 12; matrix products, arithmetic and copies ran while one was open for 5% -> 1% of each run, Pallas kernels for 15% -> 30%
where the time goes in v3:
time: 134 us; the launch traced here: 132 us
  Pallas kernels  49.6 us (37%)
  waiting for transfers between devices  38.8 us (29%)
  starting transfers between devices  34.2 us (26%)
  local copies, waits for them, and re-layouts  5.7 us (4%)
  other arithmetic  2.04 us (2%)
    ppermute x31, waiting for transfers between devices, shifted(): lax.ppermute(array, axis, [(i, (i + step) % size) for i in range(size)])  38.8 us
    ppermute x31, starting transfers between devices, shifted(): lax.ppermute(array, axis, [(i, (i + step) % size) for i in range(size)])  34.2 us
    pallas_call x3, Pallas kernels, attention_call(): pl.pallas_call(kernel, grid=(2 * slots,), out_shape=[jax.ShapeDtypeStruct...  25.8 us
    pallas_call x3, Pallas kernels, gather_columns(): pl.pallas_call(functools.partial(gather_kernel, head_count), grid_spec=pl...  9.29 us
    pallas_call x3, Pallas kernels, pick_blocks(): pl.pallas_call(functools.partial(pick_kernel, head_count, seq_count, firs...  8.08 us
    pallas_call x1, Pallas kernels, attend_own(): pl.pallas_call(functools.partial(own_kernel, head_count), grid=(2 * slots...  4.8 us
    cond x42, local copies, waits for them, and re-layouts  3.1 us
  transfers between devices with their start and end apart: 31, of which 12 were waited for; matrix products, arithmetic and copies ran while one was open for 1% of the time, Pallas kernels for 30%

profile of v3, /device:TPU:13, one launch (start us, length us, event | category | flops | bytes accessed | tf_op | source)
XLA Modules:
  0.0 132.0 jit_solution(3856973867864957043)
XLA Ops:
  0.0 0.8 copy.14
  0.8 0.7 reduce_sum.43
  2.3 2.7 %gather_columns.3 = (bf16[192,512]{1,0:T(8,128)(2,1)}, bf16[192,512]{1,0:T(8,128)(2,1)}, bf16[192,512]{1,0:T(8,128)(2,1)}, bf16[192,512]{1,0:T(8,128)(2,1)}) custom-call(s32[18]{0:T(128)S(1)} %pad_add_fusion.place_ref, bf16[192,4096]{1,0:T(8,128)(2,1)} %refs_15_.3, bf16[192,4096]{1,0:T(8,128)(2,1)} %refs_16_.3, bf16[192,4096]{1,0:T(8,128)(2,1)} %refs_15_.3, ...), custom_call_target="tpu_custom_call" | custom-call | flops 1024 | bytes 1024 | tf_op jit(solution)/shard_map/gather_columns/pallas_call | solution.py:56
  5.0 1.8 %collective-permute-start.36 = (bf16[192,512]{1,0:T(8,128)(2,1)}, bf16[192,512]{1,0:T(8,128)(2,1)S(1)}, u32[]{:S(2)}, u32[]{:S(2)}) collective-permute-start(bf16[192,512]{1,0:T(8,128)(2,1)} %get-tuple-element.232), channel_id=1, source_target_pairs={{0,1},{1,2},{2,3},{3,0},{4,5},{5,6},{6,7},{7,4},{8,9},{9,10},{10,1... | collective-permute-start | bytes 589832 | tf_op jit(solution)/shard_map/ppermute | solution.py:26
  7.5 1.3 %collective-permute-start.41 = (s32[384]{0:T(512)S(1)}, s32[384]{0:T(512)S(1)}, u32[]{:S(2)}, u32[]{:S(2)}) collective-permute-start(s32[384]{0:T(512)S(1)} %reshape.43), channel_id=1, source_target_pairs={{0,4},{4,8},{8,12},{12,0},{1,5},{5,9},{9,13},{13,1},{2,6},{6,10},{... | collective-permute-start | bytes 4616 | tf_op jit(solution)/shard_map/ppermute | solution.py:26
  8.9 1.1 collective-permute-start.40
  10.0 0.3 collective-permute-done.41.refs_2_
  10.3 1.7 %collective-permute-start.39 = (s32[384]{0:T(512)S(1)}, s32[384]{0:T(512)S(1)}, u32[]{:S(2)}, u32[]{:S(2)}) collective-permute-start(s32[384]{0:T(512)S(1)} %reshape.43), channel_id=1, source_target_pairs={{0,12},{4,0},{8,4},{12,8},{1,13},{5,1},{9,5},{13,9},{2,14},{6,2},{... | collective-permute-start | bytes 4616 | tf_op jit(solution)/shard_map/ppermute | solution.py:26
  12.1 3.3 %gather_columns.4 = (bf16[192,1280]{1,0:T(8,128)(2,1)S(1)}, bf16[192,1280]{1,0:T(8,128)(2,1)}, bf16[192,1280]{1,0:T(8,128)(2,1)}, bf16[192,1280]{1,0:T(8,128)(2,1)}) custom-call(s32[18]{0:T(128)S(1)} %pad_add_fusion.place_ref, bf16[192,4096]{1,0:T(8,128)(2,1)} %refs_15_.3, bf16[192,4096]{1,0:T(8,128)(2,1)} %refs_16_.3, bf16[192,4096]{1,0:T(8,128)(2,1)} %refs_15_.3, ...), custom_call_target="tpu_custom_call" | custom-call | flops 1024 | bytes 1024 | tf_op jit(solution)/shard_map/gather_columns/pallas_call | solution.py:56
  15.7 0.4 collective-permute-done.37.refs_5_
  16.0 0.6 collective-permute-done.38.refs_6_
  16.6 2.1 %collective-permute-start.42 = (bf16[192,1280]{1,0:T(8,128)(2,1)}, bf16[192,1280]{1,0:T(8,128)(2,1)S(1)}, u32[]{:S(2)}, u32[]{:S(2)}) collective-permute-start(bf16[192,1280]{1,0:T(8,128)(2,1)} %get-tuple-element.242), channel_id=1, source_target_pairs={{0,1},{1,2},{2,3},{3,0},{4,5},{5,6},{6,7},{7,4},{8,9},{9,10},{10,1... | collective-permute-start | bytes 1474568 | tf_op jit(solution)/shard_map/ppermute | solution.py:26
  18.7 1.2 collective-permute-start.47
  19.9 0.6 reduce_max.19
  20.5 2.7 %pick_blocks.9 = (bf16[2,768,256]{2,1,0:T(8,128)(2,1)}, bf16[4,128,256]{2,1,0:T(8,128)(2,1)}, bf16[4,128,256]{2,1,0:T(8,128)(2,1)}, bf16[4,128,256]{2,1,0:T(8,128)(2,1)}) custom-call(s32[18]{0:T(128)S(1)} %pad_add_fusion.place_ref, s32[512]{0:T(512)S(1)} %reshape.44.counts_ref, s32[384]{0:T(512)S(1)} %collective-permute-done.39.refs_0_, ...), custom_call_target="tpu_custom_call" | custom-call | flops 1024 | bytes 1024 | tf_op jit(solution)/shard_map/pick_blocks/pallas_call | solution.py:121
  23.3 3.6 %collective-permute-start.45 = (bf16[4,128,256]{2,1,0:T(8,128)(2,1)}, bf16[4,128,256]{2,1,0:T(8,128)(2,1)S(1)}, u32[]{:S(2)}, u32[]{:S(2)}) collective-permute-start(bf16[4,128,256]{2,1,0:T(8,128)(2,1)} %get-tuple-element.246), channel_id=1, source_target_pairs={{0,8},{4,12},{8,0},{12,4},{1,9},{5,13},{9,1},{13,5},{2,10},{6,14},... | collective-permute-start | bytes 786440 | tf_op jit(solution)/shard_map/ppermute | solution.py:26
  26.9 2.6 %collective-permute-done.42 = bf16[192,1280]{1,0:T(8,128)(2,1)S(1)} collective-permute-done((bf16[192,1280]{1,0:T(8,128)(2,1)}, bf16[192,1280]{1,0:T(8,128)(2,1)S(1)}, u32[]{:S(2)}, u32[]{:S(2)}) %collective-permute-start.42) | collective-permute-done | bytes 491552 | tf_op jit(solution)/shard_map/ppermute | solution.py:26
  29.4 2.7 %collective-permute-done.43 = s32[1]{0:T(128)} collective-permute-done((s32[1]{0:T(128)}, s32[1]{0:T(128)}, u32[]{:S(2)}, u32[]{:S(2)}) %collective-permute-start.43) | collective-permute-done | bytes 36 | tf_op jit(solution)/shard_map/ppermute | solution.py:26
  32.2 1.5 %collective-permute-start.46 = (bf16[4,128,256]{2,1,0:T(8,128)(2,1)}, bf16[4,128,256]{2,1,0:T(8,128)(2,1)S(1)}, u32[]{:S(2)}, u32[]{:S(2)}) collective-permute-start(bf16[4,128,256]{2,1,0:T(8,128)(2,1)} %get-tuple-element.247), channel_id=1, source_target_pairs={{0,12},{4,0},{8,4},{12,8},{1,13},{5,1},{9,5},{13,9},{2,14},{6,2},{... | collective-permute-start | bytes 786440 | tf_op jit(solution)/shard_map/ppermute | solution.py:26
  33.7 3.3 %gather_columns.5 = (bf16[192,1280]{1,0:T(8,128)(2,1)S(1)}, bf16[192,1280]{1,0:T(8,128)(2,1)}, bf16[192,1280]{1,0:T(8,128)(2,1)}, bf16[192,1280]{1,0:T(8,128)(2,1)}) custom-call(s32[18]{0:T(128)S(1)} %pad_add_fusion.place_ref, bf16[192,4096]{1,0:T(8,128)(2,1)} %refs_15_.3, bf16[192,4096]{1,0:T(8,128)(2,1)} %refs_16_.3, bf16[192,4096]{1,0:T(8,128)(2,1)} %refs_19_.3, ...), custom_call_target="tpu_custom_call" | custom-call | flops 1024 | bytes 1024 | tf_op jit(solution)/shard_map/gather_columns/pallas_call | solution.py:56
  38.2 7.5 %collective-permute-done.45 = bf16[4,128,256]{2,1,0:T(8,128)(2,1)S(1)} collective-permute-done((bf16[4,128,256]{2,1,0:T(8,128)(2,1)}, bf16[4,128,256]{2,1,0:T(8,128)(2,1)S(1)}, u32[]{:S(2)}, u32[]{:S(2)}) %collective-permute-start.45) | collective-permute-done | bytes 262176 | tf_op jit(solution)/shard_map/ppermute | solution.py:26
  45.7 3.2 %collective-permute-done.46 = bf16[4,128,256]{2,1,0:T(8,128)(2,1)S(1)} collective-permute-done((bf16[4,128,256]{2,1,0:T(8,128)(2,1)}, bf16[4,128,256]{2,1,0:T(8,128)(2,1)S(1)}, u32[]{:S(2)}, u32[]{:S(2)}) %collective-permute-start.46) | collective-permute-done | bytes 262176 | tf_op jit(solution)/shard_map/ppermute | solution.py:26
  49.0 81.9 %conditional.1 = (bf16[192,4096]{1,0:T(8,128)(2,1)S(1)}) conditional(s32[]{:T(128)} %convert_element_type.7, (s32[18]{0:T(128)S(1)}, s32[512]{0:T(512)S(1)}, s32[384]{0:T(512)S(1)}, s32[384]{0:T(512)S(1)}, s32[384]{0:T(512)S(1)}, /*index=5*/bf16[192,1280]{1,0:T(8,128)(2,1)S(1)}, bf16[192,1280]{1,0:T(8,128)(2,1)S(1)}, bf16[192,1280]{1,0:T(8,128)(2,1)S(1)}, ...), branch_computations={%region_7.8_spmd, %region_8.9_spmd} | conditional | flops 7168 | bytes 38150436 | solution.py:498
  49.0 2.6 %pick_blocks.5 = (bf16[4,768,256]{2,1,0:T(8,128)(2,1)}, bf16[5,128,256]{2,1,0:T(8,128)(2,1)}, bf16[5,128,256]{2,1,0:T(8,128)(2,1)}, bf16[5,128,256]{2,1,0:T(8,128)(2,1)}) custom-call(s32[18]{0:T(128)S(1)} %get-tuple-element.76.place_ref, s32[512]{0:T(512)S(1)} %get-tuple-element.77.counts_ref, s32[384]{0:T(512)S(1)} %get-tuple-element.82.refs_0_, ...), custom_call_target="tpu_custom_call" | custom-call | flops 1024 | bytes 1024 | tf_op jit(solution)/shard_map/cond/branch_0_fun/pick_blocks/pallas_call | solution.py:121
  51.7 1.7 %collective-permute-start.6 = (bf16[192,1280]{1,0:T(8,128)(2,1)}, bf16[192,1280]{1,0:T(8,128)(2,1)S(1)}, u32[]{:S(2)}, u32[]{:S(2)}) collective-permute-start(bf16[192,1280]{1,0:T(8,128)(2,1)} %get-tuple-element.106), channel_id=1, source_target_pairs={{0,1},{1,2},{2,3},{3,0},{4,5},{5,6},{6,7},{7,4},{8,9},{9,10},{10,1... | collective-permute-start | bytes 1474568 | tf_op jit(solution)/shard_map/cond/branch_0_fun/ppermute | solution.py:26
  53.3 1.1 collective-permute-start.7
  54.5 5.3 %collective-permute-done.3.refs_4_ = bf16[5,128,256]{2,1,0:T(8,128)(2,1)} collective-permute-done((bf16[5,128,256]{2,1,0:T(8,128)(2,1)}, bf16[5,128,256]{2,1,0:T(8,128)(2,1)}, u32[]{:S(2)}, u32[]{:S(2)}) %collective-permute-start.3) | collective-permute-done | bytes 327712 | tf_op jit(solution)/shard_map/cond/branch_0_fun/ppermute | solution.py:26
  59.8 8.2 %attend.4 = (bf16[192,256]{1,0:T(8,128)(2,1)}, bf16[192,256]{1,0:T(8,128)(2,1)}, bf16[192,256]{1,0:T(8,128)(2,1)}, bf16[192,256]{1,0:T(8,128)(2,1)}) custom-call(s32[18]{0:T(128)S(1)} %get-tuple-element.76.place_ref, s32[512]{0:T(512)S(1)} %get-tuple-element.77.counts_ref, bf16[2,768,256]{2,1,0:T(8,128)(2,1)} %get-tuple-element.92.tile_ref, ...), custom_call_target="tpu_custom_call" | custom-call | flops 1024 | bytes 1024 | tf_op jit(solution)/shard_map/cond/branch_0_fun/attend/pallas_call | solution.py:295
  68.0 10.9 %collective-permute-done.4.refs_5_ = bf16[5,128,256]{2,1,0:T(8,128)(2,1)} collective-permute-done((bf16[5,128,256]{2,1,0:T(8,128)(2,1)}, bf16[5,128,256]{2,1,0:T(8,128)(2,1)}, u32[]{:S(2)}, u32[]{:S(2)}) %collective-permute-start.4) | collective-permute-done | bytes 327712 | tf_op jit(solution)/shard_map/cond/branch_0_fun/ppermute | solution.py:26
  79.0 0.8 copy-done.1
  80.0 2.7 %pick_blocks.6 = (bf16[2,768,256]{2,1,0:T(8,128)(2,1)}, bf16[4,128,256]{2,1,0:T(8,128)(2,1)}, bf16[4,128,256]{2,1,0:T(8,128)(2,1)}, bf16[4,128,256]{2,1,0:T(8,128)(2,1)}) custom-call(s32[18]{0:T(128)S(1)} %get-tuple-element.76.place_ref, s32[512]{0:T(512)S(1)} %get-tuple-element.77.counts_ref, s32[384]{0:T(512)S(1)} %get-tuple-element.82.refs_0_, ...), custom_call_target="tpu_custom_call" | custom-call | flops 1024 | bytes 1024 | tf_op jit(solution)/shard_map/cond/branch_0_fun/pick_blocks/pallas_call | solution.py:121
  82.7 7.6 %collective-permute-start = (bf16[192,256]{1,0:T(8,128)(2,1)S(1)}, bf16[192,256]{1,0:T(8,128)(2,1)S(1)}, u32[]{:S(2)}, u32[]{:S(2)}) collective-permute-start(bf16[192,256]{1,0:T(8,128)(2,1)S(1)} %copy-done.47), channel_id=1, source_target_pairs={{0,1},{1,2},{2,3},{3,0},{4,5},{5,6},{6,7},{7,4},{8,9},{9,10},{10,1... | collective-permute-start | bytes 294920 | tf_op jit(solution)/shard_map/cond/branch_0_fun/ppermute | solution.py:26
  90.3 1.2 collective-permute-start.1
  91.5 1.2 collective-permute-start.13
  92.7 1.7 %collective-permute-start.14 = (bf16[4,128,256]{2,1,0:T(8,128)(2,1)}, bf16[4,128,256]{2,1,0:T(8,128)(2,1)S(1)}, u32[]{:S(2)}, u32[]{:S(2)}) collective-permute-start(bf16[4,128,256]{2,1,0:T(8,128)(2,1)} %get-tuple-element.115), channel_id=1, source_target_pairs={{0,12},{4,0},{8,4},{12,8},{1,13},{5,1},{9,5},{13,9},{2,14},{6,2},{... | collective-permute-start | bytes 786440 | tf_op jit(solution)/shard_map/cond/branch_0_fun/ppermute | solution.py:26
  94.6 11.9 %attend.5 = (bf16[192,512]{1,0:T(8,128)(2,1)}, bf16[192,512]{1,0:T(8,128)(2,1)}, bf16[192,512]{1,0:T(8,128)(2,1)}, bf16[192,512]{1,0:T(8,128)(2,1)}) custom-call(s32[18]{0:T(128)S(1)} %get-tuple-element.76.place_ref, s32[512]{0:T(512)S(1)} %get-tuple-element.77.counts_ref, bf16[4,768,256]{2,1,0:T(8,128)(2,1)} %get-tuple-element.116.tile_ref, ...), custom_call_target="tpu_custom_call" | custom-call | flops 1024 | bytes 1024 | tf_op jit(solution)/shard_map/cond/branch_0_fun/attend/pallas_call | solution.py:295
  106.8 2.3 %collective-permute-start.10 = (bf16[192,512]{1,0:T(8,128)(2,1)}, bf16[192,512]{1,0:T(8,128)(2,1)S(1)}, u32[]{:S(2)}, u32[]{:S(2)}) collective-permute-start(bf16[192,512]{1,0:T(8,128)(2,1)} %get-tuple-element.122), channel_id=1, source_target_pairs={{0,2},{1,3},{2,0},{3,1},{4,6},{5,7},{6,4},{7,5},{8,10},{9,11},{10,... | collective-permute-start | bytes 589832 | tf_op jit(solution)/shard_map/cond/branch_0_fun/ppermute | solution.py:26
  109.1 4.8 %attend_own.2 = (f32[2,768,128]{2,1,0:T(8,128)}, f32[2,768,128]{2,1,0:T(8,128)}, f32[2,768,128]{2,1,0:T(8,128)}) custom-call(bf16[2,768,256]{2,1,0:T(8,128)(2,1)} %get-tuple-element.124.tile_ref, bf16[192,1280]{1,0:T(8,128)(2,1)S(1)} %get-tuple-element.109.refs_3_.refs_0_, bf16[192,1280]{1,0:T(8,128)(2,1)} %copy-done.1, bf16[192,1280]{1,0:T(8,128)(2,1)} %copy-done.2, ...), custom_call_target="tpu_custom_call" | custom-call | flops 1024 | bytes 1024 | tf_op jit(solution)/shard_map/cond/branch_0_fun/attend_own/pallas_call | solution.py:333
  114.0 0.7 copy-done.15
  114.6 0.7 copy-done.17
  115.3 5.7 %attend_far.2 = (bf16[192,256]{1,0:T(8,128)(2,1)}, bf16[192,256]{1,0:T(8,128)(2,1)}, bf16[192,256]{1,0:T(8,128)(2,1)}, bf16[192,256]{1,0:T(8,128)(2,1)}) custom-call(s32[18]{0:T(128)S(1)} %get-tuple-element.76.place_ref, s32[512]{0:T(512)S(1)} %get-tuple-element.77.counts_ref, f32[2,768,128]{2,1,0:T(8,128)} %get-tuple-element.128.refs_0_, ...), custom_call_target="tpu_custom_call" | custom-call | flops 1024 | bytes 1024 | tf_op jit(solution)/shard_map/cond/branch_0_fun/attend_far/pallas_call | solution.py:295
  121.0 1.7 %collective-permute-start.15 = (bf16[192,256]{1,0:T(8,128)(2,1)}, bf16[192,256]{1,0:T(8,128)(2,1)S(1)}, u32[]{:S(2)}, u32[]{:S(2)}) collective-permute-start(bf16[192,256]{1,0:T(8,128)(2,1)} %get-tuple-element.132), channel_id=1, source_target_pairs={{0,1},{1,2},{2,3},{3,0},{4,5},{5,6},{6,7},{7,4},{8,9},{9,10},{10,1... | collective-permute-start | bytes 294920 | tf_op jit(solution)/shard_map/cond/branch_0_fun/ppermute | solution.py:26
  123.2 1.8 %collective-permute-done.15.refs_9_ = bf16[192,256]{1,0:T(8,128)(2,1)S(1)} collective-permute-done((bf16[192,256]{1,0:T(8,128)(2,1)}, bf16[192,256]{1,0:T(8,128)(2,1)S(1)}, u32[]{:S(2)}, u32[]{:S(2)}) %collective-permute-start.15) | collective-permute-done | bytes 98336 | tf_op jit(solution)/shard_map/cond/branch_0_fun/ppermute | solution.py:26
  125.0 2.7 %collective-permute-done.16.refs_10_ = bf16[192,256]{1,0:T(8,128)(2,1)S(1)} collective-permute-done((bf16[192,256]{1,0:T(8,128)(2,1)}, bf16[192,256]{1,0:T(8,128)(2,1)S(1)}, u32[]{:S(2)}, u32[]{:S(2)}) %collective-permute-start.16) | collective-permute-done | bytes 98336 | tf_op jit(solution)/shard_map/cond/branch_0_fun/ppermute | solution.py:26
  127.7 0.6 collective-permute-done.17.refs_11_
  128.4 0.6 copy-done.38
  129.0 1.7 %lay_out.2 = bf16[192,4096]{1,0:T(8,128)(2,1)S(1)} custom-call(s32[18]{0:T(128)S(1)} %get-tuple-element.76.place_ref, bf16[192,256]{1,0:T(8,128)(2,1)} %get-tuple-element.96.refs_0_, bf16[192,256]{1,0:T(8,128)(2,1)} %copy-done.28, bf16[192,256]{1,0:T(8,128)(2,1)} %copy-done.30, bf16[192,256]{1,0:T(8,128)(2,1)} %copy-done.32, ...), custom_call_target="tpu_custom_call" | custom-call | flops 1024 | bytes 1024 | tf_op jit(solution)/shard_map/cond/branch_0_fun/lay_out/pallas_call | solution.py:379
  130.9 1.1 copy-done.6
  (95 shorter events, 3.3 us)
Async XLA Ops:
  2.3 4.9 %copy-start.41 = (s32[32,1,4,3]{0,2,3,1:T(4,128)S(1)}, s32[32,1,4,3]{0,2,3,1:T(4,128)}, u32[]{:S(2)}) copy-start(s32[32,1,4,3]{0,2,3,1:T(4,128)} %param.10) | copy-start | bytes 4612
  5.0 10.7 %collective-permute-start.36 = (bf16[192,512]{1,0:T(8,128)(2,1)}, bf16[192,512]{1,0:T(8,128)(2,1)S(1)}, u32[]{:S(2)}, u32[]{:S(2)}) collective-permute-start(bf16[192,512]{1,0:T(8,128)(2,1)} %get-tuple-element.232), channel_id=1, source_target_pairs={{0,1},{1,2},{2,3},{3,0},{4,5},{5,6},{6,7},{7,4},{8,9},{9,10},{10,1... | collective-permute-start | bytes 589832 | tf_op jit(solution)/shard_map/ppermute | solution.py:26
  6.8 9.3 %collective-permute-start.37 = (bf16[192,512]{1,0:T(8,128)(2,1)}, bf16[192,512]{1,0:T(8,128)(2,1)S(1)}, u32[]{:S(2)}, u32[]{:S(2)}) collective-permute-start(bf16[192,512]{1,0:T(8,128)(2,1)} %get-tuple-element.233), channel_id=1, source_target_pairs={{0,2},{1,3},{2,0},{3,1},{4,6},{5,7},{6,4},{7,5},{8,10},{9,11},{10,... | collective-permute-start | bytes 589832 | tf_op jit(solution)/shard_map/ppermute | solution.py:26
  7.0 9.6 %collective-permute-start.38 = (bf16[192,512]{1,0:T(8,128)(2,1)}, bf16[192,512]{1,0:T(8,128)(2,1)S(1)}, u32[]{:S(2)}, u32[]{:S(2)}) collective-permute-start(bf16[192,512]{1,0:T(8,128)(2,1)} %get-tuple-element.234), channel_id=1, source_target_pairs={{0,3},{1,0},{2,1},{3,2},{4,7},{5,4},{6,5},{7,6},{8,11},{9,8},{10,9... | collective-permute-start | bytes 589832 | tf_op jit(solution)/shard_map/ppermute | solution.py:26
  7.5 7.8 %copy-start.40 = (s32[32,4,4]{0,2,1:T(4,128)S(1)}, s32[32,4,4]{0,2,1:T(4,128)}, u32[]{:S(2)}) copy-start(s32[32,4,4]{0,2,1:T(4,128)} %param.11) | copy-start | bytes 6148
  7.5 2.8 %collective-permute-start.41 = (s32[384]{0:T(512)S(1)}, s32[384]{0:T(512)S(1)}, u32[]{:S(2)}, u32[]{:S(2)}) collective-permute-start(s32[384]{0:T(512)S(1)} %reshape.43), channel_id=1, source_target_pairs={{0,4},{4,8},{8,12},{12,0},{1,5},{5,9},{9,13},{13,1},{2,6},{6,10},{... | collective-permute-start | bytes 4616 | tf_op jit(solution)/shard_map/ppermute | solution.py:26
  8.9 6.7 %collective-permute-start.40 = (s32[384]{0:T(512)S(1)}, s32[384]{0:T(512)S(1)}, u32[]{:S(2)}, u32[]{:S(2)}) collective-permute-start(s32[384]{0:T(512)S(1)} %reshape.43), channel_id=1, source_target_pairs={{0,8},{4,12},{8,0},{12,4},{1,9},{5,13},{9,1},{13,5},{2,10},{6,14},... | collective-permute-start | bytes 4616 | tf_op jit(solution)/shard_map/ppermute | solution.py:26
  10.3 5.3 %collective-permute-start.39 = (s32[384]{0:T(512)S(1)}, s32[384]{0:T(512)S(1)}, u32[]{:S(2)}, u32[]{:S(2)}) collective-permute-start(s32[384]{0:T(512)S(1)} %reshape.43), channel_id=1, source_target_pairs={{0,12},{4,0},{8,4},{12,8},{1,13},{5,1},{9,5},{13,9},{2,14},{6,2},{... | collective-permute-start | bytes 4616 | tf_op jit(solution)/shard_map/ppermute | solution.py:26
  15.7 4.8 %copy-start.19 = (bf16[192,512]{1,0:T(8,128)(2,1)}, bf16[192,512]{1,0:T(8,128)(2,1)S(1)}, u32[]{:S(2)}) copy-start(bf16[192,512]{1,0:T(8,128)(2,1)S(1)} %collective-permute-done.36.refs_4_) | copy-start | bytes 589828
  16.0 4.5 %copy-start.20 = (bf16[192,512]{1,0:T(8,128)(2,1)}, bf16[192,512]{1,0:T(8,128)(2,1)S(1)}, u32[]{:S(2)}) copy-start(bf16[192,512]{1,0:T(8,128)(2,1)S(1)} %collective-permute-done.37.refs_5_) | copy-start | bytes 589828
  16.6 3.9 %copy-start.21 = (bf16[192,512]{1,0:T(8,128)(2,1)}, bf16[192,512]{1,0:T(8,128)(2,1)S(1)}, u32[]{:S(2)}) copy-start(bf16[192,512]{1,0:T(8,128)(2,1)S(1)} %collective-permute-done.38.refs_6_) | copy-start | bytes 589828
  16.6 12.8 %collective-permute-start.42 = (bf16[192,1280]{1,0:T(8,128)(2,1)}, bf16[192,1280]{1,0:T(8,128)(2,1)S(1)}, u32[]{:S(2)}, u32[]{:S(2)}) collective-permute-start(bf16[192,1280]{1,0:T(8,128)(2,1)} %get-tuple-element.242), channel_id=1, source_target_pairs={{0,1},{1,2},{2,3},{3,0},{4,5},{5,6},{6,7},{7,4},{8,9},{9,10},{10,1... | collective-permute-start | bytes 1474568 | tf_op jit(solution)/shard_map/ppermute | solution.py:26
  18.7 30.3 %collective-permute-start.47 = (bf16[192,1280]{1,0:T(8,128)(2,1)}, bf16[192,1280]{1,0:T(8,128)(2,1)S(1)}, u32[]{:S(2)}, u32[]{:S(2)}) collective-permute-start(bf16[192,1280]{1,0:T(8,128)(2,1)} %get-tuple-element.249), channel_id=1, source_target_pairs={{0,2},{1,3},{2,0},{3,1},{4,6},{5,7},{6,4},{7,5},{8,10},{9,11},{10,... | collective-permute-start | bytes 1474568 | tf_op jit(solution)/shard_map/ppermute | solution.py:26
  19.9 29.1 %collective-permute-start.48 = (bf16[192,1280]{1,0:T(8,128)(2,1)}, bf16[192,1280]{1,0:T(8,128)(2,1)S(1)}, u32[]{:S(2)}, u32[]{:S(2)}) collective-permute-start(bf16[192,1280]{1,0:T(8,128)(2,1)} %get-tuple-element.250), channel_id=1, source_target_pairs={{0,3},{1,0},{2,1},{3,2},{4,7},{5,4},{6,5},{7,6},{8,11},{9,8},{10,9... | collective-permute-start | bytes 1474568 | tf_op jit(solution)/shard_map/ppermute | solution.py:26
  23.2 15.0 %collective-permute-start.44 = (bf16[4,128,256]{2,1,0:T(8,128)(2,1)}, bf16[4,128,256]{2,1,0:T(8,128)(2,1)S(1)}, u32[]{:S(2)}, u32[]{:S(2)}) collective-permute-start(bf16[4,128,256]{2,1,0:T(8,128)(2,1)} %get-tuple-element.245), channel_id=1, source_target_pairs={{0,4},{4,8},{8,12},{12,0},{1,5},{5,9},{9,13},{13,1},{2,6},{6,10},{... | collective-permute-start | bytes 786440 | tf_op jit(solution)/shard_map/ppermute | solution.py:26
  23.3 22.5 %collective-permute-start.45 = (bf16[4,128,256]{2,1,0:T(8,128)(2,1)}, bf16[4,128,256]{2,1,0:T(8,128)(2,1)S(1)}, u32[]{:S(2)}, u32[]{:S(2)}) collective-permute-start(bf16[4,128,256]{2,1,0:T(8,128)(2,1)} %get-tuple-element.246), channel_id=1, source_target_pairs={{0,8},{4,12},{8,0},{12,4},{1,9},{5,13},{9,1},{13,5},{2,10},{6,14},... | collective-permute-start | bytes 786440 | tf_op jit(solution)/shard_map/ppermute | solution.py:26
  29.4 2.7 %collective-permute-start.43 = (s32[1]{0:T(128)}, s32[1]{0:T(128)}, u32[]{:S(2)}, u32[]{:S(2)}) collective-permute-start(s32[1]{0:T(128)} %bitcast.3), channel_id=1, source_target_pairs={{0,16},{16,0},{1,17},{17,1},{2,18},{18,2},{3,19},{19,3},{4,20},{20... | collective-permute-start | bytes 20 | tf_op jit(solution)/shard_map/ppermute | solution.py:26
  32.2 16.8 %collective-permute-start.46 = (bf16[4,128,256]{2,1,0:T(8,128)(2,1)}, bf16[4,128,256]{2,1,0:T(8,128)(2,1)S(1)}, u32[]{:S(2)}, u32[]{:S(2)}) collective-permute-start(bf16[4,128,256]{2,1,0:T(8,128)(2,1)} %get-tuple-element.247), channel_id=1, source_target_pairs={{0,12},{4,0},{8,4},{12,8},{1,13},{5,1},{9,5},{13,9},{2,14},{6,2},{... | collective-permute-start | bytes 786440 | tf_op jit(solution)/shard_map/ppermute | solution.py:26
  49.0 4.3 %copy-start.11 = (bf16[4,128,256]{2,1,0:T(8,128)(2,1)}, bf16[4,128,256]{2,1,0:T(8,128)(2,1)S(1)}, u32[]{:S(2)}) copy-start(bf16[4,128,256]{2,1,0:T(8,128)(2,1)S(1)} %get-tuple-element.95.refs_6_) | copy-start | bytes 786436 | tf_op jit(solution)/shard_map/cond
  51.7 8.1 %collective-permute-start.3 = (bf16[5,128,256]{2,1,0:T(8,128)(2,1)}, bf16[5,128,256]{2,1,0:T(8,128)(2,1)}, u32[]{:S(2)}, u32[]{:S(2)}) collective-permute-start(bf16[5,128,256]{2,1,0:T(8,128)(2,1)} %get-tuple-element.89), channel_id=1, source_target_pairs={{0,4},{4,8},{8,12},{12,0},{1,5},{5,9},{9,13},{13,1},{2,6},{6,10},{... | collective-permute-start | bytes 983048 | tf_op jit(solution)/shard_map/cond/branch_0_fun/ppermute | solution.py:26
  51.7 27.3 %collective-permute-start.6 = (bf16[192,1280]{1,0:T(8,128)(2,1)}, bf16[192,1280]{1,0:T(8,128)(2,1)S(1)}, u32[]{:S(2)}, u32[]{:S(2)}) collective-permute-start(bf16[192,1280]{1,0:T(8,128)(2,1)} %get-tuple-element.106), channel_id=1, source_target_pairs={{0,1},{1,2},{2,3},{3,0},{4,5},{5,6},{6,7},{7,4},{8,9},{9,10},{10,1... | collective-permute-start | bytes 1474568 | tf_op jit(solution)/shard_map/cond/branch_0_fun/ppermute | solution.py:26
  53.3 25.6 %collective-permute-start.7 = (bf16[192,1280]{1,0:T(8,128)(2,1)}, bf16[192,1280]{1,0:T(8,128)(2,1)S(1)}, u32[]{:S(2)}, u32[]{:S(2)}) collective-permute-start(bf16[192,1280]{1,0:T(8,128)(2,1)} %get-tuple-element.107), channel_id=1, source_target_pairs={{0,2},{1,3},{2,0},{3,1},{4,6},{5,7},{6,4},{7,5},{8,10},{9,11},{10,... | collective-permute-start | bytes 1474568 | tf_op jit(solution)/shard_map/cond/branch_0_fun/ppermute | solution.py:26
  54.5 24.5 %collective-permute-start.8 = (bf16[192,1280]{1,0:T(8,128)(2,1)}, bf16[192,1280]{1,0:T(8,128)(2,1)S(1)}, u32[]{:S(2)}, u32[]{:S(2)}) collective-permute-start(bf16[192,1280]{1,0:T(8,128)(2,1)} %get-tuple-element.108), channel_id=1, source_target_pairs={{0,3},{1,0},{2,1},{3,2},{4,7},{5,4},{6,5},{7,6},{8,11},{9,8},{10,9... | collective-permute-start | bytes 1474568 | tf_op jit(solution)/shard_map/cond/branch_0_fun/ppermute | solution.py:26
  54.5 24.4 %collective-permute-start.4 = (bf16[5,128,256]{2,1,0:T(8,128)(2,1)}, bf16[5,128,256]{2,1,0:T(8,128)(2,1)}, u32[]{:S(2)}, u32[]{:S(2)}) collective-permute-start(bf16[5,128,256]{2,1,0:T(8,128)(2,1)} %get-tuple-element.90), channel_id=1, source_target_pairs={{0,8},{4,12},{8,0},{12,4},{1,9},{5,13},{9,1},{13,5},{2,10},{6,14},... | collective-permute-start | bytes 983048 | tf_op jit(solution)/shard_map/cond/branch_0_fun/ppermute | solution.py:26
  59.8 19.2 %collective-permute-start.5 = (bf16[5,128,256]{2,1,0:T(8,128)(2,1)}, bf16[5,128,256]{2,1,0:T(8,128)(2,1)}, u32[]{:S(2)}, u32[]{:S(2)}) collective-permute-start(bf16[5,128,256]{2,1,0:T(8,128)(2,1)} %get-tuple-element.91), channel_id=1, source_target_pairs={{0,12},{4,0},{8,4},{12,8},{1,13},{5,1},{9,5},{13,9},{2,14},{6,2},{... | collective-permute-start | bytes 983048 | tf_op jit(solution)/shard_map/cond/branch_0_fun/ppermute | solution.py:26
  68.0 14.8 %copy-start.47 = (bf16[192,256]{1,0:T(8,128)(2,1)S(1)}, bf16[192,256]{1,0:T(8,128)(2,1)}, u32[]{:S(2)}) copy-start(bf16[192,256]{1,0:T(8,128)(2,1)} %get-tuple-element.97) | copy-start | bytes 294916 | tf_op jit(solution)/shard_map/cond
  68.0 22.4 %copy-start.45 = (bf16[192,256]{1,0:T(8,128)(2,1)S(1)}, bf16[192,256]{1,0:T(8,128)(2,1)}, u32[]{:S(2)}) copy-start(bf16[192,256]{1,0:T(8,128)(2,1)} %get-tuple-element.98) | copy-start | bytes 294916 | tf_op jit(solution)/shard_map/cond
  68.0 26.4 %copy-start.43 = (bf16[192,256]{1,0:T(8,128)(2,1)S(1)}, bf16[192,256]{1,0:T(8,128)(2,1)}, u32[]{:S(2)}) copy-start(bf16[192,256]{1,0:T(8,128)(2,1)} %get-tuple-element.99) | copy-start | bytes 294916 | tf_op jit(solution)/shard_map/cond
  82.7 26.4 %collective-permute-start.12 = (bf16[4,128,256]{2,1,0:T(8,128)(2,1)}, bf16[4,128,256]{2,1,0:T(8,128)(2,1)S(1)}, u32[]{:S(2)}, u32[]{:S(2)}) collective-permute-start(bf16[4,128,256]{2,1,0:T(8,128)(2,1)} %get-tuple-element.113), channel_id=1, source_target_pairs={{0,4},{4,8},{8,12},{12,0},{1,5},{5,9},{9,13},{13,1},{2,6},{6,10},{... | collective-permute-start | bytes 786440 | tf_op jit(solution)/shard_map/cond/branch_0_fun/ppermute | solution.py:26
  82.7 11.6 %collective-permute-start = (bf16[192,256]{1,0:T(8,128)(2,1)S(1)}, bf16[192,256]{1,0:T(8,128)(2,1)S(1)}, u32[]{:S(2)}, u32[]{:S(2)}) collective-permute-start(bf16[192,256]{1,0:T(8,128)(2,1)S(1)} %copy-done.47), channel_id=1, source_target_pairs={{0,1},{1,2},{2,3},{3,0},{4,5},{5,6},{6,7},{7,4},{8,9},{9,10},{10,1... | collective-permute-start | bytes 294920 | tf_op jit(solution)/shard_map/cond/branch_0_fun/ppermute | solution.py:26
  90.3 16.2 %collective-permute-start.1 = (bf16[192,256]{1,0:T(8,128)(2,1)S(1)}, bf16[192,256]{1,0:T(8,128)(2,1)S(1)}, u32[]{:S(2)}, u32[]{:S(2)}) collective-permute-start(bf16[192,256]{1,0:T(8,128)(2,1)S(1)} %copy-done.45), channel_id=1, source_target_pairs={{0,2},{1,3},{2,0},{3,1},{4,6},{5,7},{6,4},{7,5},{8,10},{9,11},{10,... | collective-permute-start | bytes 294920 | tf_op jit(solution)/shard_map/cond/branch_0_fun/ppermute | solution.py:26
  91.5 22.5 %collective-permute-start.13 = (bf16[4,128,256]{2,1,0:T(8,128)(2,1)}, bf16[4,128,256]{2,1,0:T(8,128)(2,1)S(1)}, u32[]{:S(2)}, u32[]{:S(2)}) collective-permute-start(bf16[4,128,256]{2,1,0:T(8,128)(2,1)} %get-tuple-element.114), channel_id=1, source_target_pairs={{0,8},{4,12},{8,0},{12,4},{1,9},{5,13},{9,1},{13,5},{2,10},{6,14},... | collective-permute-start | bytes 786440 | tf_op jit(solution)/shard_map/cond/branch_0_fun/ppermute | solution.py:26
  92.7 21.2 %collective-permute-start.14 = (bf16[4,128,256]{2,1,0:T(8,128)(2,1)}, bf16[4,128,256]{2,1,0:T(8,128)(2,1)S(1)}, u32[]{:S(2)}, u32[]{:S(2)}) collective-permute-start(bf16[4,128,256]{2,1,0:T(8,128)(2,1)} %get-tuple-element.115), channel_id=1, source_target_pairs={{0,12},{4,0},{8,4},{12,8},{1,13},{5,1},{9,5},{13,9},{2,14},{6,2},{... | collective-permute-start | bytes 786440 | tf_op jit(solution)/shard_map/cond/branch_0_fun/ppermute | solution.py:26
  94.4 12.1 %copy-start.28 = (bf16[192,256]{1,0:T(8,128)(2,1)}, bf16[192,256]{1,0:T(8,128)(2,1)S(1)}, u32[]{:S(2)}) copy-start(bf16[192,256]{1,0:T(8,128)(2,1)S(1)} %collective-permute-done.refs_1_) | copy-start | bytes 294916 | tf_op jit(solution)/shard_map/cond
  94.4 12.4 %collective-permute-start.2 = (bf16[192,256]{1,0:T(8,128)(2,1)S(1)}, bf16[192,256]{1,0:T(8,128)(2,1)S(1)}, u32[]{:S(2)}, u32[]{:S(2)}) collective-permute-start(bf16[192,256]{1,0:T(8,128)(2,1)S(1)} %copy-done.43), channel_id=1, source_target_pairs={{0,3},{1,0},{2,1},{3,2},{4,7},{5,4},{6,5},{7,6},{8,11},{9,8},{10,9... | collective-permute-start | bytes 294920 | tf_op jit(solution)/shard_map/cond/branch_0_fun/ppermute | solution.py:26
  106.5 14.5 %copy-start.30 = (bf16[192,256]{1,0:T(8,128)(2,1)}, bf16[192,256]{1,0:T(8,128)(2,1)S(1)}, u32[]{:S(2)}) copy-start(bf16[192,256]{1,0:T(8,128)(2,1)S(1)} %collective-permute-done.1.refs_2_) | copy-start | bytes 294916 | tf_op jit(solution)/shard_map/cond
  106.5 16.4 %collective-permute-start.9 = (bf16[192,512]{1,0:T(8,128)(2,1)}, bf16[192,512]{1,0:T(8,128)(2,1)S(1)}, u32[]{:S(2)}, u32[]{:S(2)}) collective-permute-start(bf16[192,512]{1,0:T(8,128)(2,1)} %get-tuple-element.121), channel_id=1, source_target_pairs={{0,1},{1,2},{2,3},{3,0},{4,5},{5,6},{6,7},{7,4},{8,9},{9,10},{10,1... | collective-permute-start | bytes 589832 | tf_op jit(solution)/shard_map/cond/branch_0_fun/ppermute | solution.py:26
  106.8 14.2 %copy-start.32 = (bf16[192,256]{1,0:T(8,128)(2,1)}, bf16[192,256]{1,0:T(8,128)(2,1)S(1)}, u32[]{:S(2)}) copy-start(bf16[192,256]{1,0:T(8,128)(2,1)S(1)} %collective-permute-done.2.refs_3_) | copy-start | bytes 294916 | tf_op jit(solution)/shard_map/cond
  106.8 16.4 %collective-permute-start.10 = (bf16[192,512]{1,0:T(8,128)(2,1)}, bf16[192,512]{1,0:T(8,128)(2,1)S(1)}, u32[]{:S(2)}, u32[]{:S(2)}) collective-permute-start(bf16[192,512]{1,0:T(8,128)(2,1)} %get-tuple-element.122), channel_id=1, source_target_pairs={{0,2},{1,3},{2,0},{3,1},{4,6},{5,7},{6,4},{7,5},{8,10},{9,11},{10,... | collective-permute-start | bytes 589832 | tf_op jit(solution)/shard_map/cond/branch_0_fun/ppermute | solution.py:26
  109.1 4.8 %copy-start.13 = (bf16[4,128,256]{2,1,0:T(8,128)(2,1)}, bf16[4,128,256]{2,1,0:T(8,128)(2,1)S(1)}, u32[]{:S(2)}) copy-start(bf16[4,128,256]{2,1,0:T(8,128)(2,1)S(1)} %collective-permute-done.12.refs_7_) | copy-start | bytes 786436 | tf_op jit(solution)/shard_map/cond
  109.1 14.1 %collective-permute-start.11 = (bf16[192,512]{1,0:T(8,128)(2,1)}, bf16[192,512]{1,0:T(8,128)(2,1)S(1)}, u32[]{:S(2)}, u32[]{:S(2)}) collective-permute-start(bf16[192,512]{1,0:T(8,128)(2,1)} %get-tuple-element.123), channel_id=1, source_target_pairs={{0,3},{1,0},{2,1},{3,2},{4,7},{5,4},{6,5},{7,6},{8,11},{9,8},{10,9... | collective-permute-start | bytes 589832 | tf_op jit(solution)/shard_map/cond/branch_0_fun/ppermute | solution.py:26
  121.0 4.0 %collective-permute-start.15 = (bf16[192,256]{1,0:T(8,128)(2,1)}, bf16[192,256]{1,0:T(8,128)(2,1)S(1)}, u32[]{:S(2)}, u32[]{:S(2)}) collective-permute-start(bf16[192,256]{1,0:T(8,128)(2,1)} %get-tuple-element.132), channel_id=1, source_target_pairs={{0,1},{1,2},{2,3},{3,0},{4,5},{5,6},{6,7},{7,4},{8,9},{9,10},{10,1... | collective-permute-start | bytes 294920 | tf_op jit(solution)/shard_map/cond/branch_0_fun/ppermute | solution.py:26
  122.7 5.0 %collective-permute-start.16 = (bf16[192,256]{1,0:T(8,128)(2,1)}, bf16[192,256]{1,0:T(8,128)(2,1)S(1)}, u32[]{:S(2)}, u32[]{:S(2)}) collective-permute-start(bf16[192,256]{1,0:T(8,128)(2,1)} %get-tuple-element.133), channel_id=1, source_target_pairs={{0,2},{1,3},{2,0},{3,1},{4,6},{5,7},{6,4},{7,5},{8,10},{9,11},{10,... | collective-permute-start | bytes 294920 | tf_op jit(solution)/shard_map/cond/branch_0_fun/ppermute | solution.py:26
  123.0 5.4 %copy-start.22 = (bf16[192,512]{1,0:T(8,128)(2,1)}, bf16[192,512]{1,0:T(8,128)(2,1)S(1)}, u32[]{:S(2)}) copy-start(bf16[192,512]{1,0:T(8,128)(2,1)S(1)} %collective-permute-done.9.refs_5_) | copy-start | bytes 589828 | tf_op jit(solution)/shard_map/cond
  123.0 5.4 %collective-permute-start.17 = (bf16[192,256]{1,0:T(8,128)(2,1)}, bf16[192,256]{1,0:T(8,128)(2,1)S(1)}, u32[]{:S(2)}, u32[]{:S(2)}) collective-permute-start(bf16[192,256]{1,0:T(8,128)(2,1)} %get-tuple-element.134), channel_id=1, source_target_pairs={{0,3},{1,0},{2,1},{3,2},{4,7},{5,4},{6,5},{7,6},{8,11},{9,8},{10,9... | collective-permute-start | bytes 294920 | tf_op jit(solution)/shard_map/cond/branch_0_fun/ppermute | solution.py:26
  123.2 5.2 %copy-start.24 = (bf16[192,512]{1,0:T(8,128)(2,1)}, bf16[192,512]{1,0:T(8,128)(2,1)S(1)}, u32[]{:S(2)}) copy-start(bf16[192,512]{1,0:T(8,128)(2,1)S(1)} %collective-permute-done.10.refs_6_) | copy-start | bytes 589828 | tf_op jit(solution)/shard_map/cond
  123.2 5.2 %copy-start.26 = (bf16[192,512]{1,0:T(8,128)(2,1)}, bf16[192,512]{1,0:T(8,128)(2,1)S(1)}, u32[]{:S(2)}) copy-start(bf16[192,512]{1,0:T(8,128)(2,1)S(1)} %collective-permute-done.11.refs_7_) | copy-start | bytes 589828 | tf_op jit(solution)/shard_map/cond
  125.0 3.3 %copy-start.34 = (bf16[192,256]{1,0:T(8,128)(2,1)}, bf16[192,256]{1,0:T(8,128)(2,1)S(1)}, u32[]{:S(2)}) copy-start(bf16[192,256]{1,0:T(8,128)(2,1)S(1)} %collective-permute-done.15.refs_9_) | copy-start | bytes 294916 | tf_op jit(solution)/shard_map/cond
  (10 other events, 12.0 us)

commit v4 on v3

--- a/solution.py
+++ b/solution.py
@@ -16,12 +16,34 @@
 TILE = 768
 PAIR = 2 * DH
 LIGHT_MOST = 1
-VMEM_LIMIT = 60 * 1024 * 1024
+VMEM_LIMIT = 60 * 1024 * 1024 + 448 * 1024
 SMEM = pltpu.SMEM
+LONG = pl.CostEstimate(flops=2 * 10**11, bytes_accessed=2 * 10**9, transcendentals=0)
 BRIEF = pl.CostEstimate(flops=1024, bytes_accessed=1024, transcendentals=0)
 
 
+def paired(size):
+    return size & (size - 1) == 0
+
+
+def ahead(rank, step, size):
+    return rank ^ step if paired(size) else (rank + step) % size
+
+
+def behind(rank, step, size):
+    return rank ^ step if paired(size) else (rank + size - step) % size
+
+
+def backward(step, size):
+    return step if paired(size) else size - step
+
+
 def shifted(array, axis, step):
+    size = lax.axis_size(axis)
+    return lax.ppermute(array, axis, [(i, ahead(i, step, size)) for i in range(size)])
+
+
+def turned(array, axis, step):
     size = lax.axis_size(axis)
     return lax.ppermute(array, axis, [(i, (i + step) % size) for i in range(size)])
 
@@ -48,7 +70,7 @@
 
     def column_of(step, pair):
         def index(i, place_ref):
-            rank = lax.rem(place_ref[1] + step, head_count)
+            rank = ahead(place_ref[1], step, head_count)
             return 0, place_ref[2 + rank * local_pairs + pair]
 
         return index
@@ -81,7 +103,7 @@
     rows = TILE // head_count
     pair_at = 2 + my_head * (HEADS // 2 // head_count) + first_pair
     for step in range(head_count):
-        rank = lax.rem(my_head - step + head_count, head_count)
+        rank = behind(my_head, step, head_count)
         place = pl.ds(pl.multiple_of(rank * rows, 16), rows)
         for pair in range(len(caps)):
             for half in range(2):
@@ -153,12 +175,28 @@
     )
 
 
-def start_state(queries, keys, values, scale):
-    scores = score(queries, keys, scale)
+def start_state(queries, tile_ref, top_ref, sum_ref, mix_ref):
+    for start in range(0, TILE, GROUP):
+        scores = score(queries, tile_ref[0, start : start + GROUP, :DH], SCALE)
+        values = tile_ref[0, start : start + GROUP, DH:]
+        add_group(scores, values, top_ref, sum_ref, mix_ref, start == 0)
+
+
+def add_group(scores, values, top_ref, sum_ref, mix_ref, first):
     top = row_top(scores)
+    if not first:
+        old_top = top_ref[...]
+        top = jnp.maximum(old_top, top)
     weights = weigh(scores, top)
+    sums = fold(weights, jnp.add)
     mixture = jnp.dot(weights.astype(jnp.bfloat16), values, preferred_element_type=jnp.float32)
-    return top, fold(weights, jnp.add), mixture
+    if not first:
+        rescale = jnp.exp2(old_top - top)
+        sums = sum_ref[...] * rescale + sums
+        mixture = mix_ref[...] * rescale + mixture
+    top_ref[...] = top
+    sum_ref[...] = sums
+    mix_ref[...] = mixture
 
 
 def score(queries, keys, scale):
@@ -171,15 +209,15 @@
 SCALE = math.log2(math.e) / math.sqrt(DH)
 
 
-def fetch_blocks(place_ref, counts_ref, block_refs, k_ref, v_ref, head_count, first_pair):
+def block_copies(place_ref, counts_ref, block_refs, kv_ref, sems, head_count, first_pair, turn):
     seq_count = len(block_refs) + 1
     my_seq = place_ref[0]
-    turn = pl.program_id(0)
     half = lax.rem(turn, 2)
     pair_at = 2 + place_ref[1] * (HEADS // 2 // head_count) + first_pair
     first = 2 * place_ref[pair_at + turn // 2]
     slot_most = block_refs[0].shape[0] - 1
     used = jnp.int32(0)
+    copies = []
     for step in range(1, seq_count):
         holder = lax.rem(my_seq - step + seq_count, seq_count)
         first_count = counts_ref[(first * seq_count + my_seq) * seq_count + holder]
@@ -187,43 +225,54 @@
         count = jnp.where(half == 0, first_count, second_count)
         start = jnp.where(half == 0, 0, first_count) + turn // 2 * PAIR_MOST
         for entry in range(MOST):
-
-            @pl.when(entry < count)
-            def _():
-                place = pl.ds(pl.multiple_of((used + entry) * BLOCK, BLOCK), BLOCK)
-                slot = jnp.minimum(start + entry, slot_most)
-                k_ref[place, :] = block_refs[step - 1][slot, :, :DH]
-                v_ref[place, :] = block_refs[step - 1][slot, :, DH:]
-
+            place = pl.ds(pl.multiple_of((used + entry) * BLOCK, BLOCK), BLOCK)
+            copy = pltpu.make_async_copy(
+                block_refs[step - 1].at[jnp.minimum(start + entry, slot_most)],
+                kv_ref.at[half, place],
+                sems.at[half, len(copies)],
+            )
+            copies.append((entry < count, copy))
         used = used + count
-    return used
-
-
-def visit_blocks(used, q_ref, k_ref, v_ref, top_ref, sum_ref, mix_ref):
+    return copies, used
+
+
+def start_copies(copies, also=True):
+    for needed, copy in copies:
+        pl.when(needed & also)(copy.start)
+
+
+def wait_copies(copies):
+    for needed, copy in copies:
+        pl.when(needed)(copy.wait)
+
+
+def fetch_blocks(place_ref, counts_ref, block_refs, kv_ref, sems, head_count, first_pair):
+    turn, turns = pl.program_id(0), pl.num_programs(0)
+    shared = (place_ref, counts_ref, block_refs, kv_ref, sems, head_count, first_pair)
+    copies, used = block_copies(*shared, turn)
+
+    @pl.when(turn == 0)
+    def _():
+        kv_ref[...] = jnp.zeros_like(kv_ref)
+        start_copies(copies)
+
+    later, _ = block_copies(*shared, jnp.minimum(turn + 1, turns - 1))
+    start_copies(later, turn + 1 < turns)
+    return copies, used
+
+
+def visit_blocks(used, q_ref, kv_ref, top_ref, sum_ref, mix_ref):
+    half = lax.rem(pl.program_id(0), 2)
+
     def visit(group, carry):
         place = pl.ds(pl.multiple_of(group * GROUP, GROUP), GROUP)
         column = lax.broadcasted_iota(jnp.int32, (1, GROUP), 1) + group * GROUP
         bias = jnp.where(column < used * BLOCK, 0.0, -jnp.inf)
-        scores = score(q_ref[...], k_ref[place, :], SCALE) + bias
-        old_top = top_ref[...]
-        top = jnp.maximum(old_top, row_top(scores))
-        weights = weigh(scores, top)
-        rescale = jnp.exp2(old_top - top)
-        top_ref[...] = top
-        sum_ref[...] = sum_ref[...] * rescale + fold(weights, jnp.add)
-        mix_ref[...] = mix_ref[...] * rescale + jnp.dot(
-            weights.astype(jnp.bfloat16), v_ref[place, :], preferred_element_type=jnp.float32
-        )
+        scores = score(q_ref[...], kv_ref[half, place, :DH], SCALE) + bias
+        add_group(scores, kv_ref[half, place, DH:], top_ref, sum_ref, mix_ref, False)
         return carry
 
     lax.fori_loop(0, (used + 2) // 3, visit, 0)
-
-
-def clear_blocks(k_ref, v_ref):
-    @pl.when(pl.program_id(0) == 0)
-    def _():
-        k_ref[...] = jnp.zeros_like(k_ref)
-        v_ref[...] = jnp.zeros_like(v_ref)
 
 
 def join_pieces(query_refs, q_ref):
@@ -240,27 +289,26 @@
         ref[...] = (mix_ref[span, :] / total).astype(jnp.bfloat16)
 
 
-def attend_kernel(head_count, seq_count, first_pair, place_ref, counts_ref, tile_ref, *refs):
+def attend_kernel(head_count, seq_count, first_pair, joined, place_ref, counts_ref, tile_ref, *refs):
     query_refs, refs = refs[:head_count], refs[head_count:]
     block_refs, refs = refs[: seq_count - 1], refs[seq_count - 1 :]
+    refs = refs[head_count:] if joined else refs
     out_refs, refs = refs[:head_count], refs[head_count:]
-    q_ref, k_ref, v_ref, top_ref, sum_ref, mix_ref = refs
-    clear_blocks(k_ref, v_ref)
+    q_ref, kv_ref, top_ref, sum_ref, mix_ref, sems = refs
     join_pieces(query_refs, q_ref)
-    used = fetch_blocks(place_ref, counts_ref, block_refs, k_ref, v_ref, head_count, first_pair)
-    top_ref[...], sum_ref[...], mix_ref[...] = start_state(
-        q_ref[...], tile_ref[0, :, :DH], tile_ref[0, :, DH:], SCALE
-    )
-    visit_blocks(used, q_ref, k_ref, v_ref, top_ref, sum_ref, mix_ref)
+    copies, used = fetch_blocks(
+        place_ref, counts_ref, block_refs, kv_ref, sems, head_count, first_pair
+    )
+    start_state(q_ref[...], tile_ref, top_ref, sum_ref, mix_ref)
+    wait_copies(copies)
+    visit_blocks(used, q_ref, kv_ref, top_ref, sum_ref, mix_ref)
     split_result(out_refs, sum_ref, mix_ref)
 
 
 def own_kernel(head_count, tile_ref, *refs):
     query_refs, (top_ref, sum_ref, mix_ref, q_ref) = refs[:head_count], refs[head_count:]
     join_pieces(query_refs, q_ref)
-    top_ref[0], sum_ref[0], mix_ref[0] = start_state(
-        q_ref[...], tile_ref[0, :, :DH], tile_ref[0, :, DH:], SCALE
-    )
+    start_state(q_ref[...], tile_ref, top_ref.at[0], sum_ref.at[0], mix_ref.at[0])
 
 
 def far_kernel(head_count, seq_count, first_pair, place_ref, counts_ref, *refs):
@@ -268,12 +316,14 @@
     query_refs, refs = refs[3 : 3 + head_count], refs[3 + head_count :]
     block_refs, refs = refs[: seq_count - 1], refs[seq_count - 1 :]
     out_refs, refs = refs[:head_count], refs[head_count:]
-    q_ref, k_ref, v_ref, top_ref, sum_ref, mix_ref = refs
-    clear_blocks(k_ref, v_ref)
+    q_ref, kv_ref, top_ref, sum_ref, mix_ref, sems = refs
     join_pieces(query_refs, q_ref)
-    used = fetch_blocks(place_ref, counts_ref, block_refs, k_ref, v_ref, head_count, first_pair)
+    copies, used = fetch_blocks(
+        place_ref, counts_ref, block_refs, kv_ref, sems, head_count, first_pair
+    )
     top_ref[...], sum_ref[...], mix_ref[...] = old_top_ref[0], old_sum_ref[0], old_mix_ref[0]
-    visit_blocks(used, q_ref, k_ref, v_ref, top_ref, sum_ref, mix_ref)
+    wait_copies(copies)
+    visit_blocks(used, q_ref, kv_ref, top_ref, sum_ref, mix_ref)
     split_result(out_refs, sum_ref, mix_ref)
 
 
@@ -289,33 +339,40 @@
     return [pl.BlockSpec((piece.shape[0], DH), lambda i: (0, query_at + i)) for piece in queries]
 
 
-def attention_call(kernel, name, slots, seq_count, operands, in_specs, head_count):
+def attention_call(kernel, name, slots, seq_count, operands, in_specs, head_count, width, into):
+    written = into[1] if into else 0
+    operands = list(operands) + list(into[0] if into else [])
+    aliases = {len(operands) - head_count + i: i for i in range(head_count)} if into else {}
+    in_specs = in_specs + ([pl.BlockSpec(memory_space=pltpu.HBM)] * head_count if into else [])
     most_blocks = -(-(seq_count - 1) * MOST // 3) * 3
     rows = TILE // head_count
     return pl.pallas_call(
         kernel,
         grid=(2 * slots,),
-        out_shape=[jax.ShapeDtypeStruct((rows, slots * PAIR), jnp.bfloat16)] * head_count,
+        out_shape=[jax.ShapeDtypeStruct((rows, width * PAIR), jnp.bfloat16)] * head_count,
         in_specs=in_specs,
-        out_specs=[pl.BlockSpec((rows, DH), lambda i: (0, i))] * head_count,
+        out_specs=[pl.BlockSpec((rows, DH), lambda i: (0, 2 * written + i))] * head_count,
         scratch_shapes=[
             pltpu.VMEM((TILE, DH), jnp.bfloat16),
-            pltpu.VMEM((most_blocks * BLOCK, DH), jnp.bfloat16),
-            pltpu.VMEM((most_blocks * BLOCK, DH), jnp.bfloat16),
+            pltpu.VMEM((2, most_blocks * BLOCK, 2 * DH), jnp.bfloat16),
             pltpu.VMEM((TILE, DH), jnp.float32),
             pltpu.VMEM((TILE, DH), jnp.float32),
             pltpu.VMEM((TILE, DH), jnp.float32),
+            pltpu.SemaphoreType.DMA((2, MOST * (seq_count - 1))),
         ],
+        input_output_aliases=aliases,
         compiler_params=pltpu.CompilerParams(vmem_limit_bytes=VMEM_LIMIT),
-        cost_estimate=BRIEF,
+        cost_estimate=LONG if name == "attend_far" else BRIEF,
         name=name,
     )(*operands)
 
 
-def attend(places, counts, tile_pairs, queries, query_at, blocks, first_pair, slots):
+def attend(
+    places, counts, tile_pairs, queries, query_at, blocks, first_pair, slots, width, into=None
+):
     head_count, seq_count = len(queries), len(blocks) + 1
     return attention_call(
-        functools.partial(attend_kernel, head_count, seq_count, first_pair),
+        functools.partial(attend_kernel, head_count, seq_count, first_pair, bool(into)),
         "attend",
         slots,
         seq_count,
@@ -323,8 +380,10 @@
         [smem_spec()] * 2
         + [tile_spec()]
         + query_specs(queries, query_at)
-        + [one_block(block.shape) for block in blocks],
+        + [pl.BlockSpec(memory_space=pltpu.HBM)] * len(blocks),
         head_count,
+        width,
+        into,
     )
 
 
@@ -354,8 +413,10 @@
         [smem_spec()] * 2
         + [state_spec()] * 3
         + query_specs(queries, query_at)
-        + [one_block(block.shape) for block in blocks],
+        + [pl.BlockSpec(memory_space=pltpu.HBM)] * len(blocks),
         head_count,
+        slots,
+        None,
     )
 
 
@@ -364,7 +425,7 @@
     local_pairs = HEADS // 2 // head_count
     for number, group in enumerate(groups):
         for step in range(head_count):
-            rank = lax.rem(place_ref[1] - step + head_count, head_count)
+            rank = behind(place_ref[1], step, head_count)
             for at, pair in enumerate(group):
                 column = place_ref[2 + rank * local_pairs + pair] * PAIR
                 out_ref[:, pl.ds(pl.multiple_of(column, PAIR), PAIR)] = refs[
@@ -438,69 +499,81 @@
 
     def returned(outs):
         return [outs[0]] + [
-            shifted(outs[head_count - step], "head", step) for step in range(1, head_count)
+            shifted(outs[backward(step, head_count)], "head", step) for step in range(1, head_count)
         ]
 
     def passed_on(picked):
-        return [shifted(picked[step - 1], "seq", step) for step in range(1, seq_count)]
+        return [turned(picked[step - 1], "seq", step) for step in range(1, seq_count)]
 
     pieces = [spread(sources[0])]
     lists, counts = after((block_lists, block_counts), sources[0])
     lists, counts = lists.reshape(-1), counts.reshape(-1)
-    wanted = [shifted(lists, "seq", (seq_count - step) % seq_count) for step in range(1, seq_count)]
+    wanted = [turned(lists, "seq", seq_count - step) for step in range(1, seq_count)]
 
     def pick(number, arrived, light):
         caps = [light if pair >= 3 else PAIR_MOST for pair in groups[number]]
         return pick_blocks(places, counts, wanted, arrived, groups[number][0], caps)
 
-    def whole(number, tile_pairs, blocks):
+    def whole(number, tile_pairs, blocks, width, into=None):
         source, at = query_from[number]
         group = groups[number]
         return attend(
-            places, counts, tile_pairs, pieces[source], at, blocks, group[0], len(group)
+            places,
+            counts,
+            tile_pairs,
+            pieces[source],
+            at,
+            blocks,
+            group[0],
+            len(group),
+            width,
+            into,
         )
 
     if len(groups) == 1:
         tile_pairs, picked = pick(0, pieces[0], PAIR_MOST)
-        return lay_out(places, [returned(whole(0, tile_pairs, passed_on(picked)))], groups)
+        return lay_out(places, [returned(whole(0, tile_pairs, passed_on(picked), 1))], groups)
 
     pieces.append(spread(after(sources[1], pieces[0], wanted, counts)))
     tile_pairs, picked = pick(0, pieces[0], PAIR_MOST)
     blocks = passed_on(picked)
-    light_most = after(jnp.max(after(light_most, sources[0])), pieces[1][1])
+    light_most = after(jnp.max(after(light_most, sources[0])), pieces[1][1:-1])
     for step in range(1, part_count):
-        light_most = jnp.maximum(light_most, shifted(light_most[None], "parts", step)[0])
+        light_most = jnp.maximum(light_most, turned(light_most[None], "parts", step)[0])
     first = (tile_pairs, blocks)
-    light_most, first, arrived, third = lax.optimization_barrier(
-        (light_most, first, pieces[1], sources[2])
-    )
-
-    def finish(light, first, arrived, third):
+    ready = pick(1, pieces[1], LIGHT_MOST)
+    light_most, first, arrived, ready, third = lax.optimization_barrier(
+        (light_most, first, pieces[1], ready, sources[2])
+    )
+
+    def finish(light, first, arrived, ready, third):
         pieces[1] = arrived
-        tile_pairs, picked = pick(1, arrived, light)
+        tile_pairs, picked = ready if light == LIGHT_MOST else pick(1, arrived, light)
         pieces[2:] = [spread(after(third, picked))]
         second = (tile_pairs, passed_on(picked))
-        outs = whole(0, *after(first, picked))
+        width = len(groups[0]) + len(groups[1])
+        outs = whole(0, *after(first, picked), width)
         arrived = after(pieces[2], outs, second[1])
         tile_pairs, picked = pick(2, arrived, light)
+        blocks = passed_on(picked)
+        into = (outs, len(groups[0]))
+        outs = whole(1, *after(second, picked), width, into)
         results = [returned(outs)]
-        blocks = passed_on(picked)
-        results.append(returned(whole(1, *after(second, picked))))
         source, at = query_from[2]
         state = attend_own(tile_pairs, pieces[source], at, 1)
-        state = after(state, results[0], results[1][0])
         outs = attend_far(places, counts, state, pieces[source], at, blocks, groups[2][0], 1)
         results.append(returned(outs))
-        return lay_out(places, results, groups)
+        return lay_out(places, results, [groups[0] + groups[1], groups[2]])
 
     if max(max(group) for group in groups) < 3:
-        return finish(PAIR_MOST, first, arrived, third)
+        return finish(PAIR_MOST, first, arrived, ready, third)
     return lax.cond(
         light_most > LIGHT_MOST,
         functools.partial(finish, PAIR_MOST),
         functools.partial(finish, LIGHT_MOST),
         first,
         arrived,
+        ready,
         third,
     )
 

time: 134 us -> 125 us (0.933)
  waiting for transfers between devices: 38.8 us -> 35.7 us
  Pallas kernels: 49.6 us -> 46.8 us
  starting transfers between devices: 34.2 us -> 31.7 us
    ppermute x31 -> x28, waiting for transfers between devices: 38.8 us -> 35.7 us  [the longest x13 18.1 us: turned(): lax.ppermute(array, axis, [(i, (i + step) % size) for i in range(size)])]
    ppermute x31 -> x28, starting transfers between devices: 34.2 us -> 31.7 us  [the longest x15 16.5 us: shifted(): lax.ppermute(array, axis, [(i, ahead(i, step, size)) for i in range(size)])]
    pallas_call x3, Pallas kernels: 25.8 us -> 23.8 us  [attention_call(): pl.pallas_call(kernel, grid=(2 * slots,), out_shape=[jax.ShapeDtypeStruct...]
    cond x42 -> x24, local copies, waits for them, and re-layouts: 3.1 us -> 3.18 us
  transfers between devices with their start and end apart: 31 -> 28, of which waited for: 12 -> 11; matrix products, arithmetic and copies ran while one was open for 1% -> 1% of each run, Pallas kernels for 30% -> 32%
where the time goes in v4:
time: 125 us; the launch traced here: 124 us
  Pallas kernels  46.8 us (37%)
  waiting for transfers between devices  35.7 us (29%)
  starting transfers between devices  31.7 us (25%)
  local copies, waits for them, and re-layouts  5.78 us (5%)
  other arithmetic  2.15 us (2%)
  between operations  1.51 us (1%)
    pallas_call x3, Pallas kernels, attention_call(): pl.pallas_call(kernel, grid=(2 * slots,), out_shape=[jax.ShapeDtypeStruct...  23.8 us
    ppermute x13, waiting for transfers between devices, turned(): lax.ppermute(array, axis, [(i, (i + step) % size) for i in range(size)])  18.1 us
    ppermute x15, waiting for transfers between devices, shifted(): lax.ppermute(array, axis, [(i, ahead(i, step, size)) for i in range(size)])  17.6 us
    ppermute x15, starting transfers between devices, shifted(): lax.ppermute(array, axis, [(i, ahead(i, step, size)) for i in range(size)])  16.5 us
    ppermute x13, starting transfers between devices, turned(): lax.ppermute(array, axis, [(i, (i + step) % size) for i in range(size)])  15.2 us
    pallas_call x3, Pallas kernels, gather_columns(): pl.pallas_call(functools.partial(gather_kernel, head_count), grid_spec=pl...  9.26 us
    pallas_call x3, Pallas kernels, pick_blocks(): pl.pallas_call(functools.partial(pick_kernel, head_count, seq_count, firs...  8.06 us
    pallas_call x1, Pallas kernels, attend_own(): pl.pallas_call(functools.partial(own_kernel, head_count), grid=(2 * slots...  4.16 us
  transfers between devices with their start and end apart: 28, of which 11 were waited for; matrix products, arithmetic and copies ran while one was open for 1% of the time, Pallas kernels for 32%

profile of v4, /device:TPU:13, one launch (start us, length us, event | category | flops | bytes accessed | tf_op | source)
XLA Modules:
  0.0 124.0 jit_solution(11130440473608654579)
XLA Ops:
  0.0 0.8 copy.22
  0.8 0.7 reduce_sum.43
  2.3 2.7 %gather_columns.3 = (bf16[192,512]{1,0:T(8,128)(2,1)}, bf16[192,512]{1,0:T(8,128)(2,1)}, bf16[192,512]{1,0:T(8,128)(2,1)}, bf16[192,512]{1,0:T(8,128)(2,1)}) custom-call(s32[18]{0:T(128)S(1)} %pad_add_fusion.place_ref, bf16[192,4096]{1,0:T(8,128)(2,1)} %refs_15_.3, bf16[192,4096]{1,0:T(8,128)(2,1)} %refs_16_.3, bf16[192,4096]{1,0:T(8,128)(2,1)} %refs_15_.3, ...), custom_call_target="tpu_custom_call" | custom-call | flops 1024 | bytes 1024 | tf_op jit(solution)/shard_map/gather_columns/pallas_call | solution.py:78
  5.0 0.7 collective-permute-start.30
  5.7 1.2 collective-permute-start.31
  7.7 1.3 %collective-permute-start.35 = (s32[384]{0:T(512)S(1)}, s32[384]{0:T(512)S(1)}, u32[]{:S(2)}, u32[]{:S(2)}) collective-permute-start(s32[384]{0:T(512)S(1)} %reshape.43), channel_id=1, source_target_pairs={{0,4},{4,8},{8,12},{12,0},{1,5},{5,9},{9,13},{13,1},{2,6},{6,10},{... | collective-permute-start | bytes 4616 | tf_op jit(solution)/shard_map/ppermute | solution.py:48
  9.0 1.1 collective-permute-start.34
  10.5 1.7 %collective-permute-start.33 = (s32[384]{0:T(512)S(1)}, s32[384]{0:T(512)S(1)}, u32[]{:S(2)}, u32[]{:S(2)}) collective-permute-start(s32[384]{0:T(512)S(1)} %reshape.43), channel_id=1, source_target_pairs={{0,12},{4,0},{8,4},{12,8},{1,13},{5,1},{9,5},{13,9},{2,14},{6,2},{... | collective-permute-start | bytes 4616 | tf_op jit(solution)/shard_map/ppermute | solution.py:48
  12.2 3.3 %gather_columns.4 = (bf16[192,1280]{1,0:T(8,128)(2,1)S(1)}, bf16[192,1280]{1,0:T(8,128)(2,1)}, bf16[192,1280]{1,0:T(8,128)(2,1)}, bf16[192,1280]{1,0:T(8,128)(2,1)}) custom-call(s32[18]{0:T(128)S(1)} %pad_add_fusion.place_ref, bf16[192,4096]{1,0:T(8,128)(2,1)} %refs_15_.3, bf16[192,4096]{1,0:T(8,128)(2,1)} %refs_16_.3, bf16[192,4096]{1,0:T(8,128)(2,1)} %refs_15_.3, ...), custom_call_target="tpu_custom_call" | custom-call | flops 1024 | bytes 1024 | tf_op jit(solution)/shard_map/gather_columns/pallas_call | solution.py:78
  15.8 0.9 collective-permute-done.32.refs_6_
  16.7 0.7 collective-permute-start.36
  17.5 1.2 collective-permute-start.37
  19.2 2.8 %pick_blocks.8 = (bf16[2,768,256]{2,1,0:T(8,128)(2,1)}, bf16[4,128,256]{2,1,0:T(8,128)(2,1)}, bf16[4,128,256]{2,1,0:T(8,128)(2,1)}, bf16[4,128,256]{2,1,0:T(8,128)(2,1)}) custom-call(s32[18]{0:T(128)S(1)} %pad_add_fusion.place_ref, s32[512]{0:T(512)S(1)} %reshape.44.counts_ref, s32[384]{0:T(512)S(1)} %collective-permute-done.33.refs_0_, ...), custom_call_target="tpu_custom_call" | custom-call | flops 1024 | bytes 1024 | tf_op jit(solution)/shard_map/pick_blocks/pallas_call | solution.py:143
  22.0 1.0 collective-permute-start.39
  23.0 2.6 %collective-permute-start.40 = (bf16[4,128,256]{2,1,0:T(8,128)(2,1)}, bf16[4,128,256]{2,1,0:T(8,128)(2,1)S(1)}, u32[]{:S(2)}, u32[]{:S(2)}) collective-permute-start(bf16[4,128,256]{2,1,0:T(8,128)(2,1)} %get-tuple-element.257), channel_id=1, source_target_pairs={{0,8},{4,12},{8,0},{12,4},{1,9},{5,13},{9,1},{13,5},{2,10},{6,14},... | collective-permute-start | bytes 786440 | tf_op jit(solution)/shard_map/ppermute | solution.py:48
  25.6 3.3 %gather_columns.5 = (bf16[192,1280]{1,0:T(8,128)(2,1)S(1)}, bf16[192,1280]{1,0:T(8,128)(2,1)}, bf16[192,1280]{1,0:T(8,128)(2,1)}, bf16[192,1280]{1,0:T(8,128)(2,1)}) custom-call(s32[18]{0:T(128)S(1)} %pad_add_fusion.place_ref, bf16[192,4096]{1,0:T(8,128)(2,1)} %refs_15_.3, bf16[192,4096]{1,0:T(8,128)(2,1)} %refs_16_.3, bf16[192,4096]{1,0:T(8,128)(2,1)} %refs_19_.3, ...), custom_call_target="tpu_custom_call" | custom-call | flops 1024 | bytes 1024 | tf_op jit(solution)/shard_map/gather_columns/pallas_call | solution.py:78
  28.9 0.7 reduce_max.19
  29.6 0.9 collective-permute-done.37.refs_5_
  30.5 10.7 %collective-permute-done.42.refs_6_ = bf16[192,1280]{1,0:T(8,128)(2,1)S(1)} collective-permute-done((bf16[192,1280]{1,0:T(8,128)(2,1)}, bf16[192,1280]{1,0:T(8,128)(2,1)S(1)}, u32[]{:S(2)}, u32[]{:S(2)}) %collective-permute-start.42) | collective-permute-done | bytes 491552 | tf_op jit(solution)/shard_map/ppermute | solution.py:43
  41.2 2.7 %pick_blocks.9 = (bf16[4,768,256]{2,1,0:T(8,128)(2,1)}, bf16[5,128,256]{2,1,0:T(8,128)(2,1)}, bf16[5,128,256]{2,1,0:T(8,128)(2,1)}, bf16[5,128,256]{2,1,0:T(8,128)(2,1)}) custom-call(s32[18]{0:T(128)S(1)} %pad_add_fusion.place_ref, s32[512]{0:T(512)S(1)} %reshape.44.counts_ref, s32[384]{0:T(512)S(1)} %collective-permute-done.33.refs_0_, ...), custom_call_target="tpu_custom_call" | custom-call | flops 1024 | bytes 1024 | tf_op jit(solution)/shard_map/pick_blocks/pallas_call | solution.py:143
  45.2 0.6 collective-permute-done.40
  45.9 2.0 %collective-permute-done.41 = bf16[4,128,256]{2,1,0:T(8,128)(2,1)S(1)} collective-permute-done((bf16[4,128,256]{2,1,0:T(8,128)(2,1)}, bf16[4,128,256]{2,1,0:T(8,128)(2,1)S(1)}, u32[]{:S(2)}, u32[]{:S(2)}) %collective-permute-start.41) | collective-permute-done | bytes 262176 | tf_op jit(solution)/shard_map/ppermute | solution.py:48
  47.9 75.0 %conditional.1 = (bf16[192,4096]{1,0:T(8,128)(2,1)S(1)}) conditional(s32[]{:T(128)} %convert_element_type.7, (bf16[5,128,256]{2,1,0:T(8,128)(2,1)}, bf16[5,128,256]{2,1,0:T(8,128)(2,1)}, bf16[5,128,256]{2,1,0:T(8,128)(2,1)}, bf16[192,1280]{1,0:T(8,128)(2,1)S(1)}, bf16[192,1280]{1,0:T(8,128)(2,1)}, /*index=5*/bf16[192,1280]{1,0:T(8,128)(2,1)}, ...), branch_computations={%region_7.8_spmd, %region_8.9_spmd} | conditional | flops 199999995904 | bytes 2035395328 | solution.py:570
  47.9 0.7 copy-done.6
  48.8 1.2 collective-permute-start.3
  50.0 1.2 collective-permute-start.4
  52.2 4.0 %collective-permute-done.refs_4_ = bf16[5,128,256]{2,1,0:T(8,128)(2,1)} collective-permute-done((bf16[5,128,256]{2,1,0:T(8,128)(2,1)}, bf16[5,128,256]{2,1,0:T(8,128)(2,1)}, u32[]{:S(2)}, u32[]{:S(2)}) %collective-permute-start) | collective-permute-done | bytes 327712 | tf_op jit(solution)/shard_map/cond/branch_0_fun/ppermute | solution.py:48
  56.2 2.2 %collective-permute-start.2 = (bf16[5,128,256]{2,1,0:T(8,128)(2,1)}, bf16[5,128,256]{2,1,0:T(8,128)(2,1)}, u32[]{:S(2)}, u32[]{:S(2)}) collective-permute-start(bf16[5,128,256]{2,1,0:T(8,128)(2,1)} %get-tuple-element.89), channel_id=1, source_target_pairs={{0,12},{4,0},{8,4},{12,8},{1,13},{5,1},{9,5},{13,9},{2,14},{6,2},{... | collective-permute-start | bytes 983048 | tf_op jit(solution)/shard_map/cond/branch_0_fun/ppermute | solution.py:48
  58.5 7.1 %attend.4 = (bf16[192,768]{1,0:T(8,128)(2,1)}, bf16[192,768]{1,0:T(8,128)(2,1)}, bf16[192,768]{1,0:T(8,128)(2,1)}, bf16[192,768]{1,0:T(8,128)(2,1)}) custom-call(s32[18]{0:T(128)S(1)} %get-tuple-element.84.place_ref, s32[512]{0:T(512)S(1)} %get-tuple-element.85.counts_ref, bf16[2,768,256]{2,1,0:T(8,128)(2,1)} %get-tuple-element.105.tile_ref, ...), custom_call_target="tpu_custom_call" | custom-call | flops 1024 | bytes 1024 | tf_op jit(solution)/shard_map/cond/branch_0_fun/attend/pallas_call | solution.py:349
  65.6 9.8 %collective-permute-done.1.refs_5_ = bf16[5,128,256]{2,1,0:T(8,128)(2,1)} collective-permute-done((bf16[5,128,256]{2,1,0:T(8,128)(2,1)}, bf16[5,128,256]{2,1,0:T(8,128)(2,1)}, u32[]{:S(2)}, u32[]{:S(2)}) %collective-permute-start.1) | collective-permute-done | bytes 327712 | tf_op jit(solution)/shard_map/cond/branch_0_fun/ppermute | solution.py:48
  75.4 0.8 copy-done.2
  76.4 2.6 %pick_blocks.5 = (bf16[2,768,256]{2,1,0:T(8,128)(2,1)}, bf16[4,128,256]{2,1,0:T(8,128)(2,1)}, bf16[4,128,256]{2,1,0:T(8,128)(2,1)}, bf16[4,128,256]{2,1,0:T(8,128)(2,1)}) custom-call(s32[18]{0:T(128)S(1)} %get-tuple-element.84.place_ref, s32[512]{0:T(512)S(1)} %get-tuple-element.85.counts_ref, s32[384]{0:T(512)S(1)} %get-tuple-element.90.refs_0_, ...), custom_call_target="tpu_custom_call" | custom-call | flops 1024 | bytes 1024 | tf_op jit(solution)/shard_map/cond/branch_0_fun/pick_blocks/pallas_call | solution.py:143
  79.0 3.1 %collective-permute-start.10 = (bf16[4,128,256]{2,1,0:T(8,128)(2,1)}, bf16[4,128,256]{2,1,0:T(8,128)(2,1)S(1)}, u32[]{:S(2)}, u32[]{:S(2)}) collective-permute-start(bf16[4,128,256]{2,1,0:T(8,128)(2,1)} %get-tuple-element.122), channel_id=1, source_target_pairs={{0,8},{4,12},{8,0},{12,4},{1,9},{5,13},{9,1},{13,5},{2,10},{6,14},... | collective-permute-start | bytes 786440 | tf_op jit(solution)/shard_map/cond/branch_0_fun/ppermute | solution.py:48
  82.1 1.4 %collective-permute-start.11 = (bf16[4,128,256]{2,1,0:T(8,128)(2,1)}, bf16[4,128,256]{2,1,0:T(8,128)(2,1)S(1)}, u32[]{:S(2)}, u32[]{:S(2)}) collective-permute-start(bf16[4,128,256]{2,1,0:T(8,128)(2,1)} %get-tuple-element.123), channel_id=1, source_target_pairs={{0,12},{4,0},{8,4},{12,8},{1,13},{5,1},{9,5},{13,9},{2,14},{6,2},{... | collective-permute-start | bytes 786440 | tf_op jit(solution)/shard_map/cond/branch_0_fun/ppermute | solution.py:48
  83.6 10.4 %attend.5 = (bf16[192,768]{1,0:T(8,128)(2,1)}, bf16[192,768]{1,0:T(8,128)(2,1)}, bf16[192,768]{1,0:T(8,128)(2,1)}, bf16[192,768]{1,0:T(8,128)(2,1)}) custom-call(s32[18]{0:T(128)S(1)} %get-tuple-element.84.place_ref, s32[512]{0:T(512)S(1)} %get-tuple-element.85.counts_ref, ...), custom_call_target="tpu_custom_call", output_to_operand_aliasing={{0}: (10, {}), {1}: (11, {}), {2}: (12, {}), {3}: (13, {})} | custom-call | flops 1024 | bytes 1024 | tf_op jit(solution)/shard_map/cond/branch_0_fun/attend/pallas_call | solution.py:349
  94.0 4.9 %collective-permute-start.6 = (bf16[192,768]{1,0:T(8,128)(2,1)}, bf16[192,768]{1,0:T(8,128)(2,1)}, u32[]{:S(2)}, u32[]{:S(2)}) collective-permute-start(bf16[192,768]{1,0:T(8,128)(2,1)} %get-tuple-element.129), channel_id=1, source_target_pairs={{0,1},{1,0},{2,3},{3,2},{4,5},{5,4},{6,7},{7,6},{8,9},{9,8},{10,11... | collective-permute-start | bytes 884744 | tf_op jit(solution)/shard_map/cond/branch_0_fun/ppermute | solution.py:43
  98.8 4.2 %attend_own.2 = (f32[2,768,128]{2,1,0:T(8,128)}, f32[2,768,128]{2,1,0:T(8,128)}, f32[2,768,128]{2,1,0:T(8,128)}) custom-call(bf16[2,768,256]{2,1,0:T(8,128)(2,1)} %get-tuple-element.132.tile_ref, bf16[192,1280]{1,0:T(8,128)(2,1)S(1)} %get-tuple-element.117.refs_3_.refs_0_, bf16[192,1280]{1,0:T(8,128)(2,1)} %copy-done.2, bf16[192,1280]{1,0:T(8,128)(2,1)} %copy-done.3, ...), custom_call_target="tpu_custom_call" | custom-call | flops 1024 | bytes 1024 | tf_op jit(solution)/shard_map/cond/branch_0_fun/attend_own/pallas_call | solution.py:392
  103.0 1.8 %collective-permute-start.8 = (bf16[192,768]{1,0:T(8,128)(2,1)}, bf16[192,768]{1,0:T(8,128)(2,1)}, u32[]{:S(2)}, u32[]{:S(2)}) collective-permute-start(bf16[192,768]{1,0:T(8,128)(2,1)} %get-tuple-element.131), channel_id=1, source_target_pairs={{0,3},{1,2},{2,1},{3,0},{4,7},{5,6},{6,5},{7,4},{8,11},{9,10},{10,... | collective-permute-start | bytes 884744 | tf_op jit(solution)/shard_map/cond/branch_0_fun/ppermute | solution.py:43
  104.8 1.3 %collective-permute-done.11.refs_9_ = bf16[4,128,256]{2,1,0:T(8,128)(2,1)S(1)} collective-permute-done((bf16[4,128,256]{2,1,0:T(8,128)(2,1)}, bf16[4,128,256]{2,1,0:T(8,128)(2,1)S(1)}, u32[]{:S(2)}, u32[]{:S(2)}) %collective-permute-start.11) | collective-permute-done | bytes 262176 | tf_op jit(solution)/shard_map/cond/branch_0_fun/ppermute | solution.py:48
  106.1 0.7 copy-done.28
  106.8 6.3 %attend_far.2 = (bf16[192,256]{1,0:T(8,128)(2,1)}, bf16[192,256]{1,0:T(8,128)(2,1)}, bf16[192,256]{1,0:T(8,128)(2,1)}, bf16[192,256]{1,0:T(8,128)(2,1)}) custom-call(s32[18]{0:T(128)S(1)} %get-tuple-element.84.place_ref, s32[512]{0:T(512)S(1)} %get-tuple-element.85.counts_ref, f32[2,768,128]{2,1,0:T(8,128)} %get-tuple-element.133.refs_0_, ...), custom_call_target="tpu_custom_call" | custom-call | flops 199999995904 | bytes 2000000000 | tf_op jit(solution)/shard_map/cond/branch_0_fun/attend_far/pallas_call | solution.py:349
  113.6 1.1 collective-permute-start.13
  114.7 0.6 collective-permute-start.14
  115.3 2.8 %collective-permute-done.13.refs_6_ = bf16[192,256]{1,0:T(8,128)(2,1)S(1)} collective-permute-done((bf16[192,256]{1,0:T(8,128)(2,1)}, bf16[192,256]{1,0:T(8,128)(2,1)S(1)}, u32[]{:S(2)}, u32[]{:S(2)}) %collective-permute-start.13) | collective-permute-done | bytes 98336 | tf_op jit(solution)/shard_map/cond/branch_0_fun/ppermute | solution.py:43
  118.2 2.3 %collective-permute-done.14.refs_7_ = bf16[192,256]{1,0:T(8,128)(2,1)S(1)} collective-permute-done((bf16[192,256]{1,0:T(8,128)(2,1)}, bf16[192,256]{1,0:T(8,128)(2,1)S(1)}, u32[]{:S(2)}, u32[]{:S(2)}) %collective-permute-start.14) | collective-permute-done | bytes 98336 | tf_op jit(solution)/shard_map/cond/branch_0_fun/ppermute | solution.py:43
  120.5 0.6 copy-done.19
  121.1 1.5 %lay_out.2 = bf16[192,4096]{1,0:T(8,128)(2,1)S(1)} custom-call(s32[18]{0:T(128)S(1)} %get-tuple-element.84.place_ref, bf16[192,768]{1,0:T(8,128)(2,1)} %get-tuple-element.128.refs_0_, bf16[192,768]{1,0:T(8,128)(2,1)} %collective-permute-done.6.refs_1_, bf16[192,768]{1,0:T(8,128)(2,1)} %collective-permute-done.7.refs_2_, ...), custom_call_target="tpu_custom_call" | custom-call | flops 1024 | bytes 1024 | tf_op jit(solution)/shard_map/cond/branch_0_fun/lay_out/pallas_call | solution.py:440
  122.9 1.1 copy-done.5
  (71 shorter events, 4.7 us)
Async XLA Ops:
  2.3 5.0 %copy-start.22 = (s32[32,1,4,3]{0,2,3,1:T(4,128)S(1)}, s32[32,1,4,3]{0,2,3,1:T(4,128)}, u32[]{:S(2)}) copy-start(s32[32,1,4,3]{0,2,3,1:T(4,128)} %param.10) | copy-start | bytes 4612
  5.0 10.8 %collective-permute-start.30 = (bf16[192,512]{1,0:T(8,128)(2,1)}, bf16[192,512]{1,0:T(8,128)(2,1)S(1)}, u32[]{:S(2)}, u32[]{:S(2)}) collective-permute-start(bf16[192,512]{1,0:T(8,128)(2,1)} %get-tuple-element.242), channel_id=1, source_target_pairs={{0,1},{1,0},{2,3},{3,2},{4,5},{5,4},{6,7},{7,6},{8,9},{9,8},{10,11... | collective-permute-start | bytes 589832 | tf_op jit(solution)/shard_map/ppermute | solution.py:43
  5.7 10.1 %collective-permute-start.31 = (bf16[192,512]{1,0:T(8,128)(2,1)}, bf16[192,512]{1,0:T(8,128)(2,1)S(1)}, u32[]{:S(2)}, u32[]{:S(2)}) collective-permute-start(bf16[192,512]{1,0:T(8,128)(2,1)} %get-tuple-element.243), channel_id=1, source_target_pairs={{0,2},{1,3},{2,0},{3,1},{4,6},{5,7},{6,4},{7,5},{8,10},{9,11},{10,... | collective-permute-start | bytes 589832 | tf_op jit(solution)/shard_map/ppermute | solution.py:43
  6.9 9.8 %collective-permute-start.32 = (bf16[192,512]{1,0:T(8,128)(2,1)}, bf16[192,512]{1,0:T(8,128)(2,1)S(1)}, u32[]{:S(2)}, u32[]{:S(2)}) collective-permute-start(bf16[192,512]{1,0:T(8,128)(2,1)} %get-tuple-element.244), channel_id=1, source_target_pairs={{0,3},{1,2},{2,1},{3,0},{4,7},{5,6},{6,5},{7,4},{8,11},{9,10},{10,... | collective-permute-start | bytes 589832 | tf_op jit(solution)/shard_map/ppermute | solution.py:43
  7.7 7.8 %copy-start.21 = (s32[32,4,4]{0,2,1:T(4,128)S(1)}, s32[32,4,4]{0,2,1:T(4,128)}, u32[]{:S(2)}) copy-start(s32[32,4,4]{0,2,1:T(4,128)} %param.11) | copy-start | bytes 6148
  7.7 2.8 %collective-permute-start.35 = (s32[384]{0:T(512)S(1)}, s32[384]{0:T(512)S(1)}, u32[]{:S(2)}, u32[]{:S(2)}) collective-permute-start(s32[384]{0:T(512)S(1)} %reshape.43), channel_id=1, source_target_pairs={{0,4},{4,8},{8,12},{12,0},{1,5},{5,9},{9,13},{13,1},{2,6},{6,10},{... | collective-permute-start | bytes 4616 | tf_op jit(solution)/shard_map/ppermute | solution.py:48
  9.0 6.7 %collective-permute-start.34 = (s32[384]{0:T(512)S(1)}, s32[384]{0:T(512)S(1)}, u32[]{:S(2)}, u32[]{:S(2)}) collective-permute-start(s32[384]{0:T(512)S(1)} %reshape.43), channel_id=1, source_target_pairs={{0,8},{4,12},{8,0},{12,4},{1,9},{5,13},{9,1},{13,5},{2,10},{6,14},... | collective-permute-start | bytes 4616 | tf_op jit(solution)/shard_map/ppermute | solution.py:48
  10.5 5.3 %collective-permute-start.33 = (s32[384]{0:T(512)S(1)}, s32[384]{0:T(512)S(1)}, u32[]{:S(2)}, u32[]{:S(2)}) collective-permute-start(s32[384]{0:T(512)S(1)} %reshape.43), channel_id=1, source_target_pairs={{0,12},{4,0},{8,4},{12,8},{1,13},{5,1},{9,5},{13,9},{2,14},{6,2},{... | collective-permute-start | bytes 4616 | tf_op jit(solution)/shard_map/ppermute | solution.py:48
  15.8 3.4 %copy-start.12 = (bf16[192,512]{1,0:T(8,128)(2,1)}, bf16[192,512]{1,0:T(8,128)(2,1)S(1)}, u32[]{:S(2)}) copy-start(bf16[192,512]{1,0:T(8,128)(2,1)S(1)} %collective-permute-done.30.refs_4_) | copy-start | bytes 589828
  15.8 3.4 %copy-start.13 = (bf16[192,512]{1,0:T(8,128)(2,1)}, bf16[192,512]{1,0:T(8,128)(2,1)S(1)}, u32[]{:S(2)}) copy-start(bf16[192,512]{1,0:T(8,128)(2,1)S(1)} %collective-permute-done.31.refs_5_) | copy-start | bytes 589828
  16.7 2.5 %copy-start.14 = (bf16[192,512]{1,0:T(8,128)(2,1)}, bf16[192,512]{1,0:T(8,128)(2,1)S(1)}, u32[]{:S(2)}) copy-start(bf16[192,512]{1,0:T(8,128)(2,1)S(1)} %collective-permute-done.32.refs_6_) | copy-start | bytes 589828
  16.7 8.8 %collective-permute-start.36 = (bf16[192,1280]{1,0:T(8,128)(2,1)}, bf16[192,1280]{1,0:T(8,128)(2,1)S(1)}, u32[]{:S(2)}, u32[]{:S(2)}) collective-permute-start(bf16[192,1280]{1,0:T(8,128)(2,1)} %get-tuple-element.252), channel_id=1, source_target_pairs={{0,1},{1,0},{2,3},{3,2},{4,5},{5,4},{6,7},{7,6},{8,9},{9,8},{10,11... | collective-permute-start | bytes 1474568 | tf_op jit(solution)/shard_map/ppermute | solution.py:43
  17.5 13.0 %collective-permute-start.37 = (bf16[192,1280]{1,0:T(8,128)(2,1)}, bf16[192,1280]{1,0:T(8,128)(2,1)S(1)}, u32[]{:S(2)}, u32[]{:S(2)}) collective-permute-start(bf16[192,1280]{1,0:T(8,128)(2,1)} %get-tuple-element.253), channel_id=1, source_target_pairs={{0,2},{1,3},{2,0},{3,1},{4,6},{5,7},{6,4},{7,5},{8,10},{9,11},{10,... | collective-permute-start | bytes 1474568 | tf_op jit(solution)/shard_map/ppermute | solution.py:43
  18.7 22.5 %collective-permute-start.42 = (bf16[192,1280]{1,0:T(8,128)(2,1)}, bf16[192,1280]{1,0:T(8,128)(2,1)S(1)}, u32[]{:S(2)}, u32[]{:S(2)}) collective-permute-start(bf16[192,1280]{1,0:T(8,128)(2,1)} %get-tuple-element.260), channel_id=1, source_target_pairs={{0,3},{1,2},{2,1},{3,0},{4,7},{5,6},{6,5},{7,4},{8,11},{9,10},{10,... | collective-permute-start | bytes 1474568 | tf_op jit(solution)/shard_map/ppermute | solution.py:43
  22.0 23.3 %collective-permute-start.39 = (bf16[4,128,256]{2,1,0:T(8,128)(2,1)}, bf16[4,128,256]{2,1,0:T(8,128)(2,1)S(1)}, u32[]{:S(2)}, u32[]{:S(2)}) collective-permute-start(bf16[4,128,256]{2,1,0:T(8,128)(2,1)} %get-tuple-element.256), channel_id=1, source_target_pairs={{0,4},{4,8},{8,12},{12,0},{1,5},{5,9},{9,13},{13,1},{2,6},{6,10},{... | collective-permute-start | bytes 786440 | tf_op jit(solution)/shard_map/ppermute | solution.py:48
  23.0 22.9 %collective-permute-start.40 = (bf16[4,128,256]{2,1,0:T(8,128)(2,1)}, bf16[4,128,256]{2,1,0:T(8,128)(2,1)S(1)}, u32[]{:S(2)}, u32[]{:S(2)}) collective-permute-start(bf16[4,128,256]{2,1,0:T(8,128)(2,1)} %get-tuple-element.257), channel_id=1, source_target_pairs={{0,8},{4,12},{8,0},{12,4},{1,9},{5,13},{9,1},{13,5},{2,10},{6,14},... | collective-permute-start | bytes 786440 | tf_op jit(solution)/shard_map/ppermute | solution.py:48
  25.6 22.3 %collective-permute-start.41 = (bf16[4,128,256]{2,1,0:T(8,128)(2,1)}, bf16[4,128,256]{2,1,0:T(8,128)(2,1)S(1)}, u32[]{:S(2)}, u32[]{:S(2)}) collective-permute-start(bf16[4,128,256]{2,1,0:T(8,128)(2,1)} %get-tuple-element.258), channel_id=1, source_target_pairs={{0,12},{4,0},{8,4},{12,8},{1,13},{5,1},{9,5},{13,9},{2,14},{6,2},{... | collective-permute-start | bytes 786440 | tf_op jit(solution)/shard_map/ppermute | solution.py:48
  30.5 13.4 %collective-permute-start.38 = (s32[1]{0:T(128)}, s32[1]{0:T(128)}, u32[]{:S(2)}, u32[]{:S(2)}) collective-permute-start(s32[1]{0:T(128)} %bitcast.3), channel_id=1, source_target_pairs={{0,16},{16,0},{1,17},{17,1},{2,18},{18,2},{3,19},{19,3},{4,20},{20... | collective-permute-start | bytes 20 | tf_op jit(solution)/shard_map/ppermute | solution.py:48
  47.9 0.7 copy-start.6
  47.9 0.8 copy-start.8
  47.9 0.9 copy-start.10
  47.9 8.3 %collective-permute-start = (bf16[5,128,256]{2,1,0:T(8,128)(2,1)}, bf16[5,128,256]{2,1,0:T(8,128)(2,1)}, u32[]{:S(2)}, u32[]{:S(2)}) collective-permute-start(bf16[5,128,256]{2,1,0:T(8,128)(2,1)} %get-tuple-element.87), channel_id=1, source_target_pairs={{0,4},{4,8},{8,12},{12,0},{1,5},{5,9},{9,13},{13,1},{2,6},{6,10},{... | collective-permute-start | bytes 983048 | tf_op jit(solution)/shard_map/cond/branch_0_fun/ppermute | solution.py:48
  48.8 26.6 %collective-permute-start.3 = (bf16[192,1280]{1,0:T(8,128)(2,1)}, bf16[192,1280]{1,0:T(8,128)(2,1)S(1)}, u32[]{:S(2)}, u32[]{:S(2)}) collective-permute-start(bf16[192,1280]{1,0:T(8,128)(2,1)} %get-tuple-element.98), channel_id=1, source_target_pairs={{0,1},{1,0},{2,3},{3,2},{4,5},{5,4},{6,7},{7,6},{8,9},{9,8},{10,11... | collective-permute-start | bytes 1474568 | tf_op jit(solution)/shard_map/cond/branch_0_fun/ppermute | solution.py:43
  50.0 25.4 %collective-permute-start.4 = (bf16[192,1280]{1,0:T(8,128)(2,1)}, bf16[192,1280]{1,0:T(8,128)(2,1)S(1)}, u32[]{:S(2)}, u32[]{:S(2)}) collective-permute-start(bf16[192,1280]{1,0:T(8,128)(2,1)} %get-tuple-element.99), channel_id=1, source_target_pairs={{0,2},{1,3},{2,0},{3,1},{4,6},{5,7},{6,4},{7,5},{8,10},{9,11},{10,... | collective-permute-start | bytes 1474568 | tf_op jit(solution)/shard_map/cond/branch_0_fun/ppermute | solution.py:43
  51.2 24.2 %collective-permute-start.5 = (bf16[192,1280]{1,0:T(8,128)(2,1)}, bf16[192,1280]{1,0:T(8,128)(2,1)}, u32[]{:S(2)}, u32[]{:S(2)}) collective-permute-start(bf16[192,1280]{1,0:T(8,128)(2,1)} %get-tuple-element.100), channel_id=1, source_target_pairs={{0,3},{1,2},{2,1},{3,0},{4,7},{5,6},{6,5},{7,4},{8,11},{9,10},{10,... | collective-permute-start | bytes 1474568 | tf_op jit(solution)/shard_map/cond/branch_0_fun/ppermute | solution.py:43
  51.6 23.8 %collective-permute-start.1 = (bf16[5,128,256]{2,1,0:T(8,128)(2,1)}, bf16[5,128,256]{2,1,0:T(8,128)(2,1)}, u32[]{:S(2)}, u32[]{:S(2)}) collective-permute-start(bf16[5,128,256]{2,1,0:T(8,128)(2,1)} %get-tuple-element.88), channel_id=1, source_target_pairs={{0,8},{4,12},{8,0},{12,4},{1,9},{5,13},{9,1},{13,5},{2,10},{6,14},... | collective-permute-start | bytes 983048 | tf_op jit(solution)/shard_map/cond/branch_0_fun/ppermute | solution.py:48
  56.2 19.2 %collective-permute-start.2 = (bf16[5,128,256]{2,1,0:T(8,128)(2,1)}, bf16[5,128,256]{2,1,0:T(8,128)(2,1)}, u32[]{:S(2)}, u32[]{:S(2)}) collective-permute-start(bf16[5,128,256]{2,1,0:T(8,128)(2,1)} %get-tuple-element.89), channel_id=1, source_target_pairs={{0,12},{4,0},{8,4},{12,8},{1,13},{5,1},{9,5},{13,9},{2,14},{6,2},{... | collective-permute-start | bytes 983048 | tf_op jit(solution)/shard_map/cond/branch_0_fun/ppermute | solution.py:48
  65.6 18.0 %copy-start.4 = (bf16[4,768,256]{2,1,0:T(8,128)(2,1)S(1)}, bf16[4,768,256]{2,1,0:T(8,128)(2,1)}, u32[]{:S(2)}) copy-start(bf16[4,768,256]{2,1,0:T(8,128)(2,1)} %get-tuple-element.124.tile_ref) | copy-start | bytes 4718596 | tf_op jit(solution)/shard_map/cond
  75.4 0.8 copy-start.2
  75.4 1.0 copy-start.3
  79.0 24.0 %collective-permute-start.9 = (bf16[4,128,256]{2,1,0:T(8,128)(2,1)}, bf16[4,128,256]{2,1,0:T(8,128)(2,1)S(1)}, u32[]{:S(2)}, u32[]{:S(2)}) collective-permute-start(bf16[4,128,256]{2,1,0:T(8,128)(2,1)} %get-tuple-element.121), channel_id=1, source_target_pairs={{0,4},{4,8},{8,12},{12,0},{1,5},{5,9},{9,13},{13,1},{2,6},{6,10},{... | collective-permute-start | bytes 786440 | tf_op jit(solution)/shard_map/cond/branch_0_fun/ppermute | solution.py:48
  79.0 25.8 %collective-permute-start.10 = (bf16[4,128,256]{2,1,0:T(8,128)(2,1)}, bf16[4,128,256]{2,1,0:T(8,128)(2,1)S(1)}, u32[]{:S(2)}, u32[]{:S(2)}) collective-permute-start(bf16[4,128,256]{2,1,0:T(8,128)(2,1)} %get-tuple-element.122), channel_id=1, source_target_pairs={{0,8},{4,12},{8,0},{12,4},{1,9},{5,13},{9,1},{13,5},{2,10},{6,14},... | collective-permute-start | bytes 786440 | tf_op jit(solution)/shard_map/cond/branch_0_fun/ppermute | solution.py:48
  82.1 23.9 %collective-permute-start.11 = (bf16[4,128,256]{2,1,0:T(8,128)(2,1)}, bf16[4,128,256]{2,1,0:T(8,128)(2,1)S(1)}, u32[]{:S(2)}, u32[]{:S(2)}) collective-permute-start(bf16[4,128,256]{2,1,0:T(8,128)(2,1)} %get-tuple-element.123), channel_id=1, source_target_pairs={{0,12},{4,0},{8,4},{12,8},{1,13},{5,1},{9,5},{13,9},{2,14},{6,2},{... | collective-permute-start | bytes 786440 | tf_op jit(solution)/shard_map/cond/branch_0_fun/ppermute | solution.py:48
  94.0 20.8 %collective-permute-start.6 = (bf16[192,768]{1,0:T(8,128)(2,1)}, bf16[192,768]{1,0:T(8,128)(2,1)}, u32[]{:S(2)}, u32[]{:S(2)}) collective-permute-start(bf16[192,768]{1,0:T(8,128)(2,1)} %get-tuple-element.129), channel_id=1, source_target_pairs={{0,1},{1,0},{2,3},{3,2},{4,5},{5,4},{6,7},{7,6},{8,9},{9,8},{10,11... | collective-permute-start | bytes 884744 | tf_op jit(solution)/shard_map/cond/branch_0_fun/ppermute | solution.py:43
  98.8 16.5 %collective-permute-start.7 = (bf16[192,768]{1,0:T(8,128)(2,1)}, bf16[192,768]{1,0:T(8,128)(2,1)}, u32[]{:S(2)}, u32[]{:S(2)}) collective-permute-start(bf16[192,768]{1,0:T(8,128)(2,1)} %get-tuple-element.130), channel_id=1, source_target_pairs={{0,2},{1,3},{2,0},{3,1},{4,6},{5,7},{6,4},{7,5},{8,10},{9,11},{10,... | collective-permute-start | bytes 884744 | tf_op jit(solution)/shard_map/cond/branch_0_fun/ppermute | solution.py:43
  103.0 3.1 %copy-start.24 = (bf16[4,128,256]{2,1,0:T(8,128)(2,1)}, bf16[4,128,256]{2,1,0:T(8,128)(2,1)S(1)}, u32[]{:S(2)}) copy-start(bf16[4,128,256]{2,1,0:T(8,128)(2,1)S(1)} %collective-permute-done.9.refs_7_) | copy-start | bytes 786436 | tf_op jit(solution)/shard_map/cond
  103.0 12.3 %collective-permute-start.8 = (bf16[192,768]{1,0:T(8,128)(2,1)}, bf16[192,768]{1,0:T(8,128)(2,1)}, u32[]{:S(2)}, u32[]{:S(2)}) collective-permute-start(bf16[192,768]{1,0:T(8,128)(2,1)} %get-tuple-element.131), channel_id=1, source_target_pairs={{0,3},{1,2},{2,1},{3,0},{4,7},{5,6},{6,5},{7,4},{8,11},{9,10},{10,... | collective-permute-start | bytes 884744 | tf_op jit(solution)/shard_map/cond/branch_0_fun/ppermute | solution.py:43
  104.8 1.3 %copy-start.26 = (bf16[4,128,256]{2,1,0:T(8,128)(2,1)}, bf16[4,128,256]{2,1,0:T(8,128)(2,1)S(1)}, u32[]{:S(2)}) copy-start(bf16[4,128,256]{2,1,0:T(8,128)(2,1)S(1)} %collective-permute-done.10.refs_8_) | copy-start | bytes 786436 | tf_op jit(solution)/shard_map/cond
  106.1 0.7 copy-start.28
  113.0 2.3 %collective-permute-start.12 = (bf16[192,256]{1,0:T(8,128)(2,1)}, bf16[192,256]{1,0:T(8,128)(2,1)S(1)}, u32[]{:S(2)}, u32[]{:S(2)}) collective-permute-start(bf16[192,256]{1,0:T(8,128)(2,1)} %get-tuple-element.137), channel_id=1, source_target_pairs={{0,1},{1,0},{2,3},{3,2},{4,5},{5,4},{6,7},{7,6},{8,9},{9,8},{10,11... | collective-permute-start | bytes 294920 | tf_op jit(solution)/shard_map/cond/branch_0_fun/ppermute | solution.py:43
  113.6 4.6 %collective-permute-start.13 = (bf16[192,256]{1,0:T(8,128)(2,1)}, bf16[192,256]{1,0:T(8,128)(2,1)S(1)}, u32[]{:S(2)}, u32[]{:S(2)}) collective-permute-start(bf16[192,256]{1,0:T(8,128)(2,1)} %get-tuple-element.138), channel_id=1, source_target_pairs={{0,2},{1,3},{2,0},{3,1},{4,6},{5,7},{6,4},{7,5},{8,10},{9,11},{10,... | collective-permute-start | bytes 294920 | tf_op jit(solution)/shard_map/cond/branch_0_fun/ppermute | solution.py:43
  114.7 5.7 %collective-permute-start.14 = (bf16[192,256]{1,0:T(8,128)(2,1)}, bf16[192,256]{1,0:T(8,128)(2,1)S(1)}, u32[]{:S(2)}, u32[]{:S(2)}) collective-permute-start(bf16[192,256]{1,0:T(8,128)(2,1)} %get-tuple-element.139), channel_id=1, source_target_pairs={{0,3},{1,2},{2,1},{3,0},{4,7},{5,6},{6,5},{7,4},{8,11},{9,10},{10,... | collective-permute-start | bytes 294920 | tf_op jit(solution)/shard_map/cond/branch_0_fun/ppermute | solution.py:43
  115.3 5.1 %copy-start.15 = (bf16[192,256]{1,0:T(8,128)(2,1)}, bf16[192,256]{1,0:T(8,128)(2,1)S(1)}, u32[]{:S(2)}) copy-start(bf16[192,256]{1,0:T(8,128)(2,1)S(1)} %collective-permute-done.12.refs_5_) | copy-start | bytes 294916 | tf_op jit(solution)/shard_map/cond
  118.2 2.3 %copy-start.17 = (bf16[192,256]{1,0:T(8,128)(2,1)}, bf16[192,256]{1,0:T(8,128)(2,1)S(1)}, u32[]{:S(2)}) copy-start(bf16[192,256]{1,0:T(8,128)(2,1)S(1)} %collective-permute-done.13.refs_6_) | copy-start | bytes 294916 | tf_op jit(solution)/shard_map/cond
  120.5 0.6 copy-start.19
  122.9 1.1 copy-start.5

commit v5 on v4

--- a/solution.py
+++ b/solution.py
@@ -380,7 +380,7 @@
         [smem_spec()] * 2
         + [tile_spec()]
         + query_specs(queries, query_at)
-        + [pl.BlockSpec(memory_space=pltpu.HBM)] * len(blocks),
+        + [pl.BlockSpec(memory_space=pl.ANY)] * len(blocks),
         head_count,
         width,
         into,
@@ -413,7 +413,7 @@
         [smem_spec()] * 2
         + [state_spec()] * 3
         + query_specs(queries, query_at)
-        + [pl.BlockSpec(memory_space=pltpu.HBM)] * len(blocks),
+        + [pl.BlockSpec(memory_space=pl.ANY)] * len(blocks),
         head_count,
         slots,
         None,

time: 125 us -> 125 us (level)
  no operation moved by 1% of the time
where the time goes in v5:
time: 125 us; the launch traced here: 124 us
  Pallas kernels  46.9 us (38%)
  waiting for transfers between devices  35.7 us (29%)
  starting transfers between devices  31.7 us (25%)
  local copies, waits for them, and re-layouts  5.78 us (5%)
  other arithmetic  2.15 us (2%)
  between operations  1.51 us (1%)
    pallas_call x3, Pallas kernels, attention_call(): pl.pallas_call(kernel, grid=(2 * slots,), out_shape=[jax.ShapeDtypeStruct...  23.8 us
    ppermute x13, waiting for transfers between devices, turned(): lax.ppermute(array, axis, [(i, (i + step) % size) for i in range(size)])  18.1 us
    ppermute x15, waiting for transfers between devices, shifted(): lax.ppermute(array, axis, [(i, ahead(i, step, size)) for i in range(size)])  17.6 us
    ppermute x15, starting transfers between devices, shifted(): lax.ppermute(array, axis, [(i, ahead(i, step, size)) for i in range(size)])  16.5 us
    ppermute x13, starting transfers between devices, turned(): lax.ppermute(array, axis, [(i, (i + step) % size) for i in range(size)])  15.2 us
    pallas_call x3, Pallas kernels, gather_columns(): pl.pallas_call(functools.partial(gather_kernel, head_count), grid_spec=pl...  9.26 us
    pallas_call x3, Pallas kernels, pick_blocks(): pl.pallas_call(functools.partial(pick_kernel, head_count, seq_count, firs...  8.1 us
    pallas_call x1, Pallas kernels, attend_own(): pl.pallas_call(functools.partial(own_kernel, head_count), grid=(2 * slots...  4.16 us
  transfers between devices with their start and end apart: 28, of which 11 were waited for; matrix products, arithmetic and copies ran while one was open for 1% of the time, Pallas kernels for 32%

profile of v5, /device:TPU:13, one launch (start us, length us, event | category | flops | bytes accessed | tf_op | source)
XLA Modules:
  0.0 124.0 jit_solution(11130440473608654579)
XLA Ops:
  0.0 0.8 copy.22
  0.8 0.7 reduce_sum.43
  2.3 2.7 %gather_columns.3 = (bf16[192,512]{1,0:T(8,128)(2,1)}, bf16[192,512]{1,0:T(8,128)(2,1)}, bf16[192,512]{1,0:T(8,128)(2,1)}, bf16[192,512]{1,0:T(8,128)(2,1)}) custom-call(s32[18]{0:T(128)S(1)} %pad_add_fusion.place_ref, bf16[192,4096]{1,0:T(8,128)(2,1)} %refs_15_.3, bf16[192,4096]{1,0:T(8,128)(2,1)} %refs_16_.3, bf16[192,4096]{1,0:T(8,128)(2,1)} %refs_15_.3, ...), custom_call_target="tpu_custom_call" | custom-call | flops 1024 | bytes 1024 | tf_op jit(solution)/shard_map/gather_columns/pallas_call | solution.py:78
  5.0 0.7 collective-permute-start.30
  5.7 1.2 collective-permute-start.31
  7.7 1.3 %collective-permute-start.35 = (s32[384]{0:T(512)S(1)}, s32[384]{0:T(512)S(1)}, u32[]{:S(2)}, u32[]{:S(2)}) collective-permute-start(s32[384]{0:T(512)S(1)} %reshape.43), channel_id=1, source_target_pairs={{0,4},{4,8},{8,12},{12,0},{1,5},{5,9},{9,13},{13,1},{2,6},{6,10},{... | collective-permute-start | bytes 4616 | tf_op jit(solution)/shard_map/ppermute | solution.py:48
  9.0 1.1 collective-permute-start.34
  10.5 1.7 %collective-permute-start.33 = (s32[384]{0:T(512)S(1)}, s32[384]{0:T(512)S(1)}, u32[]{:S(2)}, u32[]{:S(2)}) collective-permute-start(s32[384]{0:T(512)S(1)} %reshape.43), channel_id=1, source_target_pairs={{0,12},{4,0},{8,4},{12,8},{1,13},{5,1},{9,5},{13,9},{2,14},{6,2},{... | collective-permute-start | bytes 4616 | tf_op jit(solution)/shard_map/ppermute | solution.py:48
  12.2 3.3 %gather_columns.4 = (bf16[192,1280]{1,0:T(8,128)(2,1)S(1)}, bf16[192,1280]{1,0:T(8,128)(2,1)}, bf16[192,1280]{1,0:T(8,128)(2,1)}, bf16[192,1280]{1,0:T(8,128)(2,1)}) custom-call(s32[18]{0:T(128)S(1)} %pad_add_fusion.place_ref, bf16[192,4096]{1,0:T(8,128)(2,1)} %refs_15_.3, bf16[192,4096]{1,0:T(8,128)(2,1)} %refs_16_.3, bf16[192,4096]{1,0:T(8,128)(2,1)} %refs_15_.3, ...), custom_call_target="tpu_custom_call" | custom-call | flops 1024 | bytes 1024 | tf_op jit(solution)/shard_map/gather_columns/pallas_call | solution.py:78
  15.8 0.9 collective-permute-done.32.refs_6_
  16.7 0.7 collective-permute-start.36
  17.5 1.2 collective-permute-start.37
  19.2 2.8 %pick_blocks.8 = (bf16[2,768,256]{2,1,0:T(8,128)(2,1)}, bf16[4,128,256]{2,1,0:T(8,128)(2,1)}, bf16[4,128,256]{2,1,0:T(8,128)(2,1)}, bf16[4,128,256]{2,1,0:T(8,128)(2,1)}) custom-call(s32[18]{0:T(128)S(1)} %pad_add_fusion.place_ref, s32[512]{0:T(512)S(1)} %reshape.44.counts_ref, s32[384]{0:T(512)S(1)} %collective-permute-done.33.refs_0_, ...), custom_call_target="tpu_custom_call" | custom-call | flops 1024 | bytes 1024 | tf_op jit(solution)/shard_map/pick_blocks/pallas_call | solution.py:143
  22.0 1.0 collective-permute-start.39
  23.0 2.6 %collective-permute-start.40 = (bf16[4,128,256]{2,1,0:T(8,128)(2,1)}, bf16[4,128,256]{2,1,0:T(8,128)(2,1)S(1)}, u32[]{:S(2)}, u32[]{:S(2)}) collective-permute-start(bf16[4,128,256]{2,1,0:T(8,128)(2,1)} %get-tuple-element.257), channel_id=1, source_target_pairs={{0,8},{4,12},{8,0},{12,4},{1,9},{5,13},{9,1},{13,5},{2,10},{6,14},... | collective-permute-start | bytes 786440 | tf_op jit(solution)/shard_map/ppermute | solution.py:48
  25.6 3.3 %gather_columns.5 = (bf16[192,1280]{1,0:T(8,128)(2,1)S(1)}, bf16[192,1280]{1,0:T(8,128)(2,1)}, bf16[192,1280]{1,0:T(8,128)(2,1)}, bf16[192,1280]{1,0:T(8,128)(2,1)}) custom-call(s32[18]{0:T(128)S(1)} %pad_add_fusion.place_ref, bf16[192,4096]{1,0:T(8,128)(2,1)} %refs_15_.3, bf16[192,4096]{1,0:T(8,128)(2,1)} %refs_16_.3, bf16[192,4096]{1,0:T(8,128)(2,1)} %refs_19_.3, ...), custom_call_target="tpu_custom_call" | custom-call | flops 1024 | bytes 1024 | tf_op jit(solution)/shard_map/gather_columns/pallas_call | solution.py:78
  28.9 0.7 reduce_max.19
  29.6 0.9 collective-permute-done.37.refs_5_
  30.5 10.7 %collective-permute-done.42.refs_6_ = bf16[192,1280]{1,0:T(8,128)(2,1)S(1)} collective-permute-done((bf16[192,1280]{1,0:T(8,128)(2,1)}, bf16[192,1280]{1,0:T(8,128)(2,1)S(1)}, u32[]{:S(2)}, u32[]{:S(2)}) %collective-permute-start.42) | collective-permute-done | bytes 491552 | tf_op jit(solution)/shard_map/ppermute | solution.py:43
  41.2 2.7 %pick_blocks.9 = (bf16[4,768,256]{2,1,0:T(8,128)(2,1)}, bf16[5,128,256]{2,1,0:T(8,128)(2,1)}, bf16[5,128,256]{2,1,0:T(8,128)(2,1)}, bf16[5,128,256]{2,1,0:T(8,128)(2,1)}) custom-call(s32[18]{0:T(128)S(1)} %pad_add_fusion.place_ref, s32[512]{0:T(512)S(1)} %reshape.44.counts_ref, s32[384]{0:T(512)S(1)} %collective-permute-done.33.refs_0_, ...), custom_call_target="tpu_custom_call" | custom-call | flops 1024 | bytes 1024 | tf_op jit(solution)/shard_map/pick_blocks/pallas_call | solution.py:143
  45.2 0.6 collective-permute-done.40
  45.9 2.0 %collective-permute-done.41 = bf16[4,128,256]{2,1,0:T(8,128)(2,1)S(1)} collective-permute-done((bf16[4,128,256]{2,1,0:T(8,128)(2,1)}, bf16[4,128,256]{2,1,0:T(8,128)(2,1)S(1)}, u32[]{:S(2)}, u32[]{:S(2)}) %collective-permute-start.41) | collective-permute-done | bytes 262176 | tf_op jit(solution)/shard_map/ppermute | solution.py:48
  47.9 75.0 %conditional.1 = (bf16[192,4096]{1,0:T(8,128)(2,1)S(1)}) conditional(s32[]{:T(128)} %convert_element_type.7, (bf16[5,128,256]{2,1,0:T(8,128)(2,1)}, bf16[5,128,256]{2,1,0:T(8,128)(2,1)}, bf16[5,128,256]{2,1,0:T(8,128)(2,1)}, bf16[192,1280]{1,0:T(8,128)(2,1)S(1)}, bf16[192,1280]{1,0:T(8,128)(2,1)}, /*index=5*/bf16[192,1280]{1,0:T(8,128)(2,1)}, ...), branch_computations={%region_7.8_spmd, %region_8.9_spmd} | conditional | flops 199999995904 | bytes 2035395328 | solution.py:570
  47.9 0.7 copy-done.6
  48.8 1.2 collective-permute-start.3
  50.0 1.2 collective-permute-start.4
  52.2 4.0 %collective-permute-done.refs_4_ = bf16[5,128,256]{2,1,0:T(8,128)(2,1)} collective-permute-done((bf16[5,128,256]{2,1,0:T(8,128)(2,1)}, bf16[5,128,256]{2,1,0:T(8,128)(2,1)}, u32[]{:S(2)}, u32[]{:S(2)}) %collective-permute-start) | collective-permute-done | bytes 327712 | tf_op jit(solution)/shard_map/cond/branch_0_fun/ppermute | solution.py:48
  56.2 2.3 %collective-permute-start.2 = (bf16[5,128,256]{2,1,0:T(8,128)(2,1)}, bf16[5,128,256]{2,1,0:T(8,128)(2,1)}, u32[]{:S(2)}, u32[]{:S(2)}) collective-permute-start(bf16[5,128,256]{2,1,0:T(8,128)(2,1)} %get-tuple-element.89), channel_id=1, source_target_pairs={{0,12},{4,0},{8,4},{12,8},{1,13},{5,1},{9,5},{13,9},{2,14},{6,2},{... | collective-permute-start | bytes 983048 | tf_op jit(solution)/shard_map/cond/branch_0_fun/ppermute | solution.py:48
  58.5 7.1 %attend.4 = (bf16[192,768]{1,0:T(8,128)(2,1)}, bf16[192,768]{1,0:T(8,128)(2,1)}, bf16[192,768]{1,0:T(8,128)(2,1)}, bf16[192,768]{1,0:T(8,128)(2,1)}) custom-call(s32[18]{0:T(128)S(1)} %get-tuple-element.84.place_ref, s32[512]{0:T(512)S(1)} %get-tuple-element.85.counts_ref, bf16[2,768,256]{2,1,0:T(8,128)(2,1)} %get-tuple-element.105.tile_ref, ...), custom_call_target="tpu_custom_call" | custom-call | flops 1024 | bytes 1024 | tf_op jit(solution)/shard_map/cond/branch_0_fun/attend/pallas_call | solution.py:349
  65.7 9.7 %collective-permute-done.1.refs_5_ = bf16[5,128,256]{2,1,0:T(8,128)(2,1)} collective-permute-done((bf16[5,128,256]{2,1,0:T(8,128)(2,1)}, bf16[5,128,256]{2,1,0:T(8,128)(2,1)}, u32[]{:S(2)}, u32[]{:S(2)}) %collective-permute-start.1) | collective-permute-done | bytes 327712 | tf_op jit(solution)/shard_map/cond/branch_0_fun/ppermute | solution.py:48
  75.4 0.8 copy-done.2
  76.4 2.7 %pick_blocks.5 = (bf16[2,768,256]{2,1,0:T(8,128)(2,1)}, bf16[4,128,256]{2,1,0:T(8,128)(2,1)}, bf16[4,128,256]{2,1,0:T(8,128)(2,1)}, bf16[4,128,256]{2,1,0:T(8,128)(2,1)}) custom-call(s32[18]{0:T(128)S(1)} %get-tuple-element.84.place_ref, s32[512]{0:T(512)S(1)} %get-tuple-element.85.counts_ref, s32[384]{0:T(512)S(1)} %get-tuple-element.90.refs_0_, ...), custom_call_target="tpu_custom_call" | custom-call | flops 1024 | bytes 1024 | tf_op jit(solution)/shard_map/cond/branch_0_fun/pick_blocks/pallas_call | solution.py:143
  79.0 3.1 %collective-permute-start.10 = (bf16[4,128,256]{2,1,0:T(8,128)(2,1)}, bf16[4,128,256]{2,1,0:T(8,128)(2,1)S(1)}, u32[]{:S(2)}, u32[]{:S(2)}) collective-permute-start(bf16[4,128,256]{2,1,0:T(8,128)(2,1)} %get-tuple-element.122), channel_id=1, source_target_pairs={{0,8},{4,12},{8,0},{12,4},{1,9},{5,13},{9,1},{13,5},{2,10},{6,14},... | collective-permute-start | bytes 786440 | tf_op jit(solution)/shard_map/cond/branch_0_fun/ppermute | solution.py:48
  82.2 1.4 %collective-permute-start.11 = (bf16[4,128,256]{2,1,0:T(8,128)(2,1)}, bf16[4,128,256]{2,1,0:T(8,128)(2,1)S(1)}, u32[]{:S(2)}, u32[]{:S(2)}) collective-permute-start(bf16[4,128,256]{2,1,0:T(8,128)(2,1)} %get-tuple-element.123), channel_id=1, source_target_pairs={{0,12},{4,0},{8,4},{12,8},{1,13},{5,1},{9,5},{13,9},{2,14},{6,2},{... | collective-permute-start | bytes 786440 | tf_op jit(solution)/shard_map/cond/branch_0_fun/ppermute | solution.py:48
  83.6 10.4 %attend.5 = (bf16[192,768]{1,0:T(8,128)(2,1)}, bf16[192,768]{1,0:T(8,128)(2,1)}, bf16[192,768]{1,0:T(8,128)(2,1)}, bf16[192,768]{1,0:T(8,128)(2,1)}) custom-call(s32[18]{0:T(128)S(1)} %get-tuple-element.84.place_ref, s32[512]{0:T(512)S(1)} %get-tuple-element.85.counts_ref, ...), custom_call_target="tpu_custom_call", output_to_operand_aliasing={{0}: (10, {}), {1}: (11, {}), {2}: (12, {}), {3}: (13, {})} | custom-call | flops 1024 | bytes 1024 | tf_op jit(solution)/shard_map/cond/branch_0_fun/attend/pallas_call | solution.py:349
  94.0 4.8 %collective-permute-start.6 = (bf16[192,768]{1,0:T(8,128)(2,1)}, bf16[192,768]{1,0:T(8,128)(2,1)}, u32[]{:S(2)}, u32[]{:S(2)}) collective-permute-start(bf16[192,768]{1,0:T(8,128)(2,1)} %get-tuple-element.129), channel_id=1, source_target_pairs={{0,1},{1,0},{2,3},{3,2},{4,5},{5,4},{6,7},{7,6},{8,9},{9,8},{10,11... | collective-permute-start | bytes 884744 | tf_op jit(solution)/shard_map/cond/branch_0_fun/ppermute | solution.py:43
  98.8 4.2 %attend_own.2 = (f32[2,768,128]{2,1,0:T(8,128)}, f32[2,768,128]{2,1,0:T(8,128)}, f32[2,768,128]{2,1,0:T(8,128)}) custom-call(bf16[2,768,256]{2,1,0:T(8,128)(2,1)} %get-tuple-element.132.tile_ref, bf16[192,1280]{1,0:T(8,128)(2,1)S(1)} %get-tuple-element.117.refs_3_.refs_0_, bf16[192,1280]{1,0:T(8,128)(2,1)} %copy-done.2, bf16[192,1280]{1,0:T(8,128)(2,1)} %copy-done.3, ...), custom_call_target="tpu_custom_call" | custom-call | flops 1024 | bytes 1024 | tf_op jit(solution)/shard_map/cond/branch_0_fun/attend_own/pallas_call | solution.py:392
  103.0 1.8 %collective-permute-start.8 = (bf16[192,768]{1,0:T(8,128)(2,1)}, bf16[192,768]{1,0:T(8,128)(2,1)}, u32[]{:S(2)}, u32[]{:S(2)}) collective-permute-start(bf16[192,768]{1,0:T(8,128)(2,1)} %get-tuple-element.131), channel_id=1, source_target_pairs={{0,3},{1,2},{2,1},{3,0},{4,7},{5,6},{6,5},{7,4},{8,11},{9,10},{10,... | collective-permute-start | bytes 884744 | tf_op jit(solution)/shard_map/cond/branch_0_fun/ppermute | solution.py:43
  104.8 1.3 %collective-permute-done.11.refs_9_ = bf16[4,128,256]{2,1,0:T(8,128)(2,1)S(1)} collective-permute-done((bf16[4,128,256]{2,1,0:T(8,128)(2,1)}, bf16[4,128,256]{2,1,0:T(8,128)(2,1)S(1)}, u32[]{:S(2)}, u32[]{:S(2)}) %collective-permute-start.11) | collective-permute-done | bytes 262176 | tf_op jit(solution)/shard_map/cond/branch_0_fun/ppermute | solution.py:48
  106.1 0.7 copy-done.28
  106.8 6.3 %attend_far.2 = (bf16[192,256]{1,0:T(8,128)(2,1)}, bf16[192,256]{1,0:T(8,128)(2,1)}, bf16[192,256]{1,0:T(8,128)(2,1)}, bf16[192,256]{1,0:T(8,128)(2,1)}) custom-call(s32[18]{0:T(128)S(1)} %get-tuple-element.84.place_ref, s32[512]{0:T(512)S(1)} %get-tuple-element.85.counts_ref, f32[2,768,128]{2,1,0:T(8,128)} %get-tuple-element.133.refs_0_, ...), custom_call_target="tpu_custom_call" | custom-call | flops 199999995904 | bytes 2000000000 | tf_op jit(solution)/shard_map/cond/branch_0_fun/attend_far/pallas_call | solution.py:349
  113.6 1.1 collective-permute-start.13
  114.7 0.6 collective-permute-start.14
  115.4 2.8 %collective-permute-done.13.refs_6_ = bf16[192,256]{1,0:T(8,128)(2,1)S(1)} collective-permute-done((bf16[192,256]{1,0:T(8,128)(2,1)}, bf16[192,256]{1,0:T(8,128)(2,1)S(1)}, u32[]{:S(2)}, u32[]{:S(2)}) %collective-permute-start.13) | collective-permute-done | bytes 98336 | tf_op jit(solution)/shard_map/cond/branch_0_fun/ppermute | solution.py:43
  118.2 2.3 %collective-permute-done.14.refs_7_ = bf16[192,256]{1,0:T(8,128)(2,1)S(1)} collective-permute-done((bf16[192,256]{1,0:T(8,128)(2,1)}, bf16[192,256]{1,0:T(8,128)(2,1)S(1)}, u32[]{:S(2)}, u32[]{:S(2)}) %collective-permute-start.14) | collective-permute-done | bytes 98336 | tf_op jit(solution)/shard_map/cond/branch_0_fun/ppermute | solution.py:43
  120.5 0.6 copy-done.19
  121.1 1.5 %lay_out.2 = bf16[192,4096]{1,0:T(8,128)(2,1)S(1)} custom-call(s32[18]{0:T(128)S(1)} %get-tuple-element.84.place_ref, bf16[192,768]{1,0:T(8,128)(2,1)} %get-tuple-element.128.refs_0_, bf16[192,768]{1,0:T(8,128)(2,1)} %collective-permute-done.6.refs_1_, bf16[192,768]{1,0:T(8,128)(2,1)} %collective-permute-done.7.refs_2_, ...), custom_call_target="tpu_custom_call" | custom-call | flops 1024 | bytes 1024 | tf_op jit(solution)/shard_map/cond/branch_0_fun/lay_out/pallas_call | solution.py:440
  122.9 1.1 copy-done.5
  (71 shorter events, 4.6 us)
Async XLA Ops:
  2.3 5.0 %copy-start.22 = (s32[32,1,4,3]{0,2,3,1:T(4,128)S(1)}, s32[32,1,4,3]{0,2,3,1:T(4,128)}, u32[]{:S(2)}) copy-start(s32[32,1,4,3]{0,2,3,1:T(4,128)} %param.10) | copy-start | bytes 4612
  5.0 10.8 %collective-permute-start.30 = (bf16[192,512]{1,0:T(8,128)(2,1)}, bf16[192,512]{1,0:T(8,128)(2,1)S(1)}, u32[]{:S(2)}, u32[]{:S(2)}) collective-permute-start(bf16[192,512]{1,0:T(8,128)(2,1)} %get-tuple-element.242), channel_id=1, source_target_pairs={{0,1},{1,0},{2,3},{3,2},{4,5},{5,4},{6,7},{7,6},{8,9},{9,8},{10,11... | collective-permute-start | bytes 589832 | tf_op jit(solution)/shard_map/ppermute | solution.py:43
  5.7 10.1 %collective-permute-start.31 = (bf16[192,512]{1,0:T(8,128)(2,1)}, bf16[192,512]{1,0:T(8,128)(2,1)S(1)}, u32[]{:S(2)}, u32[]{:S(2)}) collective-permute-start(bf16[192,512]{1,0:T(8,128)(2,1)} %get-tuple-element.243), channel_id=1, source_target_pairs={{0,2},{1,3},{2,0},{3,1},{4,6},{5,7},{6,4},{7,5},{8,10},{9,11},{10,... | collective-permute-start | bytes 589832 | tf_op jit(solution)/shard_map/ppermute | solution.py:43
  6.9 9.8 %collective-permute-start.32 = (bf16[192,512]{1,0:T(8,128)(2,1)}, bf16[192,512]{1,0:T(8,128)(2,1)S(1)}, u32[]{:S(2)}, u32[]{:S(2)}) collective-permute-start(bf16[192,512]{1,0:T(8,128)(2,1)} %get-tuple-element.244), channel_id=1, source_target_pairs={{0,3},{1,2},{2,1},{3,0},{4,7},{5,6},{6,5},{7,4},{8,11},{9,10},{10,... | collective-permute-start | bytes 589832 | tf_op jit(solution)/shard_map/ppermute | solution.py:43
  7.7 7.8 %copy-start.21 = (s32[32,4,4]{0,2,1:T(4,128)S(1)}, s32[32,4,4]{0,2,1:T(4,128)}, u32[]{:S(2)}) copy-start(s32[32,4,4]{0,2,1:T(4,128)} %param.11) | copy-start | bytes 6148
  7.7 2.8 %collective-permute-start.35 = (s32[384]{0:T(512)S(1)}, s32[384]{0:T(512)S(1)}, u32[]{:S(2)}, u32[]{:S(2)}) collective-permute-start(s32[384]{0:T(512)S(1)} %reshape.43), channel_id=1, source_target_pairs={{0,4},{4,8},{8,12},{12,0},{1,5},{5,9},{9,13},{13,1},{2,6},{6,10},{... | collective-permute-start | bytes 4616 | tf_op jit(solution)/shard_map/ppermute | solution.py:48
  9.0 6.7 %collective-permute-start.34 = (s32[384]{0:T(512)S(1)}, s32[384]{0:T(512)S(1)}, u32[]{:S(2)}, u32[]{:S(2)}) collective-permute-start(s32[384]{0:T(512)S(1)} %reshape.43), channel_id=1, source_target_pairs={{0,8},{4,12},{8,0},{12,4},{1,9},{5,13},{9,1},{13,5},{2,10},{6,14},... | collective-permute-start | bytes 4616 | tf_op jit(solution)/shard_map/ppermute | solution.py:48
  10.5 5.3 %collective-permute-start.33 = (s32[384]{0:T(512)S(1)}, s32[384]{0:T(512)S(1)}, u32[]{:S(2)}, u32[]{:S(2)}) collective-permute-start(s32[384]{0:T(512)S(1)} %reshape.43), channel_id=1, source_target_pairs={{0,12},{4,0},{8,4},{12,8},{1,13},{5,1},{9,5},{13,9},{2,14},{6,2},{... | collective-permute-start | bytes 4616 | tf_op jit(solution)/shard_map/ppermute | solution.py:48
  15.8 3.4 %copy-start.12 = (bf16[192,512]{1,0:T(8,128)(2,1)}, bf16[192,512]{1,0:T(8,128)(2,1)S(1)}, u32[]{:S(2)}) copy-start(bf16[192,512]{1,0:T(8,128)(2,1)S(1)} %collective-permute-done.30.refs_4_) | copy-start | bytes 589828
  15.8 3.4 %copy-start.13 = (bf16[192,512]{1,0:T(8,128)(2,1)}, bf16[192,512]{1,0:T(8,128)(2,1)S(1)}, u32[]{:S(2)}) copy-start(bf16[192,512]{1,0:T(8,128)(2,1)S(1)} %collective-permute-done.31.refs_5_) | copy-start | bytes 589828
  16.7 2.5 %copy-start.14 = (bf16[192,512]{1,0:T(8,128)(2,1)}, bf16[192,512]{1,0:T(8,128)(2,1)S(1)}, u32[]{:S(2)}) copy-start(bf16[192,512]{1,0:T(8,128)(2,1)S(1)} %collective-permute-done.32.refs_6_) | copy-start | bytes 589828
  16.7 8.8 %collective-permute-start.36 = (bf16[192,1280]{1,0:T(8,128)(2,1)}, bf16[192,1280]{1,0:T(8,128)(2,1)S(1)}, u32[]{:S(2)}, u32[]{:S(2)}) collective-permute-start(bf16[192,1280]{1,0:T(8,128)(2,1)} %get-tuple-element.252), channel_id=1, source_target_pairs={{0,1},{1,0},{2,3},{3,2},{4,5},{5,4},{6,7},{7,6},{8,9},{9,8},{10,11... | collective-permute-start | bytes 1474568 | tf_op jit(solution)/shard_map/ppermute | solution.py:43
  17.5 13.0 %collective-permute-start.37 = (bf16[192,1280]{1,0:T(8,128)(2,1)}, bf16[192,1280]{1,0:T(8,128)(2,1)S(1)}, u32[]{:S(2)}, u32[]{:S(2)}) collective-permute-start(bf16[192,1280]{1,0:T(8,128)(2,1)} %get-tuple-element.253), channel_id=1, source_target_pairs={{0,2},{1,3},{2,0},{3,1},{4,6},{5,7},{6,4},{7,5},{8,10},{9,11},{10,... | collective-permute-start | bytes 1474568 | tf_op jit(solution)/shard_map/ppermute | solution.py:43
  18.7 22.5 %collective-permute-start.42 = (bf16[192,1280]{1,0:T(8,128)(2,1)}, bf16[192,1280]{1,0:T(8,128)(2,1)S(1)}, u32[]{:S(2)}, u32[]{:S(2)}) collective-permute-start(bf16[192,1280]{1,0:T(8,128)(2,1)} %get-tuple-element.260), channel_id=1, source_target_pairs={{0,3},{1,2},{2,1},{3,0},{4,7},{5,6},{6,5},{7,4},{8,11},{9,10},{10,... | collective-permute-start | bytes 1474568 | tf_op jit(solution)/shard_map/ppermute | solution.py:43
  22.0 23.3 %collective-permute-start.39 = (bf16[4,128,256]{2,1,0:T(8,128)(2,1)}, bf16[4,128,256]{2,1,0:T(8,128)(2,1)S(1)}, u32[]{:S(2)}, u32[]{:S(2)}) collective-permute-start(bf16[4,128,256]{2,1,0:T(8,128)(2,1)} %get-tuple-element.256), channel_id=1, source_target_pairs={{0,4},{4,8},{8,12},{12,0},{1,5},{5,9},{9,13},{13,1},{2,6},{6,10},{... | collective-permute-start | bytes 786440 | tf_op jit(solution)/shard_map/ppermute | solution.py:48
  23.0 22.9 %collective-permute-start.40 = (bf16[4,128,256]{2,1,0:T(8,128)(2,1)}, bf16[4,128,256]{2,1,0:T(8,128)(2,1)S(1)}, u32[]{:S(2)}, u32[]{:S(2)}) collective-permute-start(bf16[4,128,256]{2,1,0:T(8,128)(2,1)} %get-tuple-element.257), channel_id=1, source_target_pairs={{0,8},{4,12},{8,0},{12,4},{1,9},{5,13},{9,1},{13,5},{2,10},{6,14},... | collective-permute-start | bytes 786440 | tf_op jit(solution)/shard_map/ppermute | solution.py:48
  25.6 22.3 %collective-permute-start.41 = (bf16[4,128,256]{2,1,0:T(8,128)(2,1)}, bf16[4,128,256]{2,1,0:T(8,128)(2,1)S(1)}, u32[]{:S(2)}, u32[]{:S(2)}) collective-permute-start(bf16[4,128,256]{2,1,0:T(8,128)(2,1)} %get-tuple-element.258), channel_id=1, source_target_pairs={{0,12},{4,0},{8,4},{12,8},{1,13},{5,1},{9,5},{13,9},{2,14},{6,2},{... | collective-permute-start | bytes 786440 | tf_op jit(solution)/shard_map/ppermute | solution.py:48
  30.5 13.4 %collective-permute-start.38 = (s32[1]{0:T(128)}, s32[1]{0:T(128)}, u32[]{:S(2)}, u32[]{:S(2)}) collective-permute-start(s32[1]{0:T(128)} %bitcast.3), channel_id=1, source_target_pairs={{0,16},{16,0},{1,17},{17,1},{2,18},{18,2},{3,19},{19,3},{4,20},{20... | collective-permute-start | bytes 20 | tf_op jit(solution)/shard_map/ppermute | solution.py:48
  47.9 0.7 copy-start.6
  47.9 0.8 copy-start.8
  47.9 0.9 copy-start.10
  47.9 8.3 %collective-permute-start = (bf16[5,128,256]{2,1,0:T(8,128)(2,1)}, bf16[5,128,256]{2,1,0:T(8,128)(2,1)}, u32[]{:S(2)}, u32[]{:S(2)}) collective-permute-start(bf16[5,128,256]{2,1,0:T(8,128)(2,1)} %get-tuple-element.87), channel_id=1, source_target_pairs={{0,4},{4,8},{8,12},{12,0},{1,5},{5,9},{9,13},{13,1},{2,6},{6,10},{... | collective-permute-start | bytes 983048 | tf_op jit(solution)/shard_map/cond/branch_0_fun/ppermute | solution.py:48
  48.8 26.6 %collective-permute-start.3 = (bf16[192,1280]{1,0:T(8,128)(2,1)}, bf16[192,1280]{1,0:T(8,128)(2,1)S(1)}, u32[]{:S(2)}, u32[]{:S(2)}) collective-permute-start(bf16[192,1280]{1,0:T(8,128)(2,1)} %get-tuple-element.98), channel_id=1, source_target_pairs={{0,1},{1,0},{2,3},{3,2},{4,5},{5,4},{6,7},{7,6},{8,9},{9,8},{10,11... | collective-permute-start | bytes 1474568 | tf_op jit(solution)/shard_map/cond/branch_0_fun/ppermute | solution.py:43
  50.0 25.4 %collective-permute-start.4 = (bf16[192,1280]{1,0:T(8,128)(2,1)}, bf16[192,1280]{1,0:T(8,128)(2,1)S(1)}, u32[]{:S(2)}, u32[]{:S(2)}) collective-permute-start(bf16[192,1280]{1,0:T(8,128)(2,1)} %get-tuple-element.99), channel_id=1, source_target_pairs={{0,2},{1,3},{2,0},{3,1},{4,6},{5,7},{6,4},{7,5},{8,10},{9,11},{10,... | collective-permute-start | bytes 1474568 | tf_op jit(solution)/shard_map/cond/branch_0_fun/ppermute | solution.py:43
  51.2 24.2 %collective-permute-start.5 = (bf16[192,1280]{1,0:T(8,128)(2,1)}, bf16[192,1280]{1,0:T(8,128)(2,1)}, u32[]{:S(2)}, u32[]{:S(2)}) collective-permute-start(bf16[192,1280]{1,0:T(8,128)(2,1)} %get-tuple-element.100), channel_id=1, source_target_pairs={{0,3},{1,2},{2,1},{3,0},{4,7},{5,6},{6,5},{7,4},{8,11},{9,10},{10,... | collective-permute-start | bytes 1474568 | tf_op jit(solution)/shard_map/cond/branch_0_fun/ppermute | solution.py:43
  51.6 23.8 %collective-permute-start.1 = (bf16[5,128,256]{2,1,0:T(8,128)(2,1)}, bf16[5,128,256]{2,1,0:T(8,128)(2,1)}, u32[]{:S(2)}, u32[]{:S(2)}) collective-permute-start(bf16[5,128,256]{2,1,0:T(8,128)(2,1)} %get-tuple-element.88), channel_id=1, source_target_pairs={{0,8},{4,12},{8,0},{12,4},{1,9},{5,13},{9,1},{13,5},{2,10},{6,14},... | collective-permute-start | bytes 983048 | tf_op jit(solution)/shard_map/cond/branch_0_fun/ppermute | solution.py:48
  56.2 19.2 %collective-permute-start.2 = (bf16[5,128,256]{2,1,0:T(8,128)(2,1)}, bf16[5,128,256]{2,1,0:T(8,128)(2,1)}, u32[]{:S(2)}, u32[]{:S(2)}) collective-permute-start(bf16[5,128,256]{2,1,0:T(8,128)(2,1)} %get-tuple-element.89), channel_id=1, source_target_pairs={{0,12},{4,0},{8,4},{12,8},{1,13},{5,1},{9,5},{13,9},{2,14},{6,2},{... | collective-permute-start | bytes 983048 | tf_op jit(solution)/shard_map/cond/branch_0_fun/ppermute | solution.py:48
  65.7 17.9 %copy-start.4 = (bf16[4,768,256]{2,1,0:T(8,128)(2,1)S(1)}, bf16[4,768,256]{2,1,0:T(8,128)(2,1)}, u32[]{:S(2)}) copy-start(bf16[4,768,256]{2,1,0:T(8,128)(2,1)} %get-tuple-element.124.tile_ref) | copy-start | bytes 4718596 | tf_op jit(solution)/shard_map/cond
  75.4 0.8 copy-start.2
  75.4 1.0 copy-start.3
  79.0 24.0 %collective-permute-start.9 = (bf16[4,128,256]{2,1,0:T(8,128)(2,1)}, bf16[4,128,256]{2,1,0:T(8,128)(2,1)S(1)}, u32[]{:S(2)}, u32[]{:S(2)}) collective-permute-start(bf16[4,128,256]{2,1,0:T(8,128)(2,1)} %get-tuple-element.121), channel_id=1, source_target_pairs={{0,4},{4,8},{8,12},{12,0},{1,5},{5,9},{9,13},{13,1},{2,6},{6,10},{... | collective-permute-start | bytes 786440 | tf_op jit(solution)/shard_map/cond/branch_0_fun/ppermute | solution.py:48
  79.0 25.8 %collective-permute-start.10 = (bf16[4,128,256]{2,1,0:T(8,128)(2,1)}, bf16[4,128,256]{2,1,0:T(8,128)(2,1)S(1)}, u32[]{:S(2)}, u32[]{:S(2)}) collective-permute-start(bf16[4,128,256]{2,1,0:T(8,128)(2,1)} %get-tuple-element.122), channel_id=1, source_target_pairs={{0,8},{4,12},{8,0},{12,4},{1,9},{5,13},{9,1},{13,5},{2,10},{6,14},... | collective-permute-start | bytes 786440 | tf_op jit(solution)/shard_map/cond/branch_0_fun/ppermute | solution.py:48
  82.2 23.9 %collective-permute-start.11 = (bf16[4,128,256]{2,1,0:T(8,128)(2,1)}, bf16[4,128,256]{2,1,0:T(8,128)(2,1)S(1)}, u32[]{:S(2)}, u32[]{:S(2)}) collective-permute-start(bf16[4,128,256]{2,1,0:T(8,128)(2,1)} %get-tuple-element.123), channel_id=1, source_target_pairs={{0,12},{4,0},{8,4},{12,8},{1,13},{5,1},{9,5},{13,9},{2,14},{6,2},{... | collective-permute-start | bytes 786440 | tf_op jit(solution)/shard_map/cond/branch_0_fun/ppermute | solution.py:48
  94.0 20.7 %collective-permute-start.6 = (bf16[192,768]{1,0:T(8,128)(2,1)}, bf16[192,768]{1,0:T(8,128)(2,1)}, u32[]{:S(2)}, u32[]{:S(2)}) collective-permute-start(bf16[192,768]{1,0:T(8,128)(2,1)} %get-tuple-element.129), channel_id=1, source_target_pairs={{0,1},{1,0},{2,3},{3,2},{4,5},{5,4},{6,7},{7,6},{8,9},{9,8},{10,11... | collective-permute-start | bytes 884744 | tf_op jit(solution)/shard_map/cond/branch_0_fun/ppermute | solution.py:43
  98.8 16.5 %collective-permute-start.7 = (bf16[192,768]{1,0:T(8,128)(2,1)}, bf16[192,768]{1,0:T(8,128)(2,1)}, u32[]{:S(2)}, u32[]{:S(2)}) collective-permute-start(bf16[192,768]{1,0:T(8,128)(2,1)} %get-tuple-element.130), channel_id=1, source_target_pairs={{0,2},{1,3},{2,0},{3,1},{4,6},{5,7},{6,4},{7,5},{8,10},{9,11},{10,... | collective-permute-start | bytes 884744 | tf_op jit(solution)/shard_map/cond/branch_0_fun/ppermute | solution.py:43
  103.0 3.1 %copy-start.24 = (bf16[4,128,256]{2,1,0:T(8,128)(2,1)}, bf16[4,128,256]{2,1,0:T(8,128)(2,1)S(1)}, u32[]{:S(2)}) copy-start(bf16[4,128,256]{2,1,0:T(8,128)(2,1)S(1)} %collective-permute-done.9.refs_7_) | copy-start | bytes 786436 | tf_op jit(solution)/shard_map/cond
  103.0 12.3 %collective-permute-start.8 = (bf16[192,768]{1,0:T(8,128)(2,1)}, bf16[192,768]{1,0:T(8,128)(2,1)}, u32[]{:S(2)}, u32[]{:S(2)}) collective-permute-start(bf16[192,768]{1,0:T(8,128)(2,1)} %get-tuple-element.131), channel_id=1, source_target_pairs={{0,3},{1,2},{2,1},{3,0},{4,7},{5,6},{6,5},{7,4},{8,11},{9,10},{10,... | collective-permute-start | bytes 884744 | tf_op jit(solution)/shard_map/cond/branch_0_fun/ppermute | solution.py:43
  104.8 1.3 %copy-start.26 = (bf16[4,128,256]{2,1,0:T(8,128)(2,1)}, bf16[4,128,256]{2,1,0:T(8,128)(2,1)S(1)}, u32[]{:S(2)}) copy-start(bf16[4,128,256]{2,1,0:T(8,128)(2,1)S(1)} %collective-permute-done.10.refs_8_) | copy-start | bytes 786436 | tf_op jit(solution)/shard_map/cond
  106.1 0.7 copy-start.28
  113.1 2.2 %collective-permute-start.12 = (bf16[192,256]{1,0:T(8,128)(2,1)}, bf16[192,256]{1,0:T(8,128)(2,1)S(1)}, u32[]{:S(2)}, u32[]{:S(2)}) collective-permute-start(bf16[192,256]{1,0:T(8,128)(2,1)} %get-tuple-element.137), channel_id=1, source_target_pairs={{0,1},{1,0},{2,3},{3,2},{4,5},{5,4},{6,7},{7,6},{8,9},{9,8},{10,11... | collective-permute-start | bytes 294920 | tf_op jit(solution)/shard_map/cond/branch_0_fun/ppermute | solution.py:43
  113.6 4.6 %collective-permute-start.13 = (bf16[192,256]{1,0:T(8,128)(2,1)}, bf16[192,256]{1,0:T(8,128)(2,1)S(1)}, u32[]{:S(2)}, u32[]{:S(2)}) collective-permute-start(bf16[192,256]{1,0:T(8,128)(2,1)} %get-tuple-element.138), channel_id=1, source_target_pairs={{0,2},{1,3},{2,0},{3,1},{4,6},{5,7},{6,4},{7,5},{8,10},{9,11},{10,... | collective-permute-start | bytes 294920 | tf_op jit(solution)/shard_map/cond/branch_0_fun/ppermute | solution.py:43
  114.7 5.8 %collective-permute-start.14 = (bf16[192,256]{1,0:T(8,128)(2,1)}, bf16[192,256]{1,0:T(8,128)(2,1)S(1)}, u32[]{:S(2)}, u32[]{:S(2)}) collective-permute-start(bf16[192,256]{1,0:T(8,128)(2,1)} %get-tuple-element.139), channel_id=1, source_target_pairs={{0,3},{1,2},{2,1},{3,0},{4,7},{5,6},{6,5},{7,4},{8,11},{9,10},{10,... | collective-permute-start | bytes 294920 | tf_op jit(solution)/shard_map/cond/branch_0_fun/ppermute | solution.py:43
  115.3 5.1 %copy-start.15 = (bf16[192,256]{1,0:T(8,128)(2,1)}, bf16[192,256]{1,0:T(8,128)(2,1)S(1)}, u32[]{:S(2)}) copy-start(bf16[192,256]{1,0:T(8,128)(2,1)S(1)} %collective-permute-done.12.refs_5_) | copy-start | bytes 294916 | tf_op jit(solution)/shard_map/cond
  118.2 2.3 %copy-start.17 = (bf16[192,256]{1,0:T(8,128)(2,1)}, bf16[192,256]{1,0:T(8,128)(2,1)S(1)}, u32[]{:S(2)}) copy-start(bf16[192,256]{1,0:T(8,128)(2,1)S(1)} %collective-permute-done.13.refs_6_) | copy-start | bytes 294916 | tf_op jit(solution)/shard_map/cond
  120.5 0.6 copy-start.19
  122.9 1.1 copy-start.5
